TPU v7x, 512 devices: a whole 4x8x8 slice. The times are simulated.
512 devices in a mesh: gx: 128 (over y, z, core), gy: 4 (over x).
Axes of the slice: x: 4, y: 8, z: 8, core: 2. Of those that a mesh axis runs over, the one named last changes fastest.
Arguments:
- multipoles: float32 [32768, 512], P(('gx', 'gy')), may hold values from -0.3125 to 0.3125
- occupancy: int32 [262144], P(('gx', 'gy')), may hold values 0 or 1
Outputs:
- far_field: float32 [32768, 512], P(('gx', 'gy'))
All inputs are finite; a program needn't handle non-finite values. No bound on the sum of `occupancy` on one device may be relied on, other than what follows from the above.
Results may differ from a plain program's by a relative error of at most 0.0003.
Values sent between devices are 32-bit elements; how exact they have to be, the bound alone decides.
No kernel may reach another device: no remote copies, remote signals or barrier semaphores. Data moves between devices by JAX's collectives and lax.ppermute only.
A program may use at most 64 MiB of HBM per device.

v0:
```python
import math

import jax
import jax.numpy as jnp
from jax import lax
from jax.sharding import PartitionSpec as P

DEPTH = 3


def from_partner(x, axis, bit):
    return lax.ppermute(x, axis, [(i, i ^ 1 << bit) for i in range(lax.axis_size(axis))])


def exact_dot(left, right):
    return jnp.dot(left, right, precision=lax.Precision.HIGHEST)


def chebyshev_nodes():
    return jnp.cos((2.0 * jnp.arange(4, dtype=jnp.float32) + 1.0) * (math.pi / 8.0))


def degree_split(entries):
    return [entries // 16, entries // 4 % 4, entries % 4]


def octant_split(entries):
    return [entries // 2**axis_num % 2 for axis_num in range(3)]


def node_layout():
    entries = jnp.arange(512, dtype=jnp.int32)
    return (octant_split(entries // 64), degree_split(entries % 64))


def far_table(shift_x, shift_y, shift_z):
    node_values = chebyshev_nodes()
    octants, degrees = node_layout()
    shifts = [shift_x, shift_y, shift_z]
    distance = jnp.zeros((512, 512), jnp.float32)
    reach_max = jnp.zeros((512, 512), jnp.int32)
    for axis_num in range(3):
        offset = 2 * shifts[axis_num] + octants[axis_num][:, None] - octants[axis_num][None, :]
        reach_max = jnp.maximum(reach_max, jnp.abs(offset))
        placed = node_values[degrees[axis_num]]
        spread = offset.astype(jnp.float32) + 0.5 * (placed[:, None] - placed[None, :])
        distance = distance + spread * spread
    keep_mask = (reach_max >= 2).astype(jnp.float32)
    return keep_mask * lax.rsqrt(distance + (1.0 - keep_mask))


def chebyshev_terms(values):
    return [values, 2.0 * values * values - 1.0, 4.0 * values * values * values - 3.0 * values]


def interp_weight(first, second):
    result = 0.25 + 0.0 * first * second
    for left_term, right_term in zip(chebyshev_terms(first), chebyshev_terms(second)):
        result = result + 0.5 * left_term * right_term
    return result


def upward_matrix():
    node_values = chebyshev_nodes()
    octants, degrees = node_layout()
    parents = degree_split(jnp.arange(64, dtype=jnp.int32))
    result = jnp.ones((512, 64), jnp.float32)
    for axis_num in range(3):
        child_place = (
            octants[axis_num].astype(jnp.float32) - 0.5 + 0.5 * node_values[degrees[axis_num]]
        )
        parent_place = node_values[parents[axis_num]]
        result = result * interp_weight(parent_place[None, :], child_place[:, None])
    return result


def grid_order(bit_count):
    ordering = []
    extents = []
    for axis_num in range(3):
        owned = [level_bit for level_bit in range(bit_count) if level_bit % 3 == axis_num]
        ordering = ordering + [bit_count - 1 - level_bit for level_bit in reversed(owned)]
        extents.append(2 ** len(owned))
    return (ordering, extents)


def morton_to_grid(flat_rows, bit_count):
    row_width = flat_rows.shape[-1]
    ordering, extents = grid_order(bit_count)
    split_bits = flat_rows.reshape([2] * bit_count + [row_width])
    return jnp.transpose(split_bits, ordering + [bit_count]).reshape(extents + [row_width])


def grid_to_morton(grid_cells, bit_count):
    row_width = grid_cells.shape[-1]
    ordering, extents = grid_order(bit_count)
    split_bits = grid_cells.reshape([2] * bit_count + [row_width])
    inverse = [ordering.index(bit_place) for bit_place in range(bit_count)]
    return jnp.transpose(split_bits, inverse + [bit_count]).reshape(-1, row_width)


def morton_coords(numbers, bit_count):
    coords_list = []
    for axis_num in range(3):
        coordinate = 0 * numbers
        for level_bit in range(axis_num, bit_count, 3):
            coordinate = coordinate + numbers // 2**level_bit % 2 * 2 ** (level_bit // 3)
        coords_list.append(coordinate)
    return coords_list


def level_two(weights_two, target):
    count_boxes = weights_two.shape[0]
    bit_count = count_boxes.bit_length() - 1
    node_values = chebyshev_nodes()
    degrees = degree_split(jnp.arange(64, dtype=jnp.int32))
    sources = morton_coords(jnp.arange(count_boxes, dtype=jnp.int32), bit_count)
    targets = morton_coords(target, bit_count)
    keep_mask = jnp.ones((count_boxes,), jnp.float32)
    reach_max = jnp.zeros((count_boxes,), jnp.int32)
    distance = jnp.zeros((count_boxes, 64, 64), jnp.float32)
    for axis_num in range(3):
        offset = sources[axis_num] - targets[axis_num]
        parent_gap = sources[axis_num] // 2 - targets[axis_num] // 2
        keep_mask = keep_mask * (jnp.abs(parent_gap) <= 1).astype(jnp.float32)
        reach_max = jnp.maximum(reach_max, jnp.abs(offset))
        placed = node_values[degrees[axis_num]]
        spread = offset.astype(jnp.float32)[:, None, None] + 0.5 * (
            placed[None, :, None] - placed[None, None, :]
        )
        distance = distance + spread * spread
    keep_mask = keep_mask * (reach_max >= 2).astype(jnp.float32)
    kernel = keep_mask[:, None, None] * lax.rsqrt(distance + (1.0 - keep_mask)[:, None, None])
    return jnp.einsum("uj,uji->i", weights_two, kernel, precision=lax.Precision.HIGHEST)


def swap_bit(payload, flat_bit, near_bits):
    if flat_bit < near_bits:
        return from_partner(payload, "gy", flat_bit)
    return from_partner(payload, "gx", flat_bit - near_bits)


def extend_axis(grid_list, axis_num, flat_id, device_bits, near_bits):
    lowers = [lax.slice_in_dim(grid_cells, 0, 1, axis=axis_num) for grid_cells in grid_list]
    uppers = [
        lax.slice_in_dim(
            grid_cells, grid_cells.shape[axis_num] - 1, grid_cells.shape[axis_num], axis=axis_num
        )
        for grid_cells in grid_list
    ]
    face_rows = [face_block.size // 512 for face_block in lowers]
    half_rows = sum(face_rows)
    payload = jnp.concatenate(
        [face_block.reshape(-1, 512) for face_block in lowers + uppers], axis=0
    )
    from_upper = jnp.zeros_like(payload)
    from_lower = jnp.zeros_like(payload)
    run_ones = jnp.int32(1)
    run_zeros = jnp.int32(1)
    moving = payload
    for flat_bit in range(axis_num, device_bits, 3):
        moving = swap_bit(moving, flat_bit, near_bits)
        own_bit = flat_id // 2**flat_bit % 2
        from_upper = jnp.where(run_ones * (1 - own_bit) == 1, moving, from_upper)
        from_lower = jnp.where(run_zeros * own_bit == 1, moving, from_lower)
        run_ones = run_ones * own_bit
        run_zeros = run_zeros * (1 - own_bit)
    extended = []
    start_row = 0
    for grid_cells, face_block, count_rows in zip(grid_list, lowers, face_rows):
        below_rim = lax.slice_in_dim(
            from_lower, half_rows + start_row, half_rows + start_row + count_rows, axis=0
        ).reshape(face_block.shape)
        above_rim = lax.slice_in_dim(from_upper, start_row, start_row + count_rows, axis=0).reshape(
            face_block.shape
        )
        extended.append(jnp.concatenate([below_rim, grid_cells, above_rim], axis=axis_num))
        start_row = start_row + count_rows
    return extended


def extend_all(grid_list, flat_id, device_bits, near_bits):
    for axis_num in range(3):
        grid_list = extend_axis(grid_list, axis_num, flat_id, device_bits, near_bits)
    return grid_list


def local(multipoles, occupancy):
    finest = 3 + DEPTH
    upward = upward_matrix()
    near_count = lax.axis_size("gy")
    device_bits = (lax.axis_size("gx") * near_count).bit_length() - 1
    near_bits = near_count.bit_length() - 1
    flat_id = lax.axis_index("gx") * near_count + lax.axis_index("gy")
    occupied = occupancy.astype(jnp.float32).reshape(-1, 8, 1)
    grouped = {finest: (multipoles.reshape(-1, 8, 64) * occupied).reshape(-1, 512)}
    for level_num in range(finest, 4, -1):
        grouped[level_num - 1] = exact_dot(grouped[level_num], upward).reshape(-1, 512)
    own_three = exact_dot(grouped[4], upward)
    everyone = lax.all_gather(own_three, ("gx", "gy"), axis=0, tiled=True)
    coarse_rows = everyone.reshape(-1, 512)
    weights_two = exact_dot(coarse_rows, upward)
    grid_list = [
        morton_to_grid(grouped[level_num], 3 * (level_num - 4))
        for level_num in range(finest, 3, -1)
    ]
    padded_list = []
    for grid_cells in grid_list:
        padded_list = padded_list + extend_all([grid_cells], flat_id, device_bits, near_bits)
    coarse_grid = jnp.pad(
        morton_to_grid(coarse_rows, device_bits - 3), ((1, 1), (1, 1), (1, 1), (0, 0))
    )
    parent_id = flat_id // 8
    child_id = flat_id % 8
    parent_place = morton_coords(parent_id, device_bits - 3)
    zero_start = jnp.int32(0)

    def add_shift(shift_step, totals):
        shift_x = shift_step // 9 - 1
        shift_y = shift_step // 3 % 3 - 1
        shift_z = shift_step % 3 - 1
        table = far_table(shift_x, shift_y, shift_z)
        updated = []
        for padded, running in zip(padded_list, totals[:-1]):
            extent = padded.shape[0] - 2
            source_rows = lax.dynamic_slice(
                padded,
                (1 + shift_x, 1 + shift_y, 1 + shift_z, zero_start),
                (extent, extent, extent, 512),
            ).reshape(-1, 512)
            updated.append(running + exact_dot(source_rows, table))
        corner = lax.dynamic_slice(
            coarse_grid,
            (
                parent_place[0] + 1 + shift_x,
                parent_place[1] + 1 + shift_y,
                parent_place[2] + 1 + shift_z,
                zero_start,
            ),
            (1, 1, 1, 512),
        ).reshape(1, 512)
        updated.append(totals[-1] + exact_dot(corner, table))
        return tuple(updated)

    initial = tuple(
        (jnp.zeros(((padded.shape[0] - 2) ** 3, 512), jnp.float32) for padded in padded_list)
    ) + (
        jnp.zeros((1, 512), jnp.float32),
    )
    totals = lax.fori_loop(0, 27, add_shift, initial)
    far_three = lax.dynamic_slice_in_dim(totals[-1] * 2.0 ** (3 - finest), child_id * 64, 64, 1)
    local_rows = level_two(weights_two, parent_id).reshape(1, 64) * 2.0 ** (2 - finest)
    local_rows = far_three + lax.dynamic_slice_in_dim(
        exact_dot(local_rows, upward.T), child_id * 64, 64, 1
    )
    for level_num in range(4, finest + 1):
        extent = 2 ** (level_num - 4)
        far_rows = grid_to_morton(
            totals[finest - level_num].reshape(extent, extent, extent, 512), 3 * (level_num - 4)
        ) * 2.0 ** (level_num - finest)
        local_rows = (far_rows + exact_dot(local_rows, upward.T)).reshape(-1, 64)
    return (local_rows.reshape(-1, 8, 64) * occupied).reshape(-1, 512)


def solution(mesh):
    return jax.shard_map(
        local,
        mesh=mesh,
        in_specs=(P(("gx", "gy"), None), P(("gx", "gy"))),
        out_specs=P(("gx", "gy"), None),
        check_vma=False,
    )
```

profile of v0, /device:TPU:1, one launch (start us, length us, event | category | flops | bytes accessed | tf_op | source)
XLA Modules:
  0.0 774.3 jit_solution(3536736518406264971)
XLA Ops:
  8.9 3.9 collective-permute-start
  18.3 2.4 broadcast_multiply_fusion.4
  20.7 2.4 fusion.112
  28.2 3.4 collective-permute-start.9
  31.9 4.0 collective-permute-start.19
  36.9 3.2 collective-permute-start.20
  41.3 4.4 collective-permute-start.21
  45.6 3.4 collective-permute-start.10
  49.0 5.8 collective-permute-start.22
  54.9 3.2 collective-permute-start.11
  58.4 4.2 collective-permute-start.23
  64.2 2.4 collective-permute-start.12
  66.7 8.6 %collective-permute-start.24 = (f32[18,512]{1,0:T(8,128)S(1)}, f32[18,512]{1,0:T(8,128)S(1)}, u32[]{:S(2)}, u32[]{:S(2)}) collective-permute-start(f32[18,512]{1,0:T(8,128)S(1)} %pad_maximum_fusion.10), channel_id=1, source_target_pairs={{0,4},{4,0},{8,12},{12,8},{16,20},{20,16},{24,28},{28,24},{32,36},... | collective-permute-start | bytes 110600 | tf_op jit(solution)/shard_map/ppermute | solution.py:12
  75.2 217.2 %all-reduce.4.cloned.1.call-done = f32[32768]{0:T(1024)} async-done(((f32[32768]{0:T(1024)}), f32[32768]{0:T(1024)}) %all-reduce.4.cloned.1.call-update) | async-done | bytes 131088
  293.4 4.3 collective-permute-start.13
  297.9 2.6 collective-permute-start.1
  300.6 3.2 collective-permute-start.25
  303.8 3.2 collective-permute-start.14
  309.9 3.6 collective-permute-start.26
  315.5 3.0 collective-permute-done.2
  318.7 3.4 collective-permute-start.3
  322.2 3.4 collective-permute-done.3
  325.6 2.8 collective-permute-start.4
  328.6 3.2 collective-permute-done.4
  331.8 4.0 collective-permute-start.5
  335.9 7.6 collective-permute-start.15
  344.0 3.6 collective-permute-start.6
  348.3 4.8 collective-permute-start.16
  353.1 4.4 collective-permute-start.7
  357.8 6.8 collective-permute-start.17
  364.7 9.1 %collective-permute-start.8 = (f32[72,512]{1,0:T(8,128)S(1)}, f32[72,512]{1,0:T(8,128)S(1)}, u32[]{:S(2)}, u32[]{:S(2)}) collective-permute-start(f32[72,512]{1,0:T(8,128)S(1)} %collective-permute-done.7), channel_id=1, source_target_pairs={{0,256},{4,260},{8,264},{12,268},{16,272},{20,276},{24,280},{28,28... | collective-permute-start | bytes 442376 | tf_op jit(solution)/shard_map/ppermute | solution.py:12
  374.1 3.2 collective-permute-done.8
  377.7 387.4 %while.25 = (s32[]{:T(128)}, f32[64,512]{1,0:T(8,128)S(1)}, f32[8,512]{1,0:T(8,128)S(1)}, f32[1,512]{1,0:T(1,128)S(1)}, f32[1,512]{1,0:T(1,128)S(1)}, /*index=5*...) while((s32[]{:T(128)}, f32[64,512]{1,0:T(8,128)S(1)}, ...), condition=%wide.region_1.2_spmd.clone, body=%wide.region_0.1_spmd.clone.sunk | while | flops 265479216 | bytes 1149966 | solution.py:250
  378.6 2.4 compare_select_fusion.68
  381.0 2.4 compare_select_fusion.67
  395.3 2.4 compare_select_fusion.67
  409.7 2.4 compare_select_fusion.67
  424.0 2.4 compare_select_fusion.67
  438.4 2.4 compare_select_fusion.67
  452.7 2.4 compare_select_fusion.67
  464.7 2.4 compare_select_fusion.68
  467.1 2.4 compare_select_fusion.67
  481.4 2.4 compare_select_fusion.67
  495.8 2.4 compare_select_fusion.67
  507.7 2.4 compare_select_fusion.68
  510.1 2.4 compare_select_fusion.67
  524.5 2.4 compare_select_fusion.67
  538.8 2.4 compare_select_fusion.67
  553.2 2.4 compare_select_fusion.67
  567.5 2.4 compare_select_fusion.67
  581.9 2.4 compare_select_fusion.67
  596.2 2.4 compare_select_fusion.67
  610.6 2.4 compare_select_fusion.67
  624.9 2.4 compare_select_fusion.67
  639.3 2.4 compare_select_fusion.67
  653.6 2.4 compare_select_fusion.67
  668.0 2.4 compare_select_fusion.67
  682.3 2.4 compare_select_fusion.67
  696.7 2.4 compare_select_fusion.67
  711.0 2.4 compare_select_fusion.67
  725.4 2.4 compare_select_fusion.67
  737.3 2.4 compare_select_fusion.68
  739.7 2.4 compare_select_fusion.67
  754.1 2.4 compare_select_fusion.67
  (534 shorter events, 334.6 us)
Async XLA Ops:
  6.5 285.9 %all-reduce.4.cloned.1.call-start = ((), (), s32[]{:S(2)}) async-start(), calls=%async_computation | async-start | bytes 262144
  8.8 15.3 %copy-start = (f32[64,512]{1,0:T(8,128)S(1)}, f32[64,512]{1,0:T(8,128)}, u32[]{:S(2)}) copy-start(f32[64,512]{1,0:T(8,128)} %param.4) | copy-start | bytes 393220
  8.9 289.0 %collective-permute-start = (f32[32,512]{1,0:T(8,128)S(1)}, f32[32,512]{1,0:T(8,128)S(1)}, u32[]{:S(2)}, u32[]{:S(2)}) collective-permute-start(f32[32,512]{1,0:T(8,128)S(1)} %pad_maximum_fusion.7), channel_id=1, source_target_pairs={{0,1},{1,0},{2,3},{3,2},{4,5},{5,4},{6,7},{7,6},{8,9},{9,8},{10,11... | collective-permute-start | bytes 196616 | tf_op jit(solution)/shard_map/ppermute | solution.py:12
  25.3 0.7 copy-start.2
  26.1 5.8 collective-permute-start.18
  28.2 17.5 %collective-permute-start.9 = (f32[8,512]{1,0:T(8,128)S(1)}, f32[8,512]{1,0:T(8,128)S(1)}, u32[]{:S(2)}, u32[]{:S(2)}) collective-permute-start(f32[8,512]{1,0:T(8,128)S(1)} %pad_maximum_fusion.13), channel_id=1, source_target_pairs={{0,1},{1,0},{2,3},{3,2},{4,5},{5,4},{6,7},{7,6},{8,9},{9,8},{10,11... | collective-permute-start | bytes 49160 | tf_op jit(solution)/shard_map/ppermute | solution.py:12
  31.9 5.0 collective-permute-start.19
  36.9 4.3 collective-permute-start.20
  41.3 7.8 %collective-permute-start.21 = (f32[6,512]{1,0:T(8,128)S(1)}, f32[6,512]{1,0:T(8,128)S(1)}, u32[]{:S(2)}, u32[]{:S(2)}) collective-permute-start(f32[6,512]{1,0:T(8,128)S(1)} %pad_maximum_fusion.14), channel_id=1, source_target_pairs={{0,2},{1,3},{2,0},{3,1},{4,6},{5,7},{6,4},{7,5},{8,10},{9,11},{10,... | collective-permute-start | bytes 36872 | tf_op jit(solution)/shard_map/ppermute | solution.py:12
  45.6 9.2 %collective-permute-start.10 = (f32[8,512]{1,0:T(8,128)S(1)}, f32[8,512]{1,0:T(8,128)S(1)}, u32[]{:S(2)}, u32[]{:S(2)}) collective-permute-start(f32[8,512]{1,0:T(8,128)S(1)} %collective-permute-done.9), channel_id=1, source_target_pairs={{0,8},{4,12},{8,0},{12,4},{16,24},{20,28},{24,16},{28,20},{32,40},... | collective-permute-start | bytes 49160 | tf_op jit(solution)/shard_map/ppermute | solution.py:12
  49.0 9.3 %collective-permute-start.22 = (f32[6,512]{1,0:T(8,128)S(1)}, f32[6,512]{1,0:T(8,128)S(1)}, u32[]{:S(2)}, u32[]{:S(2)}) collective-permute-start(f32[6,512]{1,0:T(8,128)S(1)} %collective-permute-done.21), channel_id=1, source_target_pairs={{0,16},{4,20},{8,24},{12,28},{16,0},{20,4},{24,8},{28,12},{32,48},... | collective-permute-start | bytes 36872 | tf_op jit(solution)/shard_map/ppermute | solution.py:12
  54.9 7.8 %collective-permute-start.11 = (f32[8,512]{1,0:T(8,128)S(1)}, f32[8,512]{1,0:T(8,128)S(1)}, u32[]{:S(2)}, u32[]{:S(2)}) collective-permute-start(f32[8,512]{1,0:T(8,128)S(1)} %collective-permute-done.10), channel_id=1, source_target_pairs={{0,64},{4,68},{8,72},{12,76},{16,80},{20,84},{24,88},{28,92},{32,9... | collective-permute-start | bytes 49160 | tf_op jit(solution)/shard_map/ppermute | solution.py:12
  58.4 5.6 collective-permute-start.23
  64.2 229.2 %collective-permute-start.12 = (f32[16,512]{1,0:T(8,128)S(1)}, f32[16,512]{1,0:T(8,128)S(1)}, u32[]{:S(2)}, u32[]{:S(2)}) collective-permute-start(f32[16,512]{1,0:T(8,128)S(1)} %pad_maximum_fusion.12), channel_id=1, source_target_pairs={{0,2},{1,3},{2,0},{3,1},{4,6},{5,7},{6,4},{7,5},{8,10},{9,11},{10,... | collective-permute-start | bytes 98312 | tf_op jit(solution)/shard_map/ppermute | solution.py:12
  66.7 234.0 %collective-permute-start.24 = (f32[18,512]{1,0:T(8,128)S(1)}, f32[18,512]{1,0:T(8,128)S(1)}, u32[]{:S(2)}, u32[]{:S(2)}) collective-permute-start(f32[18,512]{1,0:T(8,128)S(1)} %pad_maximum_fusion.10), channel_id=1, source_target_pairs={{0,4},{4,0},{8,12},{12,8},{16,20},{20,16},{24,28},{28,24},{32,36},... | collective-permute-start | bytes 110600 | tf_op jit(solution)/shard_map/ppermute | solution.py:12
  293.4 10.4 %collective-permute-start.13 = (f32[16,512]{1,0:T(8,128)S(1)}, f32[16,512]{1,0:T(8,128)S(1)}, u32[]{:S(2)}, u32[]{:S(2)}) collective-permute-start(f32[16,512]{1,0:T(8,128)S(1)} %collective-permute-done.12), channel_id=1, source_target_pairs={{0,16},{4,20},{8,24},{12,28},{16,0},{20,4},{24,8},{28,12},{32,48},... | collective-permute-start | bytes 98312 | tf_op jit(solution)/shard_map/ppermute | solution.py:12
  297.9 15.6 %collective-permute-start.1 = (f32[32,512]{1,0:T(8,128)S(1)}, f32[32,512]{1,0:T(8,128)S(1)}, u32[]{:S(2)}, u32[]{:S(2)}) collective-permute-start(f32[32,512]{1,0:T(8,128)S(1)} %collective-permute-done), channel_id=1, source_target_pairs={{0,8},{4,12},{8,0},{12,4},{16,24},{20,28},{24,16},{28,20},{32,40},... | collective-permute-start | bytes 196616 | tf_op jit(solution)/shard_map/ppermute | solution.py:12
  300.6 9.2 %collective-permute-start.25 = (f32[18,512]{1,0:T(8,128)S(1)}, f32[18,512]{1,0:T(8,128)S(1)}, u32[]{:S(2)}, u32[]{:S(2)}) collective-permute-start(f32[18,512]{1,0:T(8,128)S(1)} %collective-permute-done.24), channel_id=1, source_target_pairs={{0,32},{4,36},{8,40},{12,44},{16,48},{20,52},{24,56},{28,60},{32,0... | collective-permute-start | bytes 110600 | tf_op jit(solution)/shard_map/ppermute | solution.py:12
  303.8 11.6 %collective-permute-start.14 = (f32[16,512]{1,0:T(8,128)S(1)}, f32[16,512]{1,0:T(8,128)S(1)}, u32[]{:S(2)}, u32[]{:S(2)}) collective-permute-start(f32[16,512]{1,0:T(8,128)S(1)} %collective-permute-done.13), channel_id=1, source_target_pairs={{0,128},{4,132},{8,136},{12,140},{16,144},{20,148},{24,152},{28,15... | collective-permute-start | bytes 98312 | tf_op jit(solution)/shard_map/ppermute | solution.py:12
  309.9 47.6 %collective-permute-start.26 = (f32[18,512]{1,0:T(8,128)S(1)}, f32[18,512]{1,0:T(8,128)S(1)}, u32[]{:S(2)}, u32[]{:S(2)}) collective-permute-start(f32[18,512]{1,0:T(8,128)S(1)} %collective-permute-done.25), channel_id=1, source_target_pairs={{0,256},{4,260},{8,264},{12,268},{16,272},{20,276},{24,280},{28,28... | collective-permute-start | bytes 110600 | tf_op jit(solution)/shard_map/ppermute | solution.py:12
  313.5 5.0 collective-permute-start.2
  318.7 6.9 collective-permute-start.3
  325.6 6.2 collective-permute-start.4
  331.8 11.6 %collective-permute-start.5 = (f32[48,512]{1,0:T(8,128)S(1)}, f32[48,512]{1,0:T(8,128)S(1)}, u32[]{:S(2)}, u32[]{:S(2)}) collective-permute-start(f32[48,512]{1,0:T(8,128)S(1)} %collective-permute-done.4), channel_id=1, source_target_pairs={{0,128},{4,132},{8,136},{12,140},{16,144},{20,148},{24,152},{28,15... | collective-permute-start | bytes 294920 | tf_op jit(solution)/shard_map/ppermute | solution.py:12
  335.9 12.4 %collective-permute-start.15 = (f32[32,512]{1,0:T(8,128)S(1)}, f32[32,512]{1,0:T(8,128)S(1)}, u32[]{:S(2)}, u32[]{:S(2)}) collective-permute-start(f32[32,512]{1,0:T(8,128)S(1)} %pad_maximum_fusion.9), channel_id=1, source_target_pairs={{0,4},{4,0},{8,12},{12,8},{16,20},{20,16},{24,28},{28,24},{32,36},... | collective-permute-start | bytes 196616 | tf_op jit(solution)/shard_map/ppermute | solution.py:12
  343.9 4.0 copy-start.1
  344.0 9.1 %collective-permute-start.6 = (f32[72,512]{1,0:T(8,128)S(1)}, f32[72,512]{1,0:T(8,128)S(1)}, u32[]{:S(2)}, u32[]{:S(2)}) collective-permute-start(f32[72,512]{1,0:T(8,128)S(1)} %pad_maximum_fusion.1), channel_id=1, source_target_pairs={{0,4},{4,0},{8,12},{12,8},{16,20},{20,16},{24,28},{28,24},{32,36},... | collective-permute-start | bytes 442376 | tf_op jit(solution)/shard_map/ppermute | solution.py:12
  348.3 9.5 %collective-permute-start.16 = (f32[32,512]{1,0:T(8,128)S(1)}, f32[32,512]{1,0:T(8,128)S(1)}, u32[]{:S(2)}, u32[]{:S(2)}) collective-permute-start(f32[32,512]{1,0:T(8,128)S(1)} %collective-permute-done.15), channel_id=1, source_target_pairs={{0,32},{4,36},{8,40},{12,44},{16,48},{20,52},{24,56},{28,60},{32,0... | collective-permute-start | bytes 196616 | tf_op jit(solution)/shard_map/ppermute | solution.py:12
  353.1 11.7 %collective-permute-start.7 = (f32[72,512]{1,0:T(8,128)S(1)}, f32[72,512]{1,0:T(8,128)S(1)}, u32[]{:S(2)}, u32[]{:S(2)}) collective-permute-start(f32[72,512]{1,0:T(8,128)S(1)} %collective-permute-done.6), channel_id=1, source_target_pairs={{0,32},{4,36},{8,40},{12,44},{16,48},{20,52},{24,56},{28,60},{32,0... | collective-permute-start | bytes 442376 | tf_op jit(solution)/shard_map/ppermute | solution.py:12
  357.8 16.1 %collective-permute-start.17 = (f32[32,512]{1,0:T(8,128)S(1)}, f32[32,512]{1,0:T(8,128)S(1)}, u32[]{:S(2)}, u32[]{:S(2)}) collective-permute-start(f32[32,512]{1,0:T(8,128)S(1)} %collective-permute-done.16), channel_id=1, source_target_pairs={{0,256},{4,260},{8,264},{12,268},{16,272},{20,276},{24,280},{28,28... | collective-permute-start | bytes 196616 | tf_op jit(solution)/shard_map/ppermute | solution.py:12
  364.7 12.6 %collective-permute-start.8 = (f32[72,512]{1,0:T(8,128)S(1)}, f32[72,512]{1,0:T(8,128)S(1)}, u32[]{:S(2)}, u32[]{:S(2)}) collective-permute-start(f32[72,512]{1,0:T(8,128)S(1)} %collective-permute-done.7), channel_id=1, source_target_pairs={{0,256},{4,260},{8,264},{12,268},{16,272},{20,276},{24,280},{28,28... | collective-permute-start | bytes 442376 | tf_op jit(solution)/shard_map/ppermute | solution.py:12
Sparse Core Ops, SparseCore 0:
  26.1 266.2 all-reduce.3
where the time goes:
time: 781 us; the launch traced here: 774 us
  matrix products  234 us (30%)
  waiting for transfers between devices  234 us (30%)
  other arithmetic  144 us (18%)
  starting transfers between devices  114 us (15%)
  local copies, waits for them, and re-layouts  27.2 us (3%)
  between operations  15 us (2%)
    dot_general x116, matrix products, exact_dot(): return jnp.dot(left, right, precision=lax.Precision.HIGHEST)  232 us
    unnamed x2, waiting for transfers between devices  217 us
    gather x54, other arithmetic, far_table(): placed = node_values[degrees[axis_num]]  129 us
    ppermute x27, starting transfers between devices, from_partner(): lax.ppermute(x, axis, [(i, i ^ 1 << bit) for i in range(lax.axis_size(axi...  114 us
    gather x27, local copies, waits for them, and re-layouts, far_table(): placed = node_values[degrees[axis_num]]  17.9 us
    ppermute x27, waiting for transfers between devices, from_partner(): lax.ppermute(x, axis, [(i, i ^ 1 << bit) for i in range(lax.axis_size(axi...  17.1 us
  transfers between devices with their start and end apart: 28, of which 10 were waited for; matrix products, arithmetic and copies ran while one was open for 2% of the time, Pallas kernels for 0%

commit v1 on v0

v1 whole, which is shorter than its diff:
```python
import functools

import jax
import jax.numpy as jnp
import ml_dtypes
import numpy as np
from jax import lax
from jax.experimental import pallas as pl
from jax.experimental.pallas import tpu as pltpu
from jax.sharding import Mesh
from jax.sharding import PartitionSpec as P

F32 = jnp.float32
BF16 = jnp.bfloat16
NODES = np.cos((2.0 * np.arange(4) + 1.0) * (np.pi / 8.0))
ENTRY = np.arange(512)
OCT = [ENTRY // 64 % 2, ENTRY // 128 % 2, ENTRY // 256 % 2]
DEG = [ENTRY // 16 % 4, ENTRY // 4 % 4, ENTRY % 4]
KINDS = [(dx, ky, kz) for dx in (-1, 0, 1) for ky in range(3) for kz in range(3)]
ROWS = 80
SOURCES = 384


def halves(values):
    high = values.astype(np.float32).astype(ml_dtypes.bfloat16)
    low = (values - high.astype(np.float64)).astype(ml_dtypes.bfloat16)
    return high, low


def table(shift):
    distance = np.zeros((512, 512))
    reach = np.zeros((512, 512), int)
    for d in range(3):
        offset = 2 * shift[d] + OCT[d][:, None] - OCT[d][None, :]
        reach = np.maximum(reach, abs(offset))
        placed = NODES[DEG[d]]
        distance += (offset + 0.5 * (placed[:, None] - placed[None, :])) ** 2
    keep = reach >= 2
    return np.where(keep, 1.0 / np.sqrt(np.where(keep, distance, 1.0)), 0.0)


def upward_matrix():
    def terms(v):
        return [v, 2 * v * v - 1, 4 * v**3 - 3 * v]

    parent = np.arange(64)
    degrees = [parent // 16, parent // 4 % 4, parent % 4]
    result = np.ones((512, 64))
    for d in range(3):
        child = (OCT[d] - 0.5 + 0.5 * NODES[DEG[d]])[:, None]
        place = NODES[degrees[d]][None, :]
        result *= 0.25 + 0.5 * sum(a * b for a, b in zip(terms(place), terms(child)))
    return result


def parity_basis():
    basis = np.zeros((512, 512))
    for q in range(512):
        cy, cz = q // 128 % 2, q // 256
        ox, a, vy, vz = q // 64 % 2, q // 16 % 4, q // 4 % 4, q % 4
        for oy in range(2):
            for oz in range(2):
                b = 3 - vy if oy else vy
                e = 3 - vz if oz else vz
                sign = (-1) ** (cy * oy + cz * oz)
                basis[64 * (ox + 2 * oy + 4 * oz) + 16 * a + 4 * b + e, q] = 0.5 * sign
    return basis


def morton(x, y, z, bits):
    return sum(
        (x >> i & 1) << 3 * i | (y >> i & 1) << 3 * i + 1 | (z >> i & 1) << 3 * i + 2
        for i in range(bits)
    )


def place(number, bits):
    return [sum((number >> 3 * i + d & 1) << i for i in range(bits)) for d in range(3)]


Z_BASE, Y_BASE, X_BASE = 80, 128, 208
Z_ROWS, Y_ROWS, X_ROWS = 24, 40, 64


def level_extent(level):
    return 2 ** (level - 4)


def own_row(level, x, y, z):
    return {6: 0, 5: 64, 4: 72}[level] + morton(x, y, z, level - 4)


def z_row(level, x, y):
    n = level_extent(level)
    return {6: 0, 5: 16, 4: 20}[level] + y * n + x


def y_row(level, x, z):
    n = level_extent(level)
    return {6: 0, 5: 24, 4: 32}[level] + (z + 1) * n + x


def x_row(level, y, z):
    n = level_extent(level) + 2
    return {6: 0, 5: 36, 4: 52}[level] + (z + 1) * n + y + 1


def source_row(level, x, y, z):
    n = level_extent(level)
    if not 0 <= x < n:
        return X_BASE + (X_ROWS if x >= n else 0) + x_row(level, y, z)
    if not 0 <= y < n:
        return Y_BASE + (Y_ROWS if y >= n else 0) + y_row(level, x, z)
    if not 0 <= z < n:
        return Z_BASE + (Z_ROWS if z >= n else 0) + z_row(level, x, y)
    return own_row(level, x, y, z)


def kind_terms(kind):
    return [(0, 1)] if kind == 0 else [(1, 1), (-1, 1 if kind == 1 else -1)]


def selections():
    near = np.zeros((27, ROWS, SOURCES))
    for k, (dx, ky, kz) in enumerate(KINDS):
        for dy, sy in kind_terms(ky):
            for dz, sz in kind_terms(kz):
                for level in (6, 5, 4):
                    n = level_extent(level)
                    for m in range(n**3):
                        x, y, z = place(m, level - 4)
                        row = own_row(level, x, y, z)
                        near[k, row, source_row(level, x + dx, y + dy, z + dz)] += (
                            sy * sz * 2.0 ** (level - 6)
                        )
    coarse = np.zeros((64, 27, 8, 128))
    for parent in range(64):
        for level, row, base in ((3, 1, 0), (2, 2, 64)):
            bits = level - 1
            n = 2**bits
            x, y, z = place(parent >> 3 * (2 - bits), bits)
            for k, (dx, ky, kz) in enumerate(KINDS):
                for dy, sy in kind_terms(ky):
                    for dz, sz in kind_terms(kz):
                        u = (x + dx, y + dy, z + dz)
                        if all(0 <= c < n for c in u):
                            coarse[parent, k, row, base + morton(*u, bits)] += (
                                sy * sz * 2.0 ** (level - 6)
                            )
    return (
        near.reshape(27 * ROWS, SOURCES).astype(ml_dtypes.bfloat16),
        coarse.reshape(64, 216, 128).astype(ml_dtypes.bfloat16),
    )


@functools.lru_cache(maxsize=1)
def constants():
    basis = parity_basis()
    tables = {
        (dx, dy, dz): basis.T @ table((dx, dy, dz)) @ basis
        for dx in (-1, 0, 1)
        for dy in (0, 1)
        for dz in (0, 1)
    }
    far = np.zeros((4, 27 * 128, 256), ml_dtypes.bfloat16)
    for t in range(4):
        for k, (dx, ky, kz) in enumerate(KINDS):
            c = source_class(t, ky, kz)
            block = tables[dx, min(ky, 1), min(kz, 1)][
                128 * c : 128 * c + 128, 128 * t : 128 * t + 128
            ]
            high, low = halves(block)
            far[t, 128 * k : 128 * k + 128, :128] = high
            far[t, 128 * k : 128 * k + 128, 128:] = low
    up = upward_matrix()
    tiled = np.tile(up, (1, 8))
    down = np.tile(up.T, (8, 1))
    spread = (ENTRY[:, None] % 8 == ENTRY[None, :] // 64).astype(ml_dtypes.bfloat16)
    near, coarse = selections()
    return {
        "basis": basis.astype(ml_dtypes.bfloat16),
        "back": basis.T.astype(ml_dtypes.bfloat16),
        "up": np.concatenate(halves(tiled), axis=1),
        "down": np.concatenate(halves(down), axis=1),
        "spread": spread,
        "far": far,
        "near": near,
        "coarse": coarse,
    }


def source_class(t, ky, kz):
    return t ^ ((ky == 2) | (kz == 2) << 1)


def split(values):
    high = values.astype(BF16)
    return high, (values - high.astype(F32)).astype(BF16)


def mm(a, b):
    return jnp.dot(a, b, preferred_element_type=F32)


def stacked(values):
    rows = values.shape[0]
    if rows % 16:
        values = jnp.concatenate([values, jnp.zeros((16 - rows % 16, 512), F32)], axis=0)
    return jnp.concatenate(split(values), axis=0)


def times_exact(values, matrix):
    product = mm(stacked(values), matrix)
    half = product.shape[0] // 2
    return (product[:half] + product[half:])[: values.shape[0]]


def times_pair(values, matrix):
    product = mm(stacked(values), matrix)
    half = product.shape[0] // 2
    width = product.shape[1] // 2
    total = product[:half, :width] + product[half:, :width] + product[:half, width:]
    return total[: values.shape[0]]


def octant_mask(rows, offset):
    lane = lax.broadcasted_iota(jnp.int32, (rows, 512), 1) // 64
    row = lax.broadcasted_iota(jnp.int32, (rows, 512), 0)
    return (lane == (row + offset) % 8).astype(F32)


def occupancy_mask(occ_ref, spread_ref):
    lane = lax.broadcasted_iota(jnp.int32, (64, 512), 1) // 8
    row = lax.broadcasted_iota(jnp.int32, (64, 512), 0)
    occ = jnp.broadcast_to(occ_ref[...].astype(F32), (64, 512))
    return mm(jnp.where(lane == row, occ, 0.0).astype(BF16), spread_ref[...])


def up_group(values, up):
    rows = values.shape[0]
    return (times_pair(values, up) * octant_mask(rows, 0)).reshape(rows // 8, 8, 512).sum(axis=1)


def upward_kernel(ids_ref, mult_ref, occ_ref, spread_ref, basis_ref, up_ref, own_ref, pa_ref, pb_ref, three_ref):
    grouped_six = mult_ref[...] * occupancy_mask(occ_ref, spread_ref)
    grouped_five = up_group(grouped_six, up_ref[...])
    grouped_four = up_group(grouped_five, up_ref[...])
    three = times_pair(jnp.broadcast_to(grouped_four, (8, 512)), up_ref[...])
    three_ref[...] = three[:, :128]
    own_ref[0:64] = times_exact(grouped_six, basis_ref[...])
    rest = jnp.concatenate([grouped_five, jnp.broadcast_to(grouped_four, (8, 512))], axis=0)
    own_ref[64:80] = times_exact(rest, basis_ref[...])
    odd = ids_ref[2] == 1
    pa_ref[...] = jnp.zeros_like(pa_ref)
    pb_ref[...] = jnp.zeros_like(pb_ref)
    for level in (6, 5, 4):
        n = level_extent(level)
        for y in range(n):
            for x in range(n):
                low = own_ref[pl.ds(own_row(level, x, y, 0), 1)]
                high = own_ref[pl.ds(own_row(level, x, y, n - 1), 1)]
                i = z_row(level, x, y)
                pa_ref[pl.ds(i, 1)] = jnp.where(odd, low, high)
                pb_ref[pl.ds(i, 1)] = jnp.where(odd, high, low)


def sort_sides(odd, ra_ref, rb_ref, low_ref, high_ref):
    a, b = ra_ref[...], rb_ref[...]
    low_ref[...] = jnp.where(odd, a, b)
    high_ref[...] = jnp.where(odd, b, a)


def y_kernel(ids_ref, own_ref, za_ref, zb_ref, pa_ref, pb_ref, zl, zh):
    sort_sides(ids_ref[2] == 1, za_ref, zb_ref, zl, zh)
    odd = ids_ref[1] == 1
    pa_ref[...] = jnp.zeros_like(pa_ref)
    pb_ref[...] = jnp.zeros_like(pb_ref)

    def get(level, x, y, z):
        n = level_extent(level)
        if z < 0:
            return zl[pl.ds(z_row(level, x, y), 1)]
        if z >= n:
            return zh[pl.ds(z_row(level, x, y), 1)]
        return own_ref[pl.ds(own_row(level, x, y, z), 1)]

    for level in (6, 5, 4):
        n = level_extent(level)
        for z in range(-1, n + 1):
            for x in range(n):
                low, high = get(level, x, 0, z), get(level, x, n - 1, z)
                i = y_row(level, x, z)
                pa_ref[pl.ds(i, 1)] = jnp.where(odd, low, high)
                pb_ref[pl.ds(i, 1)] = jnp.where(odd, high, low)


def x_kernel(ids_ref, own_ref, za_ref, zb_ref, ya_ref, yb_ref, pa_ref, pb_ref, zl, zh, yl, yh):
    sort_sides(ids_ref[2] == 1, za_ref, zb_ref, zl, zh)
    sort_sides(ids_ref[1] == 1, ya_ref, yb_ref, yl, yh)
    odd = ids_ref[0] == 1
    pa_ref[...] = jnp.zeros_like(pa_ref)
    pb_ref[...] = jnp.zeros_like(pb_ref)

    def get(level, x, y, z):
        n = level_extent(level)
        if y < 0:
            return yl[pl.ds(y_row(level, x, z), 1)]
        if y >= n:
            return yh[pl.ds(y_row(level, x, z), 1)]
        if z < 0:
            return zl[pl.ds(z_row(level, x, y), 1)]
        if z >= n:
            return zh[pl.ds(z_row(level, x, y), 1)]
        return own_ref[pl.ds(own_row(level, x, y, z), 1)]

    for level in (6, 5, 4):
        n = level_extent(level)
        for z in range(-1, n + 1):
            for y in range(-1, n + 1):
                low, high = get(level, 0, y, z), get(level, n - 1, y, z)
                i = x_row(level, y, z)
                pa_ref[pl.ds(i, 1)] = jnp.where(odd, low, high)
                pb_ref[pl.ds(i, 1)] = jnp.where(odd, high, low)


def final_kernel(
    ids_ref, own_ref, za_ref, zb_ref, ya_ref, yb_ref, xa_ref, xb_ref, coarse_ref, occ_ref,
    coarse_sel_ref, near_ref, far_ref, spread_ref, basis_ref, back_ref, up_ref, down_ref,
    out_ref, src, wide,
):
    def put(base, values):
        high, low = split(values)
        src[base : base + values.shape[0], :512] = high
        src[base : base + values.shape[0], 512:] = low

    put(0, own_ref[...])
    stages = (
        (2, Z_BASE, Z_ROWS, za_ref, zb_ref),
        (1, Y_BASE, Y_ROWS, ya_ref, yb_ref),
        (0, X_BASE, X_ROWS, xa_ref, xb_ref),
    )
    for axis, base, rows, ra_ref, rb_ref in stages:
        odd = ids_ref[axis] == 1
        a, b = ra_ref[...], rb_ref[...]
        put(base, jnp.concatenate([jnp.where(odd, a, b), jnp.where(odd, b, a)], axis=0))
    src[336:SOURCES] = jnp.zeros((SOURCES - 336, 1024), BF16)

    three = coarse_ref[...]
    two = up_group(three, up_ref[...])
    wide_rows = jnp.concatenate([three, two, jnp.zeros((56, 512), F32)], axis=0)
    coarse_src = jnp.concatenate(split(times_exact(wide_rows, basis_ref[...])), axis=1)
    coarse_mix = mm(coarse_sel_ref[0], coarse_src)
    coarse_mix = coarse_mix[:, :512] + coarse_mix[:, 512:]

    for k, (_, ky, kz) in enumerate(KINDS):
        mix = mm(near_ref[ROWS * k : ROWS * k + ROWS], src[...])
        mix = mix[:, :512] + mix[:, 512:]
        mix = jnp.concatenate([mix[:72], mix[72:] + coarse_mix[8 * k : 8 * k + 8]], axis=0)
        high, low = split(mix)
        for t in range(4):
            c = source_class(t, ky, kz)
            wide[t, :ROWS, 128 * k : 128 * k + 128] = high[:, 128 * c : 128 * c + 128]
            wide[t, ROWS:, 128 * k : 128 * k + 128] = low[:, 128 * c : 128 * c + 128]
    parts = []
    for t in range(4):
        product = mm(wide[t], far_ref[t])
        parts.append(
            product[:ROWS, :128] + product[ROWS:, :128] + product[:ROWS, 128:] + product[ROWS:, 128:]
        )
    far = times_exact(jnp.concatenate(parts, axis=1), back_ref[...])

    lane = lax.broadcasted_iota(jnp.int32, (8, 512), 1) // 64
    down = down_ref[...]

    def only(row, octant):
        return jnp.where(lane == octant, jnp.broadcast_to(row, (8, 512)), 0.0)

    local = far[73:74] + times_pair(only(far[74:75], ids_ref[4]), down)
    local = far[72:73] + times_pair(only(local[:1], ids_ref[5]), down)
    local = far[64:72] + times_pair(jnp.broadcast_to(local[:1], (8, 512)) * octant_mask(8, 0), down)
    local = jnp.broadcast_to(local[:, None, :], (8, 8, 512)).reshape(64, 512) * octant_mask(64, 0)
    local = far[:64] + times_pair(local, down)
    out_ref[...] = local * occupancy_mask(occ_ref, spread_ref)


def pairs(axis, outer):
    result = []
    for i in range(512):
        c = place(i, 3)
        c[axis] = (c[axis] ^ 1) if not outer else c[axis] + (1 if c[axis] % 2 else -1)
        if 0 <= c[axis] < 8:
            result.append((i, morton(*c, 3)))
    return result


def exchange(pa, pb, axis):
    return lax.ppermute(pa, "d", pairs(axis, False)), lax.ppermute(pb, "d", pairs(axis, True))


SMEM = pl.BlockSpec(memory_space=pltpu.SMEM)
VMEM = pl.BlockSpec(memory_space=pltpu.VMEM)


def call(kernel, shapes, scratch, *args):
    return pl.pallas_call(
        kernel,
        out_shape=[jax.ShapeDtypeStruct(shape, F32) for shape in shapes],
        in_specs=[SMEM] + [VMEM] * (len(args) - 1),
        out_specs=[VMEM] * len(shapes),
        scratch_shapes=[pltpu.VMEM(shape, F32) for shape in scratch],
        compiler_params=pltpu.CompilerParams(vmem_limit_bytes=48 * 2**20),
    )(*args)


def local(multipoles, occupancy):
    const = {name: jnp.asarray(value) for name, value in constants().items()}
    me = lax.axis_index("d")
    parent = me // 8
    ids = jnp.stack([me % 2, me // 2 % 2, me // 4 % 2, parent, parent % 8, me % 8]).astype(jnp.int32)
    occ = occupancy.reshape(1, 512)
    own, pa, pb, three = call(
        upward_kernel,
        [(ROWS, 512), (Z_ROWS, 512), (Z_ROWS, 512), (8, 128)],
        [],
        ids, multipoles, occ, const["spread"], const["basis"], const["up"],
    )
    za, zb = exchange(pa, pb, 2)
    spread_three = jnp.broadcast_to(three[:1, :64], (512, 64))
    coarse = lax.all_to_all(spread_three, "d", 0, 0, tiled=True).reshape(64, 512)
    pa, pb = call(y_kernel, [(Y_ROWS, 512)] * 2, [(Z_ROWS, 512)] * 2, ids, own, za, zb)
    ya, yb = exchange(pa, pb, 1)
    pa, pb = call(
        x_kernel, [(X_ROWS, 512)] * 2, [(Z_ROWS, 512)] * 2 + [(Y_ROWS, 512)] * 2,
        ids, own, za, zb, ya, yb,
    )
    xa, xb = exchange(pa, pb, 0)
    whole = [own, za, zb, ya, yb, xa, xb, coarse, occ]
    tables = [const[name] for name in ("near", "far", "spread", "basis", "back", "up", "down")]
    full = lambda a: pl.BlockSpec(a.shape, lambda i, s, r=a.ndim: (0,) * r)
    return pl.pallas_call(
        final_kernel,
        out_shape=jax.ShapeDtypeStruct((64, 512), F32),
        grid_spec=pltpu.PrefetchScalarGridSpec(
            num_scalar_prefetch=1,
            grid=(1,),
            in_specs=[full(a) for a in whole]
            + [pl.BlockSpec((1, 216, 128), lambda i, s: (s[3], 0, 0))]
            + [full(a) for a in tables],
            out_specs=pl.BlockSpec((64, 512), lambda i, s: (0, 0)),
            scratch_shapes=[
                pltpu.VMEM((SOURCES, 1024), BF16),
                pltpu.VMEM((4, 2 * ROWS, 27 * 128), BF16),
            ],
        ),
        compiler_params=pltpu.CompilerParams(vmem_limit_bytes=52 * 2**20),
    )(ids, *whole, const["coarse"], *tables)


def solution(mesh):
    line = Mesh(mesh.devices.reshape(-1), ("d",))
    return jax.shard_map(
        local,
        mesh=line,
        in_specs=(P("d", None), P("d")),
        out_specs=P("d", None),
        check_vma=False,
    )
```

time: 781 us -> 79.1 us (0.10)
  the two profiles are of different devices: /device:TPU:1 before, /device:TPU:24 now
where the time goes in v1:
time: 79.1 us; the launch traced here: 78.7 us
  starting transfers between devices  43.9 us (55%)
  Pallas kernels  15.5 us (20%)
  waiting for transfers between devices  11.5 us (15%)
  local copies, waits for them, and re-layouts  6.45 us (8%)
  other arithmetic  1.29 us (2%)
    all_to_all x1, starting transfers between devices, local(): lax.all_to_all(spread_three, 'd', 0, 0, tiled=True).reshape(64, 512)  25.4 us
    pallas_call x1, Pallas kernels, local(): pl.pallas_call(final_kernel, out_shape=jax.ShapeDtypeStruct((64, 512), F3...  12.7 us
    ppermute x3, waiting for transfers between devices, exchange(): lax.ppermute(pb, 'd', pairs(axis, True))  11.5 us
    ppermute x3, starting transfers between devices, exchange(): lax.ppermute(pa, 'd', pairs(axis, False))  9.32 us
    ppermute x3, starting transfers between devices, exchange(): lax.ppermute(pb, 'd', pairs(axis, True))  9.11 us
    unnamed x16, local copies, waits for them, and re-layouts  4.9 us
    pallas_call x3, Pallas kernels, call(): pl.pallas_call(kernel, out_shape=[jax.ShapeDtypeStruct(shape, F32) for sh...  2.8 us
  transfers between devices with their start and end apart: 7, of which 2 were waited for; matrix products, arithmetic and copies ran while one was open for 3% of the time, Pallas kernels for 2%

profile of v1, /device:TPU:24, one launch (start us, length us, event | category | flops | bytes accessed | tf_op | source)
XLA Modules:
  0.0 78.7 jit_solution(5032088349241214025)
XLA Ops:
  0.0 0.0 copy-start.7
  0.0 0.1 stack.27.ids_ref
  0.1 0.0 copy-start
  0.1 1.2 %copy-done = bf16[512,1024]{1,0:T(8,128)(2,1)S(1)} copy-done((bf16[512,1024]{1,0:T(8,128)(2,1)S(1)}, bf16[512,1024]{1,0:T(8,128)(2,1)}, u32[]{:S(2)}) %copy-start) | copy-done | bytes 1048600
  1.3 0.0 copy-start.1
  1.3 1.0 %copy-done.1 = bf16[512,512]{1,0:T(8,128)(2,1)S(1)} copy-done((bf16[512,512]{1,0:T(8,128)(2,1)S(1)}, bf16[512,512]{1,0:T(8,128)(2,1)}, u32[]{:S(2)}) %copy-start.1) | copy-done | bytes 524312
  2.4 0.0 copy-start.3
  2.4 1.0 %copy-done.3 = bf16[512,512]{1,0:T(8,128)(2,1)S(1)} copy-done((bf16[512,512]{1,0:T(8,128)(2,1)S(1)}, bf16[512,512]{1,0:T(8,128)(2,1)}, u32[]{:S(2)}) %copy-start.3) | copy-done | bytes 524312
  3.4 0.0 copy-start.5
  3.4 0.9 %copy-done.5 = f32[64,512]{1,0:T(8,128)S(1)} copy-done((f32[64,512]{1,0:T(8,128)S(1)}, f32[64,512]{1,0:T(8,128)}, u32[]{:S(2)}) %copy-start.5) | copy-done | bytes 131096
  4.3 0.0 copy-start.6
  4.3 0.7 copy-done.6
  5.0 0.0 copy-start.2
  5.0 0.0 copy-start.4
  5.0 1.6 %shard_map.100 = (f32[80,512]{1,0:T(8,128)S(1)}, f32[24,512]{1,0:T(8,128)S(1)}, f32[24,512]{1,0:T(8,128)S(1)}, f32[8,128]{1,0:T(8,128)S(1)}) custom-call(s32[6]{0:T(128)S(1)} %stack.27.ids_ref, f32[64,512]{1,0:T(8,128)S(1)} %copy-done.5, s32[1,512]{1,0:T(1,128)S(1)} %bitcast.9, bf16[512,512]{1,0:T(8,128)(2,1)S(1)} %copy-done.1, ...), custom_call_target="tpu_custom_call" | custom-call | tf_op jit(solution)/shard_map/pallas_call | solution.py:405
  6.6 1.9 %collective-permute-start = (f32[24,512]{1,0:T(8,128)S(1)}, f32[24,512]{1,0:T(8,128)S(1)}, u32[]{:S(2)}, u32[]{:S(2)}) collective-permute-start(f32[24,512]{1,0:T(8,128)S(1)} %get-tuple-element.14), channel_id=1, source_target_pairs={{0,4},{1,5},{2,6},{3,7},{4,0},{5,1},{6,2},{7,3},{8,12},{9,13},{10,... | collective-permute-start | bytes 147464 | tf_op jit(solution)/shard_map/ppermute | solution.py:397
  8.5 0.7 collective-permute-start.1
  9.2 0.8 %broadcast_in_dim.2 = f32[512,1,64]{2,1,0:T(1,128)} broadcast(f32[64]{0:T(128)S(1)} %slice_bitcast_fusion), dimensions={2} | broadcast | bytes 131328 | tf_op jit(solution)/shard_map/broadcast_in_dim | solution.py:428
  10.0 25.4 %all-to-all-start = ((f32[512,1,64]{2,1,0:T(1,128)}), f32[512,1,64]{2,1,0:T(1,128)S(1)}, u32[]{:S(2)}, u32[]{:S(2)}) async-start(f32[512,1,64]{2,1,0:T(1,128)} %broadcast_in_dim.2), calls=%async_computation | async-start | bytes 524288 | tf_op jit(solution)/shard_map/all_to_all | solution.py:429
  35.4 0.0 collective-permute-done.za_ref
  35.5 0.0 collective-permute-done.1.zb_ref
  35.5 0.6 shard_map.101
  36.1 4.9 %collective-permute-start.2 = (f32[40,512]{1,0:T(8,128)S(1)}, f32[40,512]{1,0:T(8,128)S(1)}, u32[]{:S(2)}, u32[]{:S(2)}) collective-permute-start(f32[40,512]{1,0:T(8,128)S(1)} %get-tuple-element.16), channel_id=1, source_target_pairs={{0,2},{1,3},{2,0},{3,1},{4,6},{5,7},{6,4},{7,5},{8,10},{9,11},{10,... | collective-permute-start | bytes 245768 | tf_op jit(solution)/shard_map/ppermute | solution.py:397
  41.0 5.2 %collective-permute-start.3 = (f32[40,512]{1,0:T(8,128)S(1)}, f32[40,512]{1,0:T(8,128)S(1)}, u32[]{:S(2)}, u32[]{:S(2)}) collective-permute-start(f32[40,512]{1,0:T(8,128)S(1)} %get-tuple-element.17), channel_id=1, source_target_pairs={{2,16},{3,17},{6,20},{7,21},{10,24},{11,25},{14,28},{15,29},{16,2}... | collective-permute-start | bytes 245768 | tf_op jit(solution)/shard_map/ppermute | solution.py:397
  46.2 0.0 collective-permute-done.2.ya_ref
  46.2 8.0 %collective-permute-done.3.yb_ref = f32[40,512]{1,0:T(8,128)S(1)} collective-permute-done((f32[40,512]{1,0:T(8,128)S(1)}, f32[40,512]{1,0:T(8,128)S(1)}, u32[]{:S(2)}, u32[]{:S(2)}) %collective-permute-start.3) | collective-permute-done | bytes 81952 | tf_op jit(solution)/shard_map/ppermute | solution.py:397
  54.2 0.6 shard_map.102
  54.9 2.5 %collective-permute-start.4 = (f32[64,512]{1,0:T(8,128)S(1)}, f32[64,512]{1,0:T(8,128)S(1)}, u32[]{:S(2)}, u32[]{:S(2)}) collective-permute-start(f32[64,512]{1,0:T(8,128)S(1)} %get-tuple-element.18), channel_id=1, source_target_pairs={{0,1},{1,0},{2,3},{3,2},{4,5},{5,4},{6,7},{7,6},{8,9},{9,8},{10,11... | collective-permute-start | bytes 393224 | tf_op jit(solution)/shard_map/ppermute | solution.py:397
  57.3 3.3 %collective-permute-start.5 = (f32[64,512]{1,0:T(8,128)S(1)}, f32[64,512]{1,0:T(8,128)S(1)}, u32[]{:S(2)}, u32[]{:S(2)}) collective-permute-start(f32[64,512]{1,0:T(8,128)S(1)} %get-tuple-element.19), channel_id=1, source_target_pairs={{1,8},{3,10},{5,12},{7,14},{8,1},{9,64},{10,3},{11,66},{12,5},{13,... | collective-permute-start | bytes 393224 | tf_op jit(solution)/shard_map/ppermute | solution.py:397
  60.6 0.0 all-to-all-done
  60.6 0.5 broadcast.15
  61.2 1.3 %reduce.3 = f32[512,64]{1,0:T(8,128)S(1)} reduce(f32[512,1,64]{2,1,0:T(1,128)S(1)} %all-to-all-done, f32[]{:T(128)} %broadcast.15), dimensions={1}, to_apply=%all_to_all.4.reduce_sub_computation.3 | reduce | bytes 262148 | tf_op jit(solution)/shard_map/all_to_all | solution.py:429
  62.4 0.1 reshape.14.coarse_ref
  62.6 0.0 collective-permute-done.4.xa_ref
  62.6 3.4 %collective-permute-done.5.xb_ref = f32[64,512]{1,0:T(8,128)S(1)} collective-permute-done((f32[64,512]{1,0:T(8,128)S(1)}, f32[64,512]{1,0:T(8,128)S(1)}, u32[]{:S(2)}, u32[]{:S(2)}) %collective-permute-start.5) | collective-permute-done | bytes 131104 | tf_op jit(solution)/shard_map/ppermute | solution.py:397
  66.0 0.0 copy-done.7
  66.0 0.0 copy-done.2
  66.0 0.0 copy-done.4
  66.0 12.7 %shard_map.103 = f32[64,512]{1,0:T(8,128)} custom-call(s32[6]{0:T(128)S(1)} %stack.27.ids_ref, f32[80,512]{1,0:T(8,128)S(1)} %get-tuple-element.13.own_ref, f32[24,512]{1,0:T(8,128)S(1)} %collective-permute-done.za_ref, f32[24,512]{1,0:T(8,128)S(1)} %collective-permute-done.1.zb_ref, f32[40,512]{1,0:T(8,128)S(1)} %collective-permute-done.2.ya_ref, ...), custom_call_target="tpu_custom_call" | custom-call | tf_op jit(solution)/shard_map/pallas_call | solution.py:440
  (1 shorter events, 0.0 us)
Async XLA Ops:
  0.0 66.0 %copy-start.7 = (s32[512]{0:T(512)S(1)}, s32[512]{0:T(512)}, u32[]{:S(2)}) copy-start(s32[512]{0:T(512)} %param.11) | copy-start | bytes 6148
  0.1 1.2 %copy-start = (bf16[512,1024]{1,0:T(8,128)(2,1)S(1)}, bf16[512,1024]{1,0:T(8,128)(2,1)}, u32[]{:S(2)}) copy-start(bf16[512,1024]{1,0:T(8,128)(2,1)} %constant.86.clone.up_ref) | copy-start | bytes 3145732
  1.3 1.0 %copy-start.1 = (bf16[512,512]{1,0:T(8,128)(2,1)S(1)}, bf16[512,512]{1,0:T(8,128)(2,1)}, u32[]{:S(2)}) copy-start(bf16[512,512]{1,0:T(8,128)(2,1)} %constant.88.clone.spread_ref) | copy-start | bytes 1572868
  2.4 1.0 %copy-start.3 = (bf16[512,512]{1,0:T(8,128)(2,1)S(1)}, bf16[512,512]{1,0:T(8,128)(2,1)}, u32[]{:S(2)}) copy-start(bf16[512,512]{1,0:T(8,128)(2,1)} %constant.84.clone.basis_ref) | copy-start | bytes 1572868
  3.4 0.9 %copy-start.5 = (f32[64,512]{1,0:T(8,128)S(1)}, f32[64,512]{1,0:T(8,128)}, u32[]{:S(2)}) copy-start(f32[64,512]{1,0:T(8,128)} %mult_ref.1) | copy-start | bytes 393220
  4.3 0.7 copy-start.6
  5.0 61.0 %copy-start.2 = (bf16[512,512]{1,0:T(8,128)(2,1)S(1)}, bf16[512,512]{1,0:T(8,128)(2,1)}, u32[]{:S(2)}) copy-start(bf16[512,512]{1,0:T(8,128)(2,1)} %constant.88.clone.spread_ref) | copy-start | bytes 1572868
  5.0 61.0 %copy-start.4 = (bf16[512,512]{1,0:T(8,128)(2,1)S(1)}, bf16[512,512]{1,0:T(8,128)(2,1)}, u32[]{:S(2)}) copy-start(bf16[512,512]{1,0:T(8,128)(2,1)} %constant.84.clone.basis_ref) | copy-start | bytes 1572868
  6.6 28.9 %collective-permute-start = (f32[24,512]{1,0:T(8,128)S(1)}, f32[24,512]{1,0:T(8,128)S(1)}, u32[]{:S(2)}, u32[]{:S(2)}) collective-permute-start(f32[24,512]{1,0:T(8,128)S(1)} %get-tuple-element.14), channel_id=1, source_target_pairs={{0,4},{1,5},{2,6},{3,7},{4,0},{5,1},{6,2},{7,3},{8,12},{9,13},{10,... | collective-permute-start | bytes 147464 | tf_op jit(solution)/shard_map/ppermute | solution.py:397
  8.5 27.0 %collective-permute-start.1 = (f32[24,512]{1,0:T(8,128)S(1)}, f32[24,512]{1,0:T(8,128)S(1)}, u32[]{:S(2)}, u32[]{:S(2)}) collective-permute-start(f32[24,512]{1,0:T(8,128)S(1)} %get-tuple-element.15), channel_id=1, source_target_pairs={{4,32},{5,33},{6,34},{7,35},{12,40},{13,41},{14,42},{15,43},{20,48... | collective-permute-start | bytes 147464 | tf_op jit(solution)/shard_map/ppermute | solution.py:397
  10.0 50.6 %all-to-all-start = ((f32[512,1,64]{2,1,0:T(1,128)}), f32[512,1,64]{2,1,0:T(1,128)S(1)}, u32[]{:S(2)}, u32[]{:S(2)}) async-start(f32[512,1,64]{2,1,0:T(1,128)} %broadcast_in_dim.2), calls=%async_computation | async-start | bytes 524288 | tf_op jit(solution)/shard_map/all_to_all | solution.py:429
  36.1 10.1 %collective-permute-start.2 = (f32[40,512]{1,0:T(8,128)S(1)}, f32[40,512]{1,0:T(8,128)S(1)}, u32[]{:S(2)}, u32[]{:S(2)}) collective-permute-start(f32[40,512]{1,0:T(8,128)S(1)} %get-tuple-element.16), channel_id=1, source_target_pairs={{0,2},{1,3},{2,0},{3,1},{4,6},{5,7},{6,4},{7,5},{8,10},{9,11},{10,... | collective-permute-start | bytes 245768 | tf_op jit(solution)/shard_map/ppermute | solution.py:397
  41.0 13.2 %collective-permute-start.3 = (f32[40,512]{1,0:T(8,128)S(1)}, f32[40,512]{1,0:T(8,128)S(1)}, u32[]{:S(2)}, u32[]{:S(2)}) collective-permute-start(f32[40,512]{1,0:T(8,128)S(1)} %get-tuple-element.17), channel_id=1, source_target_pairs={{2,16},{3,17},{6,20},{7,21},{10,24},{11,25},{14,28},{15,29},{16,2}... | collective-permute-start | bytes 245768 | tf_op jit(solution)/shard_map/ppermute | solution.py:397
  54.9 7.7 %collective-permute-start.4 = (f32[64,512]{1,0:T(8,128)S(1)}, f32[64,512]{1,0:T(8,128)S(1)}, u32[]{:S(2)}, u32[]{:S(2)}) collective-permute-start(f32[64,512]{1,0:T(8,128)S(1)} %get-tuple-element.18), channel_id=1, source_target_pairs={{0,1},{1,0},{2,3},{3,2},{4,5},{5,4},{6,7},{7,6},{8,9},{9,8},{10,11... | collective-permute-start | bytes 393224 | tf_op jit(solution)/shard_map/ppermute | solution.py:397
  57.3 8.7 %collective-permute-start.5 = (f32[64,512]{1,0:T(8,128)S(1)}, f32[64,512]{1,0:T(8,128)S(1)}, u32[]{:S(2)}, u32[]{:S(2)}) collective-permute-start(f32[64,512]{1,0:T(8,128)S(1)} %get-tuple-element.19), channel_id=1, source_target_pairs={{1,8},{3,10},{5,12},{7,14},{8,1},{9,64},{10,3},{11,66},{12,5},{13,... | collective-permute-start | bytes 393224 | tf_op jit(solution)/shard_map/ppermute | solution.py:397

commit v2 on v1

v2 whole, which is shorter than its diff:
```python
import functools

import jax
import jax.numpy as jnp
import ml_dtypes
import numpy as np
from jax import lax
from jax.experimental import pallas as pl
from jax.experimental.pallas import tpu as pltpu
from jax.sharding import Mesh
from jax.sharding import PartitionSpec as P

F32 = jnp.float32
BF16 = jnp.bfloat16
NODES = np.cos((2.0 * np.arange(4) + 1.0) * (np.pi / 8.0))
ENTRY = np.arange(512)
OCT = [ENTRY // 64 % 2, ENTRY // 128 % 2, ENTRY // 256 % 2]
DEG = [ENTRY // 16 % 4, ENTRY // 4 % 4, ENTRY % 4]
KINDS = [(dx, ky, kz) for dx in (-1, 0, 1) for ky in range(3) for kz in range(3)]
ROWS = 80
SMALL = 16
PIECES = {
    "up": 512, "basis": 1024, "small": 432, "fine": 1728, "far": 13824, "back": 1024, "down": 512,
    "coarse": 64 * 224,
}


def halves(values):
    high = values.astype(np.float32).astype(ml_dtypes.bfloat16)
    low = (values - high.astype(np.float64)).astype(ml_dtypes.bfloat16)
    return high, low


def table(shift):
    distance = np.zeros((512, 512))
    reach = np.zeros((512, 512), int)
    for d in range(3):
        offset = 2 * shift[d] + OCT[d][:, None] - OCT[d][None, :]
        reach = np.maximum(reach, abs(offset))
        placed = NODES[DEG[d]]
        distance += (offset + 0.5 * (placed[:, None] - placed[None, :])) ** 2
    keep = reach >= 2
    return np.where(keep, 1.0 / np.sqrt(np.where(keep, distance, 1.0)), 0.0)


def upward_matrix():
    def terms(v):
        return [v, 2 * v * v - 1, 4 * v**3 - 3 * v]

    parent = np.arange(64)
    degrees = [parent // 16, parent // 4 % 4, parent % 4]
    result = np.ones((512, 64))
    for d in range(3):
        child = (OCT[d] - 0.5 + 0.5 * NODES[DEG[d]])[:, None]
        place = NODES[degrees[d]][None, :]
        result *= 0.25 + 0.5 * sum(a * b for a, b in zip(terms(place), terms(child)))
    return result


def parity_basis():
    basis = np.zeros((512, 512))
    for q in range(512):
        cy, cz = q // 128 % 2, q // 256
        ox, a, vy, vz = q // 64 % 2, q // 16 % 4, q // 4 % 4, q % 4
        for oy in range(2):
            for oz in range(2):
                b = 3 - vy if oy else vy
                e = 3 - vz if oz else vz
                sign = (-1) ** (cy * oy + cz * oz)
                basis[64 * (ox + 2 * oy + 4 * oz) + 16 * a + 4 * b + e, q] = 0.5 * sign
    return basis


def morton(x, y, z, bits):
    return sum(
        (x >> i & 1) << 3 * i | (y >> i & 1) << 3 * i + 1 | (z >> i & 1) << 3 * i + 2
        for i in range(bits)
    )


def place(number, bits):
    return [sum((number >> 3 * i + d & 1) << i for i in range(bits)) for d in range(3)]


Z_ROWS, Y_ROWS, X_ROWS = 24, 40, 64
Z_THREE, Y_THREE = 21, 35
FINE_PARTS = ((0, 64), (0, 16), (0, 16), (0, 24), (0, 24), (0, 40), (0, 40))
SMALL_PARTS = ((64, 80), (16, 24), (16, 24), (24, 40), (24, 40), (32, 64), (32, 64))


def level_extent(level):
    return 2 ** (level - 4)


def own_row(level, x, y, z):
    return {6: 0, 5: 64, 4: 72}[level] + morton(x, y, z, level - 4)


def z_row(level, x, y):
    n = level_extent(level)
    return {6: 0, 5: 16, 4: 20}[level] + y * n + x


def y_row(level, x, z):
    n = level_extent(level)
    return {6: 0, 5: 24, 4: 32}[level] + (z + 1) * n + x


def x_row(level, y, z):
    n = level_extent(level) + 2
    return {6: 0, 5: 36, 4: 52}[level] + (z + 1) * n + y + 1


def source_row(level, x, y, z):
    n = level_extent(level)
    if not 0 <= x < n:
        part, row = (6 if x >= n else 5), x_row(level, y, z)
    elif not 0 <= y < n:
        part, row = (4 if y >= n else 3), y_row(level, x, z)
    elif not 0 <= z < n:
        part, row = (2 if z >= n else 1), z_row(level, x, y)
    else:
        part, row = 0, own_row(level, x, y, z)
    parts = FINE_PARTS if level == 6 else SMALL_PARTS
    start, stop = parts[part]
    assert start <= row < stop
    return sum(q - p for p, q in parts[:part]) + row - start


def kind_terms(kind):
    return [(0, 1)] if kind == 0 else [(1, 1), (-1, 1 if kind == 1 else -1)]


def selections():
    fine = np.zeros((27, 64, 256))
    small = np.zeros((27, SMALL, 128))
    for k, (dx, ky, kz) in enumerate(KINDS):
        for dy, sy in kind_terms(ky):
            for dz, sz in kind_terms(kz):
                for level in (6, 5, 4):
                    n = level_extent(level)
                    into = fine[k] if level == 6 else small[k]
                    for m in range(n**3):
                        x, y, z = place(m, level - 4)
                        row = own_row(level, x, y, z) % 64
                        into[row, source_row(level, x + dx, y + dy, z + dz)] += (
                            sy * sz * 2.0 ** (level - 6)
                        )
    coarse = np.zeros((64, 27, SMALL, 128))
    for parent in range(64):
        for level, row, base in ((3, 9, 0), (2, 10, 64)):
            bits = level - 1
            n = 2**bits
            x, y, z = place(parent >> 3 * (2 - bits), bits)
            for k, (dx, ky, kz) in enumerate(KINDS):
                for dy, sy in kind_terms(ky):
                    for dz, sz in kind_terms(kz):
                        u = (x + dx, y + dy, z + dz)
                        if all(0 <= c < n for c in u):
                            coarse[parent, k, row, base + morton(*u, bits)] += (
                                sy * sz * 2.0 ** (level - 6)
                            )
    return (
        fine.reshape(27 * 64, 256).astype(ml_dtypes.bfloat16),
        small.reshape(27 * SMALL, 128).astype(ml_dtypes.bfloat16),
        np.concatenate(
            np.split(np.pad(coarse.reshape(64, 27 * SMALL, 128), ((0, 0), (0, 16), (0, 0))), 2, axis=1),
            axis=2,
        ).reshape(64 * 224, 256),
    )


@functools.lru_cache(maxsize=1)
def constants():
    basis = parity_basis()
    tables = {
        (dx, dy, dz): basis.T @ table((dx, dy, dz)) @ basis
        for dx in (-1, 0, 1)
        for dy in (0, 1)
        for dz in (0, 1)
    }
    far = np.zeros((4, 27 * 128, 256), ml_dtypes.bfloat16)
    for t in range(4):
        for k, (dx, ky, kz) in enumerate(KINDS):
            c = source_class(t, ky, kz)
            block = tables[dx, min(ky, 1), min(kz, 1)][
                128 * c : 128 * c + 128, 128 * t : 128 * t + 128
            ]
            high, low = halves(block)
            far[t, 128 * k : 128 * k + 128, :128] = high
            far[t, 128 * k : 128 * k + 128, 128:] = low
    up = upward_matrix()
    fine, small, coarse = selections()
    wide_down = np.concatenate(halves(np.tile(up.T, (2, 1))), axis=1)
    pieces = {
        "up": np.concatenate(halves(np.tile(up, (1, 2))), axis=1),
        "basis": in_lanes(basis),
        "small": np.pad(small, ((0, 0), (0, 128))),
        "fine": fine,
        "far": far.reshape(-1, 256),
        "back": in_lanes(basis.T),
        "down": in_lanes(wide_down),
        "coarse": coarse,
    }
    assert {name: len(piece) for name, piece in pieces.items()} == PIECES
    return np.concatenate([piece.astype(ml_dtypes.bfloat16) for piece in pieces.values()])


def in_lanes(matrix):
    return np.concatenate(np.split(matrix, matrix.shape[1] // 256, axis=1))


def source_class(t, ky, kz):
    return t ^ ((ky == 2) | (kz == 2) << 1)


def split(values):
    high = values.astype(BF16)
    return high, (values - high.astype(F32)).astype(BF16)


def mm(a, b):
    return jnp.dot(a, b, preferred_element_type=F32)


def stacked(values):
    rows, width = values.shape
    if rows % 16:
        values = jnp.concatenate([values, jnp.zeros((16 - rows % 16, width), F32)], axis=0)
    return jnp.concatenate(split(values), axis=0)


def times_exact(values, matrix):
    product = mm(stacked(values), matrix)
    half = product.shape[0] // 2
    return (product[:half] + product[half:])[: values.shape[0]]


def times_pair(values, matrix):
    product = mm(stacked(values), matrix)
    half = product.shape[0] // 2
    width = product.shape[1] // 2
    total = product[:half, :width] + product[half:, :width] + product[:half, width:]
    return total[: values.shape[0]]


def exact_times(matrix, values):
    product = mm(matrix, jnp.concatenate(split(values), axis=1))
    width = values.shape[1]
    return product[:, :width] + product[:, width:]


def piece_copy(blob, name, ref, sem, part=0, parts=1):
    start = sum(list(PIECES.values())[: list(PIECES).index(name)])
    rows = PIECES[name] // parts
    source = blob.at[pl.ds(pl.multiple_of(start + part * rows, 16), rows)]
    target = ref if ref.shape[0] == rows else ref.at[pl.ds(part * rows, rows)]
    return pltpu.make_async_copy(source, target, sem)


def in_columns(ref):
    rows = ref.shape[0] // 2
    return jnp.concatenate([ref[:rows], ref[rows:]], axis=1)


def iota(shape, axis):
    return lax.broadcasted_iota(jnp.int32, shape, axis)


def octant_mask(rows):
    return (iota((rows, 512), 1) // 64 == iota((rows, 512), 0) % 8).astype(F32)


def occupancy_mask(occ):
    kept = jnp.where(
        iota((64, 512), 1) // 8 == iota((64, 512), 0), jnp.broadcast_to(occ.astype(F32), (64, 512)), 0.0
    )
    spread = iota((512, 512), 0) % 8 == iota((512, 512), 1) // 64
    return mm(kept.astype(BF16), jnp.where(spread, 1.0, 0.0).astype(BF16))


def upward(values, up):
    twice = times_pair(values, up)
    return jnp.concatenate([twice] * 4, axis=1)


def up_group(values, up):
    rows = values.shape[0]
    return (upward(values, up) * octant_mask(rows)).reshape(rows // 8, 8, 512).sum(axis=1)


def downward(masked, down):
    folded = masked[:, :128] + masked[:, 128:256] + masked[:, 256:384] + masked[:, 384:]
    return times_pair(folded, down)


def upward_kernel(
    ids_ref, mult_hbm, occ_hbm, blob, own_ref, pa_ref, pb_ref, mask_ref,
    mult_ref, occ_ref, up_ref, basis_ref, sem,
):
    copies = [
        pltpu.make_async_copy(occ_hbm, occ_ref, sem.at[0]),
        pltpu.make_async_copy(mult_hbm, mult_ref, sem.at[1]),
        piece_copy(blob, "up", up_ref, sem.at[2]),
        piece_copy(blob, "basis", basis_ref, sem.at[3]),
    ]
    for copy in copies:
        copy.start()
    copies[0].wait()
    mask_ref[...] = occupancy_mask(occ_ref[...])
    copies[1].wait()
    copies[2].wait()
    grouped_six = mult_ref[...] * mask_ref[...]
    grouped_five = up_group(grouped_six, up_ref[...])
    grouped_four = up_group(grouped_five, up_ref[...])
    three = upward(jnp.broadcast_to(grouped_four, (8, 512)), up_ref[...])
    copies[3].wait()
    basis = in_columns(basis_ref)
    own_ref[0:64] = times_exact(grouped_six, basis)
    rest = jnp.concatenate([grouped_five, jnp.broadcast_to(grouped_four, (8, 512))], axis=0)
    own_ref[64:80] = times_exact(rest, basis)
    odd = ids_ref[2] == 1
    for p_ref in (pa_ref, pb_ref):
        p_ref[Z_ROWS - 8 :] = three
    for level in (6, 5, 4):
        n = level_extent(level)
        for y in range(n):
            for x in range(n):
                low = own_ref[pl.ds(own_row(level, x, y, 0), 1)]
                high = own_ref[pl.ds(own_row(level, x, y, n - 1), 1)]
                i = z_row(level, x, y)
                pa_ref[pl.ds(i, 1)] = jnp.where(odd, low, high)
                pb_ref[pl.ds(i, 1)] = jnp.where(odd, high, low)


def sort_sides(odd, ra_ref, rb_ref, low_ref, high_ref):
    a, b = ra_ref[...], rb_ref[...]
    low_ref[...] = jnp.where(odd, a, b)
    high_ref[...] = jnp.where(odd, b, a)


def y_kernel(ids_ref, own_ref, sent_ref, za_ref, zb_ref, pa_ref, pb_ref, zl, zh):
    sort_sides(ids_ref[2] == 1, za_ref, zb_ref, zl, zh)
    odd = ids_ref[1] == 1
    pa_ref[...] = jnp.zeros_like(pa_ref)
    pb_ref[...] = jnp.zeros_like(pb_ref)
    mine, other = sent_ref[pl.ds(Z_THREE, 1)], za_ref[pl.ds(Z_THREE, 1)]
    pa_ref[pl.ds(Y_THREE, 1)] = jnp.where(
        iota((1, 512), 1) // 128 % 2 == ids_ref[2], mine, other
    )

    def get(level, x, y, z):
        n = level_extent(level)
        if z < 0:
            return zl[pl.ds(z_row(level, x, y), 1)]
        if z >= n:
            return zh[pl.ds(z_row(level, x, y), 1)]
        return own_ref[pl.ds(own_row(level, x, y, z), 1)]

    for level in (6, 5, 4):
        n = level_extent(level)
        for z in range(-1, n + 1):
            for x in range(n):
                low, high = get(level, x, 0, z), get(level, x, n - 1, z)
                i = y_row(level, x, z)
                pa_ref[pl.ds(i, 1)] = jnp.where(odd, low, high)
                pb_ref[pl.ds(i, 1)] = jnp.where(odd, high, low)


def x_kernel(ids_ref, own_ref, za_ref, zb_ref, ya_ref, yb_ref, pa_ref, pb_ref, zl, zh, yl, yh):
    sort_sides(ids_ref[2] == 1, za_ref, zb_ref, zl, zh)
    sort_sides(ids_ref[1] == 1, ya_ref, yb_ref, yl, yh)
    odd = ids_ref[0] == 1
    pa_ref[...] = jnp.zeros_like(pa_ref)
    pb_ref[...] = jnp.zeros_like(pb_ref)

    def get(level, x, y, z):
        n = level_extent(level)
        if y < 0:
            return yl[pl.ds(y_row(level, x, z), 1)]
        if y >= n:
            return yh[pl.ds(y_row(level, x, z), 1)]
        if z < 0:
            return zl[pl.ds(z_row(level, x, y), 1)]
        if z >= n:
            return zh[pl.ds(z_row(level, x, y), 1)]
        return own_ref[pl.ds(own_row(level, x, y, z), 1)]

    for level in (6, 5, 4):
        n = level_extent(level)
        for z in range(-1, n + 1):
            for y in range(-1, n + 1):
                low, high = get(level, 0, y, z), get(level, n - 1, y, z)
                i = x_row(level, y, z)
                pa_ref[pl.ds(i, 1)] = jnp.where(odd, low, high)
                pb_ref[pl.ds(i, 1)] = jnp.where(odd, high, low)


def coarse_rows(quads):
    half = iota((128, 128), 1) // 64
    keep = half == iota((128, 128), 0) % 2
    blocks = []
    for i in range(4):
        pair = quads[:, 128 * (i // 2) : 128 * (i // 2) + 128]
        both = jnp.where(half == i % 2, pair, pltpu.roll(pair, 64, 1))
        blocks.append(jnp.where(keep, both, 0.0))
    gather = jnp.where(iota((64, 128), 0) == iota((64, 128), 1) // 2, 1.0, 0.0).astype(BF16)
    return exact_times(gather, jnp.concatenate(blocks, axis=1))


def final_kernel(
    ids_ref, own_ref, za_ref, zb_ref, ya_ref, yb_ref, xa_ref, xb_ref, quads_ref, mask_ref, blob,
    out_ref, fine_src, small_src, wide, coarse_ref, up_ref, basis_ref, small_ref, fine_ref, far_ref,
    back_ref, down_ref, sem,
):
    small_copy = piece_copy(blob, "small", small_ref, sem.at[0])
    fine_copy = piece_copy(blob, "fine", fine_ref, sem.at[1])
    up_copy = piece_copy(blob, "up", up_ref, sem.at[2])
    basis_copy = piece_copy(blob, "basis", basis_ref, sem.at[3])
    coarse_copy = piece_copy(blob, "coarse", coarse_ref, sem.at[4], ids_ref[3], 64)
    far_copies = [piece_copy(blob, "far", far_ref, sem.at[5 + t], t, 4) for t in range(4)]
    back_copy = piece_copy(blob, "back", back_ref, sem.at[9])
    down_copy = piece_copy(blob, "down", down_ref, sem.at[10])
    first = (small_copy, up_copy, basis_copy, coarse_copy, fine_copy)
    for copy in (*first, *far_copies, back_copy, down_copy):
        copy.start()
    fine_src[224:] = jnp.zeros((32, 512), F32)
    stack = [own_ref[...]]
    for axis, ra_ref, rb_ref in ((2, za_ref, zb_ref), (1, ya_ref, yb_ref), (0, xa_ref, xb_ref)):
        odd = ids_ref[axis] == 1
        a, b = ra_ref[...], rb_ref[...]
        stack += [jnp.where(odd, a, b), jnp.where(odd, b, a)]
    for target, parts in ((fine_src, FINE_PARTS), (small_src, SMALL_PARTS)):
        base = 0
        for values, (start, stop) in zip(stack, parts):
            target[base : base + stop - start] = values[start:stop]
            base += stop - start

    small_copy.wait()
    small = exact_times(small_ref[:, :128], small_src[...])
    three = coarse_rows(quads_ref[...])
    up_copy.wait()
    two = up_group(three, up_ref[...])
    upper = jnp.concatenate([three, two, jnp.zeros((56, 512), F32)], axis=0)
    basis_copy.wait()
    upper = times_exact(upper, in_columns(basis_ref))
    coarse_copy.wait()
    chosen = jnp.concatenate([coarse_ref[:, :128], coarse_ref[:208, 128:]], axis=0)
    small = small + exact_times(chosen, upper)

    fine_split = jnp.concatenate(split(fine_src[...]), axis=1)
    fine_copy.wait()
    for group in range(3):
        mixes = mm(fine_ref[576 * group : 576 * group + 576], fine_split)
        mixes = mixes[:, :512] + mixes[:, 512:]
        for j in range(9):
            k = 9 * group + j
            _, ky, kz = KINDS[k]
            mix = jnp.concatenate(
                [mixes[64 * j : 64 * j + 64], small[SMALL * k : SMALL * k + SMALL]], axis=0
            )
            high, low = split(mix)
            for t in range(4):
                c = source_class(t, ky, kz)
                wide[t, :ROWS, 128 * k : 128 * k + 128] = high[:, 128 * c : 128 * c + 128]
                wide[t, ROWS:, 128 * k : 128 * k + 128] = low[:, 128 * c : 128 * c + 128]
    parts = []
    for t in range(4):
        far_copies[t].wait()
        product = mm(wide[t], far_ref[3456 * t : 3456 * t + 3456])
        parts.append(
            product[:ROWS, :128] + product[ROWS:, :128] + product[:ROWS, 128:] + product[ROWS:, 128:]
        )
    back_copy.wait()
    far = times_exact(jnp.concatenate(parts, axis=1), in_columns(back_ref))
    down_copy.wait()

    lane = iota((8, 512), 1) // 64
    down = jnp.concatenate([down_ref[128 * i : 128 * i + 128] for i in range(4)], axis=1)

    def only(row, octant):
        return jnp.where(lane == octant, jnp.broadcast_to(row, (8, 512)), 0.0)

    local = far[73:74] + downward(only(far[74:75], ids_ref[4]), down)
    local = far[72:73] + downward(only(local[:1], ids_ref[5]), down)
    local = far[64:72] + downward(jnp.broadcast_to(local[:1], (8, 512)) * octant_mask(8), down)
    local = jnp.broadcast_to(local[:, None, :], (8, 8, 512)).reshape(64, 512) * octant_mask(64)
    out_ref[...] = (far[:64] + downward(local, down)) * mask_ref[...]


def pairs(axis, outer):
    result = []
    for i in range(512):
        c = place(i, 3)
        c[axis] = (c[axis] ^ 1) if not outer else c[axis] + (1 if c[axis] % 2 else -1)
        if 0 <= c[axis] < 8:
            result.append((i, morton(*c, 3)))
    return result


def exchange(pa, pb, axis):
    return (
        lax.ppermute(pa, AXES, pairs(axis, False)),
        lax.ppermute(pb, AXES, pairs(axis, True)),
    )


SMEM = pl.BlockSpec(memory_space=pltpu.SMEM)
VMEM = pl.BlockSpec(memory_space=pltpu.VMEM)
HBM = pl.BlockSpec(memory_space=pltpu.HBM)
AXES = ("upper", "bit2", "bit1", "bit0")
LIMIT = 52 * 2**20


def call(kernel, shapes, scratch, ids, vmem_args, hbm_args=(), micros=1):
    return pl.pallas_call(
        kernel,
        out_shape=[jax.ShapeDtypeStruct(shape, F32) for shape in shapes],
        in_specs=[SMEM] + [VMEM] * len(vmem_args) + [HBM] * len(hbm_args),
        out_specs=[VMEM] * len(shapes),
        scratch_shapes=scratch,
        compiler_params=pltpu.CompilerParams(vmem_limit_bytes=LIMIT),
        cost_estimate=pl.CostEstimate(flops=micros * 10**9, bytes_accessed=0, transcendentals=0),
    )(ids, *vmem_args, *hbm_args)


def rows_of(*counts):
    return [(count, 512) for count in counts]


def scratch_rows(*counts):
    return [pltpu.VMEM((count, 512), F32) for count in counts]


def table_scratch(*names):
    return [pltpu.VMEM((PIECES[name], 256), BF16) for name in names]


def local(multipoles, occupancy):
    blob = jnp.asarray(constants())
    me = lax.axis_index(AXES)
    parent = me // 8
    ids = jnp.stack([me % 2, me // 2 % 2, me // 4 % 2, parent, parent % 8, me % 8]).astype(jnp.int32)
    own, pa, pb, mask = call(
        upward_kernel,
        rows_of(ROWS, Z_ROWS, Z_ROWS, 64),
        scratch_rows(64)
        + [pltpu.VMEM((1, 512), jnp.int32)]
        + table_scratch("up", "basis")
        + [pltpu.SemaphoreType.DMA((4,))],
        ids, [], [multipoles, occupancy.reshape(1, 512), blob], micros=4,
    )
    za, zb = exchange(pa, pb, 2)
    pa, pb = call(
        y_kernel, rows_of(Y_ROWS, Y_ROWS), scratch_rows(Z_ROWS, Z_ROWS), ids, [own, pa, za, zb]
    )
    ya, yb = exchange(pa, pb, 1)
    ours, theirs = (p[Y_THREE : Y_THREE + 1, :256] for p in (pa, ya))
    quad = jnp.where(jnp.arange(256)[None] // 64 % 2 == ids[1], ours, theirs)
    quads = lax.all_to_all(
        jnp.broadcast_to(quad, (128, 256)), ("upper", "bit0"), 0, 0, tiled=True
    )
    pa, pb = call(
        x_kernel, rows_of(X_ROWS, X_ROWS), scratch_rows(Z_ROWS, Z_ROWS, Y_ROWS, Y_ROWS),
        ids, [own, za, zb, ya, yb], micros=40,
    )
    xa, xb = exchange(pa, pb, 0)
    (out,) = call(
        final_kernel,
        rows_of(64),
        scratch_rows(256, 128)
        + [pltpu.VMEM((4, 2 * ROWS, 27 * 128), BF16), pltpu.VMEM((224, 256), BF16)]
        + table_scratch(*list(PIECES)[:-1])
        + [pltpu.SemaphoreType.DMA((11,))],
        ids, [own, za, zb, ya, yb, xa, xb, quads, mask], [blob], micros=8,
    )
    return out


def solution(mesh):
    fine_mesh = Mesh(mesh.devices.reshape(64, 2, 2, 2), AXES)
    return jax.shard_map(
        local,
        mesh=fine_mesh,
        in_specs=(P(AXES, None), P(AXES)),
        out_specs=P(AXES, None),
        check_vma=False,
    )
```

time: 79.1 us -> 66.9 us (0.85)
  the two profiles are of different devices: /device:TPU:24 before, /device:TPU:1 now
where the time goes in v2:
time: 66.9 us; the launch traced here: 66.5 us
  starting transfers between devices  40 us (60%)
  Pallas kernels  12.4 us (19%)
  waiting for transfers between devices  11.6 us (17%)
  local copies, waits for them, and re-layouts  2.41 us (4%)
    all_to_all x1, starting transfers between devices, local(): lax.all_to_all(jnp.broadcast_to(quad, (128, 256)), ('upper', 'bit0'), 0,...  17.6 us
    ppermute x3, starting transfers between devices, exchange(): lax.ppermute(pb, AXES, pairs(axis, True))  13.4 us
    pallas_call x4, Pallas kernels, call(): pl.pallas_call(kernel, out_shape=[jax.ShapeDtypeStruct(shape, F32) for sh...  12.4 us
    ppermute x3, starting transfers between devices, exchange(): lax.ppermute(pa, AXES, pairs(axis, False))  9.05 us
    all_to_all x1, waiting for transfers between devices, local(): lax.all_to_all(jnp.broadcast_to(quad, (128, 256)), ('upper', 'bit0'), 0,...  8.4 us
    ppermute x3, waiting for transfers between devices, exchange(): lax.ppermute(pa, AXES, pairs(axis, False))  3.15 us
    unnamed x5, local copies, waits for them, and re-layouts  1.6 us
  transfers between devices with their start and end apart: 7, of which 3 were waited for; matrix products, arithmetic and copies ran while one was open for 1% of the time, Pallas kernels for 1%

profile of v2, /device:TPU:1, one launch (start us, length us, event | category | flops | bytes accessed | tf_op | source)
XLA Modules:
  0.0 66.5 jit_solution(3112763008009181987)
XLA Ops:
  0.0 0.1 stack.27.ids_ref
  0.1 0.0 copy-start
  0.1 0.9 %copy-done = f32[64,512]{1,0:T(8,128)S(1)} copy-done((f32[64,512]{1,0:T(8,128)S(1)}, f32[64,512]{1,0:T(8,128)}, u32[]{:S(2)}) %copy-start) | copy-done | bytes 131096
  1.0 0.0 copy-start.1
  1.0 0.7 %copy-done.1 = s32[512]{0:T(512)S(1)} copy-done((s32[512]{0:T(512)S(1)}, s32[512]{0:T(512)}, u32[]{:S(2)}) %copy-start.1) | copy-done | bytes 2072
  1.7 2.5 %shard_map.37 = (f32[80,512]{1,0:T(8,128)S(1)}, f32[24,512]{1,0:T(8,128)S(1)}, f32[24,512]{1,0:T(8,128)S(1)}, f32[64,512]{1,0:T(8,128)S(1)}) custom-call(s32[6]{0:T(128)S(1)} %stack.27.ids_ref, f32[64,512]{1,0:T(8,128)S(1)} %copy-done, s32[1,512]{1,0:T(1,128)S(1)} %bitcast.12, bf16[33392,256]{1,0:T(8,128)(2,1)} %constant.106.clone.blob), custom_call_target="tpu_custom_call" | custom-call | flops 4000000000 | tf_op jit(solution)/shard_map/pallas_call | solution.py:516
  4.2 12.0 %collective-permute-start.1 = (f32[24,512]{1,0:T(8,128)S(1)}, f32[24,512]{1,0:T(8,128)S(1)}, u32[]{:S(2)}, u32[]{:S(2)}) collective-permute-start(f32[24,512]{1,0:T(8,128)S(1)} %get-tuple-element.15), channel_id=1, source_target_pairs={{4,32},{5,33},{6,34},{7,35},{12,40},{13,41},{14,42},{15,43},{20,48... | collective-permute-start | bytes 147464 | tf_op jit(solution)/shard_map/ppermute | solution.py:504
  16.2 1.9 %collective-permute-start = (f32[24,512]{1,0:T(8,128)S(1)}, f32[24,512]{1,0:T(8,128)S(1)}, u32[]{:S(2)}, u32[]{:S(2)}) collective-permute-start(f32[24,512]{1,0:T(8,128)S(1)} %get-tuple-element.14.sent_ref), channel_id=1, source_target_pairs={{0,4},{1,5},{2,6},{3,7},{4,0},{5,1},{6,2},{7,3},{8,12},{9,13},{10,... | collective-permute-start | bytes 147464 | tf_op jit(solution)/shard_map/ppermute | solution.py:503
  18.2 0.0 collective-permute-done.1.zb_ref
  18.2 1.2 %collective-permute-done.za_ref = f32[24,512]{1,0:T(8,128)S(1)} collective-permute-done((f32[24,512]{1,0:T(8,128)S(1)}, f32[24,512]{1,0:T(8,128)S(1)}, u32[]{:S(2)}, u32[]{:S(2)}) %collective-permute-start) | collective-permute-done | bytes 49184 | tf_op jit(solution)/shard_map/ppermute | solution.py:503
  19.4 0.6 shard_map.38
  20.0 4.7 %collective-permute-start.2 = (f32[40,512]{1,0:T(8,128)S(1)}, f32[40,512]{1,0:T(8,128)S(1)}, u32[]{:S(2)}, u32[]{:S(2)}) collective-permute-start(f32[40,512]{1,0:T(8,128)S(1)} %get-tuple-element.16), channel_id=1, source_target_pairs={{0,2},{1,3},{2,0},{3,1},{4,6},{5,7},{6,4},{7,5},{8,10},{9,11},{10,... | collective-permute-start | bytes 245768 | tf_op jit(solution)/shard_map/ppermute | solution.py:503
  24.6 0.7 %collective-permute-start.3 = (f32[40,512]{1,0:T(8,128)S(1)}, f32[40,512]{1,0:T(8,128)S(1)}, u32[]{:S(2)}, u32[]{:S(2)}) collective-permute-start(f32[40,512]{1,0:T(8,128)S(1)} %get-tuple-element.17), channel_id=1, source_target_pairs={{2,16},{3,17},{6,20},{7,21},{10,24},{11,25},{14,28},{15,29},{16,2}... | collective-permute-start | bytes 245768 | tf_op jit(solution)/shard_map/ppermute | solution.py:504
  25.3 2.0 %collective-permute-done.2.ya_ref = f32[40,512]{1,0:T(8,128)S(1)} collective-permute-done((f32[40,512]{1,0:T(8,128)S(1)}, f32[40,512]{1,0:T(8,128)S(1)}, u32[]{:S(2)}, u32[]{:S(2)}) %collective-permute-start.2) | collective-permute-done | bytes 81952 | tf_op jit(solution)/shard_map/ppermute | solution.py:503
  27.3 0.7 %broadcast_in_dim.2 = f32[128,1,256]{2,1,0:T(1,128)} broadcast(f32[256]{0:T(256)S(1)} %bitcast.13), dimensions={2} | broadcast | bytes 132096 | tf_op jit(solution)/shard_map/broadcast_in_dim | solution.py:561
  28.0 17.6 %all-to-all-start = ((f32[128,1,256]{2,1,0:T(1,128)}), f32[128,1,256]{2,1,0:T(1,128)S(1)}, u32[]{:S(2)}, u32[]{:S(2)}) async-start(f32[128,1,256]{2,1,0:T(1,128)} %broadcast_in_dim.2), calls=%async_computation | async-start | bytes 262144 | tf_op jit(solution)/shard_map/all_to_all | solution.py:560
  45.6 0.0 collective-permute-done.3.yb_ref
  45.6 0.6 shard_map.39
  46.3 2.5 %collective-permute-start.4 = (f32[64,512]{1,0:T(8,128)S(1)}, f32[64,512]{1,0:T(8,128)S(1)}, u32[]{:S(2)}, u32[]{:S(2)}) collective-permute-start(f32[64,512]{1,0:T(8,128)S(1)} %get-tuple-element.18), channel_id=1, source_target_pairs={{0,1},{1,0},{2,3},{3,2},{4,5},{5,4},{6,7},{7,6},{8,9},{9,8},{10,11... | collective-permute-start | bytes 393224 | tf_op jit(solution)/shard_map/ppermute | solution.py:503
  48.8 0.7 %collective-permute-start.5 = (f32[64,512]{1,0:T(8,128)S(1)}, f32[64,512]{1,0:T(8,128)S(1)}, u32[]{:S(2)}, u32[]{:S(2)}) collective-permute-start(f32[64,512]{1,0:T(8,128)S(1)} %get-tuple-element.19), channel_id=1, source_target_pairs={{1,8},{3,10},{5,12},{7,14},{8,1},{9,64},{10,3},{11,66},{12,5},{13,... | collective-permute-start | bytes 393224 | tf_op jit(solution)/shard_map/ppermute | solution.py:504
  49.4 8.4 %all-to-all-done = f32[128,1,256]{2,1,0:T(1,128)S(1)} async-done(((f32[128,1,256]{2,1,0:T(1,128)}), f32[128,1,256]{2,1,0:T(1,128)S(1)}, u32[]{:S(2)}, u32[]{:S(2)}) %all-to-all-start) | async-done | bytes 131104 | tf_op jit(solution)/shard_map/all_to_all | solution.py:560
  57.8 0.0 collective-permute-done.4.xa_ref
  57.9 0.0 collective-permute-done.5.xb_ref
  57.9 8.7 %shard_map.40 = f32[64,512]{1,0:T(8,128)} custom-call(s32[6]{0:T(128)S(1)} %stack.27.ids_ref, f32[80,512]{1,0:T(8,128)S(1)} %get-tuple-element.13.own_ref, f32[24,512]{1,0:T(8,128)S(1)} %collective-permute-done.za_ref, f32[24,512]{1,0:T(8,128)S(1)} %collective-permute-done.1.zb_ref, f32[40,512]{1,0:T(8,128)S(1)} %collective-permute-done.2.ya_ref, ...), custom_call_target="tpu_custom_call" | custom-call | flops 8000000000 | tf_op jit(solution)/shard_map/pallas_call | solution.py:516
  (2 shorter events, 0.0 us)
Async XLA Ops:
  0.1 0.9 %copy-start = (f32[64,512]{1,0:T(8,128)S(1)}, f32[64,512]{1,0:T(8,128)}, u32[]{:S(2)}) copy-start(f32[64,512]{1,0:T(8,128)} %mult_hbm.1) | copy-start | bytes 393220
  1.0 0.7 %copy-start.1 = (s32[512]{0:T(512)S(1)}, s32[512]{0:T(512)}, u32[]{:S(2)}) copy-start(s32[512]{0:T(512)} %param.4) | copy-start | bytes 6148
  4.2 14.0 %collective-permute-start.1 = (f32[24,512]{1,0:T(8,128)S(1)}, f32[24,512]{1,0:T(8,128)S(1)}, u32[]{:S(2)}, u32[]{:S(2)}) collective-permute-start(f32[24,512]{1,0:T(8,128)S(1)} %get-tuple-element.15), channel_id=1, source_target_pairs={{4,32},{5,33},{6,34},{7,35},{12,40},{13,41},{14,42},{15,43},{20,48... | collective-permute-start | bytes 147464 | tf_op jit(solution)/shard_map/ppermute | solution.py:504
  16.2 3.1 %collective-permute-start = (f32[24,512]{1,0:T(8,128)S(1)}, f32[24,512]{1,0:T(8,128)S(1)}, u32[]{:S(2)}, u32[]{:S(2)}) collective-permute-start(f32[24,512]{1,0:T(8,128)S(1)} %get-tuple-element.14.sent_ref), channel_id=1, source_target_pairs={{0,4},{1,5},{2,6},{3,7},{4,0},{5,1},{6,2},{7,3},{8,12},{9,13},{10,... | collective-permute-start | bytes 147464 | tf_op jit(solution)/shard_map/ppermute | solution.py:503
  20.0 7.3 %collective-permute-start.2 = (f32[40,512]{1,0:T(8,128)S(1)}, f32[40,512]{1,0:T(8,128)S(1)}, u32[]{:S(2)}, u32[]{:S(2)}) collective-permute-start(f32[40,512]{1,0:T(8,128)S(1)} %get-tuple-element.16), channel_id=1, source_target_pairs={{0,2},{1,3},{2,0},{3,1},{4,6},{5,7},{6,4},{7,5},{8,10},{9,11},{10,... | collective-permute-start | bytes 245768 | tf_op jit(solution)/shard_map/ppermute | solution.py:503
  24.6 21.0 %collective-permute-start.3 = (f32[40,512]{1,0:T(8,128)S(1)}, f32[40,512]{1,0:T(8,128)S(1)}, u32[]{:S(2)}, u32[]{:S(2)}) collective-permute-start(f32[40,512]{1,0:T(8,128)S(1)} %get-tuple-element.17), channel_id=1, source_target_pairs={{2,16},{3,17},{6,20},{7,21},{10,24},{11,25},{14,28},{15,29},{16,2}... | collective-permute-start | bytes 245768 | tf_op jit(solution)/shard_map/ppermute | solution.py:504
  28.0 29.8 %all-to-all-start = ((f32[128,1,256]{2,1,0:T(1,128)}), f32[128,1,256]{2,1,0:T(1,128)S(1)}, u32[]{:S(2)}, u32[]{:S(2)}) async-start(f32[128,1,256]{2,1,0:T(1,128)} %broadcast_in_dim.2), calls=%async_computation | async-start | bytes 262144 | tf_op jit(solution)/shard_map/all_to_all | solution.py:560
  46.3 11.6 %collective-permute-start.4 = (f32[64,512]{1,0:T(8,128)S(1)}, f32[64,512]{1,0:T(8,128)S(1)}, u32[]{:S(2)}, u32[]{:S(2)}) collective-permute-start(f32[64,512]{1,0:T(8,128)S(1)} %get-tuple-element.18), channel_id=1, source_target_pairs={{0,1},{1,0},{2,3},{3,2},{4,5},{5,4},{6,7},{7,6},{8,9},{9,8},{10,11... | collective-permute-start | bytes 393224 | tf_op jit(solution)/shard_map/ppermute | solution.py:503
  48.8 9.1 %collective-permute-start.5 = (f32[64,512]{1,0:T(8,128)S(1)}, f32[64,512]{1,0:T(8,128)S(1)}, u32[]{:S(2)}, u32[]{:S(2)}) collective-permute-start(f32[64,512]{1,0:T(8,128)S(1)} %get-tuple-element.19), channel_id=1, source_target_pairs={{1,8},{3,10},{5,12},{7,14},{8,1},{9,64},{10,3},{11,66},{12,5},{13,... | collective-permute-start | bytes 393224 | tf_op jit(solution)/shard_map/ppermute | solution.py:504

commit v3 on v2

--- a/solution.py
+++ b/solution.py
@@ -20,8 +20,8 @@
 ROWS = 80
 SMALL = 16
 PIECES = {
-    "up": 512, "basis": 1024, "small": 432, "fine": 1728, "far": 13824, "back": 1024, "down": 512,
-    "coarse": 64 * 224,
+    "up": 512, "basis": 1024, "small": 432, "fine": 1728, "rim": 288, "spot": 80, "far": 9216,
+    "back": 1024, "down": 512, "coarse": 64 * 224,
 }
 
 
@@ -57,18 +57,17 @@
     return result
 
 
-def parity_basis():
-    basis = np.zeros((512, 512))
+def parity_signs():
+    signs = np.zeros((512, 512))
     for q in range(512):
-        cy, cz = q // 128 % 2, q // 256
-        ox, a, vy, vz = q // 64 % 2, q // 16 % 4, q // 4 % 4, q % 4
-        for oy in range(2):
-            for oz in range(2):
-                b = 3 - vy if oy else vy
-                e = 3 - vz if oz else vz
-                sign = (-1) ** (cy * oy + cz * oz)
-                basis[64 * (ox + 2 * oy + 4 * oz) + 16 * a + 4 * b + e, q] = 0.5 * sign
-    return basis
+        odd = [q // 64 % 2, q // 128 % 2, q // 256]
+        degree = [q // 16 % 4, q // 4 % 4, q % 4]
+        for o in range(8):
+            octant = [o % 2, o // 2 % 2, o // 4]
+            a, b, e = (3 - v if side else v for v, side in zip(degree, octant))
+            sign = (-1) ** sum(c * side for c, side in zip(odd, octant))
+            signs[64 * o + 16 * a + 4 * b + e, q] = sign
+    return signs
 
 
 def morton(x, y, z, bits):
@@ -84,8 +83,9 @@
 
 Z_ROWS, Y_ROWS, X_ROWS = 24, 40, 64
 Z_THREE, Y_THREE = 21, 35
-FINE_PARTS = ((0, 64), (0, 16), (0, 16), (0, 24), (0, 24), (0, 40), (0, 40))
-SMALL_PARTS = ((64, 80), (16, 24), (16, 24), (24, 40), (24, 40), (32, 64), (32, 64))
+FINE_PARTS = ((0, 64), (0, 16), (0, 16), (0, 24), (0, 24))
+SMALL_PARTS = ((64, 80), (16, 24), (16, 24), (24, 40), (24, 40))
+RIM = 32
 
 
 def level_extent(level):
@@ -113,9 +113,7 @@
 
 def source_row(level, x, y, z):
     n = level_extent(level)
-    if not 0 <= x < n:
-        part, row = (6 if x >= n else 5), x_row(level, y, z)
-    elif not 0 <= y < n:
+    if not 0 <= y < n:
         part, row = (4 if y >= n else 3), y_row(level, x, z)
     elif not 0 <= z < n:
         part, row = (2 if z >= n else 1), z_row(level, x, y)
@@ -131,21 +129,32 @@
     return [(0, 1)] if kind == 0 else [(1, 1), (-1, 1 if kind == 1 else -1)]
 
 
+def rim_target(level, y, z):
+    return {6: 0, 5: 16, 4: 20}[level] + z * level_extent(level) + y
+
+
 def selections():
     fine = np.zeros((27, 64, 256))
     small = np.zeros((27, SMALL, 128))
+    rim = np.zeros((9, RIM, 256))
+    spot = np.zeros((ROWS, 256))
     for k, (dx, ky, kz) in enumerate(KINDS):
         for dy, sy in kind_terms(ky):
             for dz, sz in kind_terms(kz):
                 for level in (6, 5, 4):
                     n = level_extent(level)
+                    factor = sy * sz * 2.0 ** (level - 6)
                     into = fine[k] if level == 6 else small[k]
                     for m in range(n**3):
                         x, y, z = place(m, level - 4)
                         row = own_row(level, x, y, z) % 64
-                        into[row, source_row(level, x + dx, y + dy, z + dz)] += (
-                            sy * sz * 2.0 ** (level - 6)
-                        )
+                        if 0 <= x + dx < n:
+                            into[row, source_row(level, x + dx, y + dy, z + dz)] += factor
+                        elif dx == 1:
+                            rim[k - 18, rim_target(level, y, z), x_row(level, y + dy, z + dz)] += factor
+                            spot[own_row(level, x, y, z), rim_target(level, y, z)] = 1
+                        else:
+                            spot[own_row(level, x, y, z), RIM + rim_target(level, y, z)] = 1
     coarse = np.zeros((64, 27, SMALL, 128))
     for parent in range(64):
         for level, row, base in ((3, 9, 0), (2, 10, 64)):
@@ -160,50 +169,47 @@
                             coarse[parent, k, row, base + morton(*u, bits)] += (
                                 sy * sz * 2.0 ** (level - 6)
                             )
-    return (
-        fine.reshape(27 * 64, 256).astype(ml_dtypes.bfloat16),
-        small.reshape(27 * SMALL, 128).astype(ml_dtypes.bfloat16),
-        np.concatenate(
-            np.split(np.pad(coarse.reshape(64, 27 * SMALL, 128), ((0, 0), (0, 16), (0, 0))), 2, axis=1),
-            axis=2,
-        ).reshape(64 * 224, 256),
-    )
+    coarse = np.pad(coarse.reshape(64, 27 * SMALL, 128), ((0, 0), (0, 16), (0, 0)))
+    return {
+        "small": np.pad(small.reshape(27 * SMALL, 128), ((0, 0), (0, 128))),
+        "fine": fine.reshape(27 * 64, 256),
+        "rim": rim.reshape(9 * RIM, 256),
+        "spot": spot,
+        "coarse": np.concatenate(np.split(coarse, 2, axis=1), axis=2).reshape(64 * 224, 256),
+    }
 
 
 @functools.lru_cache(maxsize=1)
 def constants():
-    basis = parity_basis()
+    basis, back = 0.5 * parity_signs(), 0.25 * parity_signs().T
     tables = {
-        (dx, dy, dz): basis.T @ table((dx, dy, dz)) @ basis
-        for dx in (-1, 0, 1)
+        (dx, dy, dz): back @ table((dx, dy, dz)) @ basis
+        for dx in (0, 1)
         for dy in (0, 1)
         for dz in (0, 1)
     }
-    far = np.zeros((4, 27 * 128, 256), ml_dtypes.bfloat16)
+    far = np.zeros((2, 4, 9 * 128, 256), ml_dtypes.bfloat16)
     for t in range(4):
-        for k, (dx, ky, kz) in enumerate(KINDS):
+        for k, (dx, ky, kz) in enumerate(KINDS[9:]):
             c = source_class(t, ky, kz)
             block = tables[dx, min(ky, 1), min(kz, 1)][
                 128 * c : 128 * c + 128, 128 * t : 128 * t + 128
             ]
             high, low = halves(block)
-            far[t, 128 * k : 128 * k + 128, :128] = high
-            far[t, 128 * k : 128 * k + 128, 128:] = low
+            j = 128 * (k % 9)
+            far[dx, t, j : j + 128, :128] = high
+            far[dx, t, j : j + 128, 128:] = low
     up = upward_matrix()
-    fine, small, coarse = selections()
     wide_down = np.concatenate(halves(np.tile(up.T, (2, 1))), axis=1)
-    pieces = {
+    pieces = selections() | {
         "up": np.concatenate(halves(np.tile(up, (1, 2))), axis=1),
         "basis": in_lanes(basis),
-        "small": np.pad(small, ((0, 0), (0, 128))),
-        "fine": fine,
         "far": far.reshape(-1, 256),
-        "back": in_lanes(basis.T),
+        "back": in_lanes(back),
         "down": in_lanes(wide_down),
-        "coarse": coarse,
     }
     assert {name: len(piece) for name, piece in pieces.items()} == PIECES
-    return np.concatenate([piece.astype(ml_dtypes.bfloat16) for piece in pieces.values()])
+    return np.concatenate([pieces[name].astype(ml_dtypes.bfloat16) for name in PIECES])
 
 
 def in_lanes(matrix):
@@ -339,7 +345,7 @@
     high_ref[...] = jnp.where(odd, b, a)
 
 
-def y_kernel(ids_ref, own_ref, sent_ref, za_ref, zb_ref, pa_ref, pb_ref, zl, zh):
+def y_kernel(ids_ref, own_ref, sent_ref, zb_ref, za_ref, pa_ref, pb_ref, zl, zh):
     sort_sides(ids_ref[2] == 1, za_ref, zb_ref, zl, zh)
     odd = ids_ref[1] == 1
     pa_ref[...] = jnp.zeros_like(pa_ref)
@@ -367,7 +373,7 @@
                 pb_ref[pl.ds(i, 1)] = jnp.where(odd, high, low)
 
 
-def x_kernel(ids_ref, own_ref, za_ref, zb_ref, ya_ref, yb_ref, pa_ref, pb_ref, zl, zh, yl, yh):
+def x_kernel(ids_ref, own_ref, zb_ref, za_ref, ya_ref, yb_ref, pa_ref, pb_ref, zl, zh, yl, yh):
     sort_sides(ids_ref[2] == 1, za_ref, zb_ref, zl, zh)
     sort_sides(ids_ref[1] == 1, ya_ref, yb_ref, yl, yh)
     odd = ids_ref[0] == 1
@@ -408,25 +414,52 @@
     return exact_times(gather, jnp.concatenate(blocks, axis=1))
 
 
-def final_kernel(
-    ids_ref, own_ref, za_ref, zb_ref, ya_ref, yb_ref, xa_ref, xb_ref, quads_ref, mask_ref, blob,
-    out_ref, fine_src, small_src, wide, coarse_ref, up_ref, basis_ref, small_ref, fine_ref, far_ref,
-    back_ref, down_ref, sem,
+def place_mix(wide, j, ky, kz, mix, row):
+    rows, half = mix.shape[0], wide.shape[1] // 2
+    high, low = split(mix)
+    for t in range(4):
+        c = source_class(t, ky, kz)
+        wide[t, row : row + rows, 128 * j : 128 * j + 128] = high[:, 128 * c : 128 * c + 128]
+        wide[t, half + row : half + row + rows, 128 * j : 128 * j + 128] = low[:, 128 * c : 128 * c + 128]
+
+
+def far_rows(wide, far_ref, dx):
+    parts = []
+    for t in range(4):
+        rows = 1152 * (4 * dx + t)
+        product = mm(wide[t], far_ref[rows : rows + 1152])
+        half = product.shape[0] // 2
+        top, bottom = product[:half], product[half:]
+        parts.append((top[:, :128] + bottom[:, :128]) + (top[:, 128:] + bottom[:, 128:]))
+    return jnp.concatenate(parts, axis=1)
+
+
+def reflected(rows):
+    return jnp.where(iota(rows.shape, 1) // 64 % 2 == 1, -rows, rows)
+
+
+def whole_down(down_ref):
+    return jnp.concatenate([down_ref[128 * i : 128 * i + 128] for i in range(4)], axis=1)
+
+
+def only(row, octant):
+    kept = iota((8, 512), 1) // 64 == octant
+    return jnp.where(kept, jnp.broadcast_to(row, (8, 512)), 0.0)
+
+
+def inner_kernel(
+    ids_ref, own_ref, zb_ref, za_ref, ya_ref, yb_ref, blob, out_ref,
+    fine_src, small_src, wide_zero, wide_one, small_ref, fine_ref, far_ref, sem,
 ):
     small_copy = piece_copy(blob, "small", small_ref, sem.at[0])
     fine_copy = piece_copy(blob, "fine", fine_ref, sem.at[1])
-    up_copy = piece_copy(blob, "up", up_ref, sem.at[2])
-    basis_copy = piece_copy(blob, "basis", basis_ref, sem.at[3])
-    coarse_copy = piece_copy(blob, "coarse", coarse_ref, sem.at[4], ids_ref[3], 64)
-    far_copies = [piece_copy(blob, "far", far_ref, sem.at[5 + t], t, 4) for t in range(4)]
-    back_copy = piece_copy(blob, "back", back_ref, sem.at[9])
-    down_copy = piece_copy(blob, "down", down_ref, sem.at[10])
-    first = (small_copy, up_copy, basis_copy, coarse_copy, fine_copy)
-    for copy in (*first, *far_copies, back_copy, down_copy):
+    tables = [piece_copy(blob, "far", far_ref, sem.at[2 + dx], dx, 2) for dx in range(2)]
+    for copy in (small_copy, fine_copy, *tables):
         copy.start()
-    fine_src[224:] = jnp.zeros((32, 512), F32)
+    fine_src[144:] = jnp.zeros((112, 512), F32)
+    small_src[64:] = jnp.zeros((64, 512), F32)
     stack = [own_ref[...]]
-    for axis, ra_ref, rb_ref in ((2, za_ref, zb_ref), (1, ya_ref, yb_ref), (0, xa_ref, xb_ref)):
+    for axis, ra_ref, rb_ref in ((2, za_ref, zb_ref), (1, ya_ref, yb_ref)):
         odd = ids_ref[axis] == 1
         a, b = ra_ref[...], rb_ref[...]
         stack += [jnp.where(odd, a, b), jnp.where(odd, b, a)]
@@ -435,55 +468,92 @@
         for values, (start, stop) in zip(stack, parts):
             target[base : base + stop - start] = values[start:stop]
             base += stop - start
-
     small_copy.wait()
     small = exact_times(small_ref[:, :128], small_src[...])
-    three = coarse_rows(quads_ref[...])
-    up_copy.wait()
-    two = up_group(three, up_ref[...])
-    upper = jnp.concatenate([three, two, jnp.zeros((56, 512), F32)], axis=0)
-    basis_copy.wait()
-    upper = times_exact(upper, in_columns(basis_ref))
-    coarse_copy.wait()
-    chosen = jnp.concatenate([coarse_ref[:, :128], coarse_ref[:208, 128:]], axis=0)
-    small = small + exact_times(chosen, upper)
-
     fine_split = jnp.concatenate(split(fine_src[...]), axis=1)
     fine_copy.wait()
-    for group in range(3):
+    far = 0.0
+    for group in (1, 0, 2):
         mixes = mm(fine_ref[576 * group : 576 * group + 576], fine_split)
         mixes = mixes[:, :512] + mixes[:, 512:]
         for j in range(9):
             k = 9 * group + j
             _, ky, kz = KINDS[k]
-            mix = jnp.concatenate(
-                [mixes[64 * j : 64 * j + 64], small[SMALL * k : SMALL * k + SMALL]], axis=0
-            )
-            high, low = split(mix)
-            for t in range(4):
-                c = source_class(t, ky, kz)
-                wide[t, :ROWS, 128 * k : 128 * k + 128] = high[:, 128 * c : 128 * c + 128]
-                wide[t, ROWS:, 128 * k : 128 * k + 128] = low[:, 128 * c : 128 * c + 128]
-    parts = []
-    for t in range(4):
-        far_copies[t].wait()
-        product = mm(wide[t], far_ref[3456 * t : 3456 * t + 3456])
-        parts.append(
-            product[:ROWS, :128] + product[ROWS:, :128] + product[:ROWS, 128:] + product[ROWS:, 128:]
-        )
-    back_copy.wait()
-    far = times_exact(jnp.concatenate(parts, axis=1), in_columns(back_ref))
-    down_copy.wait()
-
-    lane = iota((8, 512), 1) // 64
-    down = jnp.concatenate([down_ref[128 * i : 128 * i + 128] for i in range(4)], axis=1)
-
-    def only(row, octant):
-        return jnp.where(lane == octant, jnp.broadcast_to(row, (8, 512)), 0.0)
-
+            mix = [mixes[64 * j : 64 * j + 64], small[SMALL * k : SMALL * k + SMALL]]
+            mix = jnp.concatenate(mix, axis=0)
+            if group == 1:
+                place_mix(wide_zero, j, ky, kz, mix, 0)
+            else:
+                mix = reflected(mix) if group == 0 else mix
+                place_mix(wide_one, j, ky, kz, mix, ROWS if group == 0 else 0)
+        if group == 1:
+            tables[0].wait()
+            far = far_rows(wide_zero, far_ref, 0)
+    tables[1].wait()
+    both = far_rows(wide_one, far_ref, 1)
+    out_ref[...] = far + both[:ROWS] + reflected(both[ROWS:])
+
+
+def outer_kernel(
+    ids_ref, far_in_ref, xb_ref, xa_ref, quads_ref, mask_ref, blob, out_ref,
+    wide_zero, wide_one, coarse_ref, up_ref, basis_ref, rim_ref, far_ref, spot_ref, back_ref, down_ref, sem,
+):
+    first = [
+        piece_copy(blob, "up", up_ref, sem.at[0]),
+        piece_copy(blob, "basis", basis_ref, sem.at[1]),
+        piece_copy(blob, "coarse", coarse_ref, sem.at[2], ids_ref[3], 64),
+        piece_copy(blob, "rim", rim_ref, sem.at[3]),
+    ]
+    tables = [piece_copy(blob, "far", far_ref, sem.at[4 + dx], dx, 2) for dx in range(2)]
+    last = [
+        piece_copy(blob, "spot", spot_ref, sem.at[6]),
+        piece_copy(blob, "back", back_ref, sem.at[7]),
+        piece_copy(blob, "down", down_ref, sem.at[8]),
+    ]
+    for copy in (*first, *tables, *last):
+        copy.start()
+    three = coarse_rows(quads_ref[...])
+    odd = ids_ref[0] == 1
+    a, b = xa_ref[...], xb_ref[...]
+    low, high = jnp.where(odd, a, b), jnp.where(odd, b, a)
+    sides = jnp.concatenate([*split(high), *split(reflected(low))], axis=1)
+    for copy in first:
+        copy.wait()
+    two = up_group(three, up_ref[...])
+    mixes = mm(rim_ref[:, :X_ROWS], sides)
+    upper = jnp.concatenate([three, two, jnp.zeros((56, 512), F32)], axis=0)
+    upper = times_exact(upper, in_columns(basis_ref))
+    chosen = jnp.concatenate([coarse_ref[:, :128], coarse_ref[:208, 128:]], axis=0)
+    coarse = exact_times(chosen, upper)
+    for side in range(2):
+        mix = mixes[:, 1024 * side : 1024 * side + 512] + mixes[:, 1024 * side + 512 : 1024 * side + 1024]
+        for j in range(9):
+            _, ky, kz = KINDS[j]
+            place_mix(wide_one, j, ky, kz, mix[RIM * j : RIM * j + RIM], RIM * side)
+    for k, (dx, ky, kz) in enumerate(KINDS):
+        mix = coarse[SMALL * k : SMALL * k + SMALL]
+        if dx == 0:
+            place_mix(wide_zero, k % 9, ky, kz, mix, 0)
+        elif dx == 1:
+            place_mix(wide_one, k % 9, ky, kz, mix, 2 * RIM)
+        else:
+            place_mix(wide_one, k % 9, ky, kz, reflected(mix), 2 * RIM + SMALL)
+    tables[0].wait()
+    zero = far_rows(wide_zero, far_ref, 0)
+    tables[1].wait()
+    one = far_rows(wide_one, far_ref, 1)
+    rims = jnp.concatenate([one[:RIM], reflected(one[RIM : 2 * RIM])], axis=0)
+    small = zero + one[2 * RIM : 2 * RIM + SMALL] + reflected(one[2 * RIM + SMALL :])
+    for copy in last:
+        copy.wait()
+    far = far_in_ref[...] + exact_times(spot_ref[:, : 2 * RIM], rims)
+    far = jnp.concatenate([far[:64], far[64:] + small], axis=0)
+    far = times_exact(far, in_columns(back_ref))
+    down = whole_down(down_ref)
     local = far[73:74] + downward(only(far[74:75], ids_ref[4]), down)
     local = far[72:73] + downward(only(local[:1], ids_ref[5]), down)
-    local = far[64:72] + downward(jnp.broadcast_to(local[:1], (8, 512)) * octant_mask(8), down)
+    local = jnp.broadcast_to(local[:1], (8, 512)) * octant_mask(8)
+    local = far[64:72] + downward(local, down)
     local = jnp.broadcast_to(local[:, None, :], (8, 8, 512)).reshape(64, 512) * octant_mask(64)
     out_ref[...] = (far[:64] + downward(local, down)) * mask_ref[...]
 
@@ -534,6 +604,10 @@
 
 def table_scratch(*names):
     return [pltpu.VMEM((PIECES[name], 256), BF16) for name in names]
+
+
+def wide_scratch(*shape):
+    return [pltpu.VMEM(shape, BF16)]
 
 
 def local(multipoles, occupancy):
@@ -552,7 +626,7 @@
     )
     za, zb = exchange(pa, pb, 2)
     pa, pb = call(
-        y_kernel, rows_of(Y_ROWS, Y_ROWS), scratch_rows(Z_ROWS, Z_ROWS), ids, [own, pa, za, zb]
+        y_kernel, rows_of(Y_ROWS, Y_ROWS), scratch_rows(Z_ROWS, Z_ROWS), ids, [own, pa, zb, za]
     )
     ya, yb = exchange(pa, pb, 1)
     ours, theirs = (p[Y_THREE : Y_THREE + 1, :256] for p in (pa, ya))
@@ -562,17 +636,28 @@
     )
     pa, pb = call(
         x_kernel, rows_of(X_ROWS, X_ROWS), scratch_rows(Z_ROWS, Z_ROWS, Y_ROWS, Y_ROWS),
-        ids, [own, za, zb, ya, yb], micros=40,
+        ids, [own, zb, za, ya, yb], micros=40,
     )
     xa, xb = exchange(pa, pb, 0)
+    (far,) = call(
+        inner_kernel,
+        rows_of(ROWS),
+        scratch_rows(256, 128)
+        + wide_scratch(4, 2 * ROWS, 9 * 128)
+        + wide_scratch(4, 4 * ROWS, 9 * 128)
+        + table_scratch("small", "fine", "far")
+        + [pltpu.SemaphoreType.DMA((4,))],
+        ids, [own, zb, za, ya, yb], [blob], micros=1,
+    )
     (out,) = call(
-        final_kernel,
+        outer_kernel,
         rows_of(64),
-        scratch_rows(256, 128)
-        + [pltpu.VMEM((4, 2 * ROWS, 27 * 128), BF16), pltpu.VMEM((224, 256), BF16)]
-        + table_scratch(*list(PIECES)[:-1])
-        + [pltpu.SemaphoreType.DMA((11,))],
-        ids, [own, za, zb, ya, yb, xa, xb, quads, mask], [blob], micros=8,
+        wide_scratch(4, 2 * SMALL, 9 * 128)
+        + wide_scratch(4, 4 * RIM + 4 * SMALL, 9 * 128)
+        + wide_scratch(224, 256)
+        + table_scratch("up", "basis", "rim", "far", "spot", "back", "down")
+        + [pltpu.SemaphoreType.DMA((9,))],
+        ids, [far, xb, xa, quads, mask], [blob], micros=4,
     )
     return out
 

time: 66.9 us -> 64 us (0.957)
  waiting for transfers between devices: 11.6 us -> 4.15 us
  starting transfers between devices: 40 us -> 42.5 us
  Pallas kernels: 12.4 us -> 14.5 us
    all_to_all x1, waiting for transfers between devices: 8.4 us -> 1 us  [local(): lax.all_to_all(jnp.broadcast_to(quad, (128, 256)), ('upper', 'bit0'), 0,...]
    ppermute x3, starting transfers between devices: 9.05 us -> 11.5 us  [exchange(): lax.ppermute(pa, AXES, pairs(axis, False))]
    pallas_call x4 -> x5, Pallas kernels: 12.4 us -> 14.5 us  [call(): pl.pallas_call(kernel, out_shape=[jax.ShapeDtypeStruct(shape, F32) for sh...]
  transfers between devices with their start and end apart: 7 -> 7, of which waited for: 3 -> 3; matrix products, arithmetic and copies ran while one was open for 1% -> 1% of each run, Pallas kernels for 1% -> 9%
where the time goes in v3:
time: 64 us; the launch traced here: 63.7 us
  starting transfers between devices  42.5 us (66%)
  Pallas kernels  14.5 us (23%)
  waiting for transfers between devices  4.15 us (6%)
  local copies, waits for them, and re-layouts  2.41 us (4%)
    all_to_all x1, starting transfers between devices, local(): lax.all_to_all(jnp.broadcast_to(quad, (128, 256)), ('upper', 'bit0'), 0,...  17.6 us
    pallas_call x5, Pallas kernels, call(): pl.pallas_call(kernel, out_shape=[jax.ShapeDtypeStruct(shape, F32) for sh...  14.5 us
    ppermute x3, starting transfers between devices, exchange(): lax.ppermute(pb, AXES, pairs(axis, True))  13.4 us
    ppermute x3, starting transfers between devices, exchange(): lax.ppermute(pa, AXES, pairs(axis, False))  11.5 us
    ppermute x3, waiting for transfers between devices, exchange(): lax.ppermute(pa, AXES, pairs(axis, False))  3.15 us
    unnamed x5, local copies, waits for them, and re-layouts  1.6 us
  transfers between devices with their start and end apart: 7, of which 3 were waited for; matrix products, arithmetic and copies ran while one was open for 1% of the time, Pallas kernels for 9%

profile of v3, /device:TPU:1, one launch (start us, length us, event | category | flops | bytes accessed | tf_op | source)
XLA Modules:
  0.0 63.7 jit_solution(10124659657707538763)
XLA Ops:
  0.0 0.1 stack.27.ids_ref
  0.1 0.0 copy-start
  0.1 0.9 %copy-done = f32[64,512]{1,0:T(8,128)S(1)} copy-done((f32[64,512]{1,0:T(8,128)S(1)}, f32[64,512]{1,0:T(8,128)}, u32[]{:S(2)}) %copy-start) | copy-done | bytes 131096
  1.0 0.0 copy-start.1
  1.0 0.7 %copy-done.1 = s32[512]{0:T(512)S(1)} copy-done((s32[512]{0:T(512)S(1)}, s32[512]{0:T(512)}, u32[]{:S(2)}) %copy-start.1) | copy-done | bytes 2072
  1.7 2.5 %shard_map.37 = (f32[80,512]{1,0:T(8,128)S(1)}, f32[24,512]{1,0:T(8,128)S(1)}, f32[24,512]{1,0:T(8,128)S(1)}, f32[64,512]{1,0:T(8,128)S(1)}) custom-call(s32[6]{0:T(128)S(1)} %stack.27.ids_ref, f32[64,512]{1,0:T(8,128)S(1)} %copy-done, s32[1,512]{1,0:T(1,128)S(1)} %bitcast.12, bf16[29152,256]{1,0:T(8,128)(2,1)} %constant.106.clone.blob), custom_call_target="tpu_custom_call" | custom-call | flops 4000000000 | tf_op jit(solution)/shard_map/pallas_call | solution.py:586
  4.2 12.0 %collective-permute-start = (f32[24,512]{1,0:T(8,128)S(1)}, f32[24,512]{1,0:T(8,128)S(1)}, u32[]{:S(2)}, u32[]{:S(2)}) collective-permute-start(f32[24,512]{1,0:T(8,128)S(1)} %get-tuple-element.14), channel_id=1, source_target_pairs={{4,32},{5,33},{6,34},{7,35},{12,40},{13,41},{14,42},{15,43},{20,48... | collective-permute-start | bytes 147464 | tf_op jit(solution)/shard_map/ppermute | solution.py:574
  16.2 1.9 %collective-permute-start.1 = (f32[24,512]{1,0:T(8,128)S(1)}, f32[24,512]{1,0:T(8,128)S(1)}, u32[]{:S(2)}, u32[]{:S(2)}) collective-permute-start(f32[24,512]{1,0:T(8,128)S(1)} %get-tuple-element.15.sent_ref), channel_id=1, source_target_pairs={{0,4},{1,5},{2,6},{3,7},{4,0},{5,1},{6,2},{7,3},{8,12},{9,13},{10,... | collective-permute-start | bytes 147464 | tf_op jit(solution)/shard_map/ppermute | solution.py:573
  18.2 0.0 collective-permute-done.zb_ref
  18.2 1.2 %collective-permute-done.1.za_ref = f32[24,512]{1,0:T(8,128)S(1)} collective-permute-done((f32[24,512]{1,0:T(8,128)S(1)}, f32[24,512]{1,0:T(8,128)S(1)}, u32[]{:S(2)}, u32[]{:S(2)}) %collective-permute-start.1) | collective-permute-done | bytes 49184 | tf_op jit(solution)/shard_map/ppermute | solution.py:573
  19.4 0.6 shard_map.38
  19.9 4.7 %collective-permute-start.2 = (f32[40,512]{1,0:T(8,128)S(1)}, f32[40,512]{1,0:T(8,128)S(1)}, u32[]{:S(2)}, u32[]{:S(2)}) collective-permute-start(f32[40,512]{1,0:T(8,128)S(1)} %get-tuple-element.16), channel_id=1, source_target_pairs={{0,2},{1,3},{2,0},{3,1},{4,6},{5,7},{6,4},{7,5},{8,10},{9,11},{10,... | collective-permute-start | bytes 245768 | tf_op jit(solution)/shard_map/ppermute | solution.py:573
  24.6 0.7 %collective-permute-start.3 = (f32[40,512]{1,0:T(8,128)S(1)}, f32[40,512]{1,0:T(8,128)S(1)}, u32[]{:S(2)}, u32[]{:S(2)}) collective-permute-start(f32[40,512]{1,0:T(8,128)S(1)} %get-tuple-element.17), channel_id=1, source_target_pairs={{2,16},{3,17},{6,20},{7,21},{10,24},{11,25},{14,28},{15,29},{16,2}... | collective-permute-start | bytes 245768 | tf_op jit(solution)/shard_map/ppermute | solution.py:574
  25.3 2.0 %collective-permute-done.2.ya_ref = f32[40,512]{1,0:T(8,128)S(1)} collective-permute-done((f32[40,512]{1,0:T(8,128)S(1)}, f32[40,512]{1,0:T(8,128)S(1)}, u32[]{:S(2)}, u32[]{:S(2)}) %collective-permute-start.2) | collective-permute-done | bytes 81952 | tf_op jit(solution)/shard_map/ppermute | solution.py:573
  27.3 0.7 %broadcast_in_dim.2 = f32[128,1,256]{2,1,0:T(1,128)} broadcast(f32[256]{0:T(256)S(1)} %bitcast.13), dimensions={2} | broadcast | bytes 132096 | tf_op jit(solution)/shard_map/broadcast_in_dim | solution.py:635
  28.0 17.6 %all-to-all-start = ((f32[128,1,256]{2,1,0:T(1,128)}), f32[128,1,256]{2,1,0:T(1,128)S(1)}, u32[]{:S(2)}, u32[]{:S(2)}) async-start(f32[128,1,256]{2,1,0:T(1,128)} %broadcast_in_dim.2), calls=%async_computation | async-start | bytes 262144 | tf_op jit(solution)/shard_map/all_to_all | solution.py:634
  45.6 0.0 collective-permute-done.3.yb_ref
  45.6 0.6 shard_map.40
  46.3 0.7 %collective-permute-start.4 = (f32[64,512]{1,0:T(8,128)S(1)}, f32[64,512]{1,0:T(8,128)S(1)}, u32[]{:S(2)}, u32[]{:S(2)}) collective-permute-start(f32[64,512]{1,0:T(8,128)S(1)} %get-tuple-element.18), channel_id=1, source_target_pairs={{1,8},{3,10},{5,12},{7,14},{8,1},{9,64},{10,3},{11,66},{12,5},{13,... | collective-permute-start | bytes 393224 | tf_op jit(solution)/shard_map/ppermute | solution.py:574
  46.9 4.9 %collective-permute-start.5 = (f32[64,512]{1,0:T(8,128)S(1)}, f32[64,512]{1,0:T(8,128)S(1)}, u32[]{:S(2)}, u32[]{:S(2)}) collective-permute-start(f32[64,512]{1,0:T(8,128)S(1)} %get-tuple-element.19), channel_id=1, source_target_pairs={{0,1},{1,0},{2,3},{3,2},{4,5},{5,4},{6,7},{7,6},{8,9},{9,8},{10,11... | collective-permute-start | bytes 393224 | tf_op jit(solution)/shard_map/ppermute | solution.py:573
  51.9 5.0 %shard_map.39.far_in_ref = f32[80,512]{1,0:T(8,128)S(1)} custom-call(s32[6]{0:T(128)S(1)} %stack.27.ids_ref, f32[80,512]{1,0:T(8,128)S(1)} %get-tuple-element.13.own_ref, f32[24,512]{1,0:T(8,128)S(1)} %collective-permute-done.zb_ref, f32[24,512]{1,0:T(8,128)S(1)} %collective-permute-done.1.za_ref, f32[40,512]{1,0:T(8,128)S(1)} %collective-permute-done.2.ya_ref, ...), custom_call_target="tpu_custom_call" | custom-call | flops 1000000000 | tf_op jit(solution)/shard_map/pallas_call | solution.py:586
  56.8 1.0 %all-to-all-done = f32[128,1,256]{2,1,0:T(1,128)S(1)} async-done(((f32[128,1,256]{2,1,0:T(1,128)}), f32[128,1,256]{2,1,0:T(1,128)S(1)}, u32[]{:S(2)}, u32[]{:S(2)}) %all-to-all-start) | async-done | bytes 131104 | tf_op jit(solution)/shard_map/all_to_all | solution.py:634
  57.8 0.0 collective-permute-done.4.xb_ref
  57.9 0.0 collective-permute-done.5.xa_ref
  57.9 5.8 %shard_map.41 = f32[64,512]{1,0:T(8,128)} custom-call(s32[6]{0:T(128)S(1)} %stack.27.ids_ref, f32[80,512]{1,0:T(8,128)S(1)} %shard_map.39.far_in_ref, f32[64,512]{1,0:T(8,128)S(1)} %collective-permute-done.4.xb_ref, f32[64,512]{1,0:T(8,128)S(1)} %collective-permute-done.5.xa_ref, f32[128,256]{1,0:T(8,128)S(1)} %bitcast.11, ...), custom_call_target="tpu_custom_call" | custom-call | flops 4000000000 | tf_op jit(solution)/shard_map/pallas_call | solution.py:586
  (2 shorter events, 0.0 us)
Async XLA Ops:
  0.1 0.9 %copy-start = (f32[64,512]{1,0:T(8,128)S(1)}, f32[64,512]{1,0:T(8,128)}, u32[]{:S(2)}) copy-start(f32[64,512]{1,0:T(8,128)} %mult_hbm.1) | copy-start | bytes 393220
  1.0 0.7 %copy-start.1 = (s32[512]{0:T(512)S(1)}, s32[512]{0:T(512)}, u32[]{:S(2)}) copy-start(s32[512]{0:T(512)} %param.4) | copy-start | bytes 6148
  4.2 14.0 %collective-permute-start = (f32[24,512]{1,0:T(8,128)S(1)}, f32[24,512]{1,0:T(8,128)S(1)}, u32[]{:S(2)}, u32[]{:S(2)}) collective-permute-start(f32[24,512]{1,0:T(8,128)S(1)} %get-tuple-element.14), channel_id=1, source_target_pairs={{4,32},{5,33},{6,34},{7,35},{12,40},{13,41},{14,42},{15,43},{20,48... | collective-permute-start | bytes 147464 | tf_op jit(solution)/shard_map/ppermute | solution.py:574
  16.2 3.1 %collective-permute-start.1 = (f32[24,512]{1,0:T(8,128)S(1)}, f32[24,512]{1,0:T(8,128)S(1)}, u32[]{:S(2)}, u32[]{:S(2)}) collective-permute-start(f32[24,512]{1,0:T(8,128)S(1)} %get-tuple-element.15.sent_ref), channel_id=1, source_target_pairs={{0,4},{1,5},{2,6},{3,7},{4,0},{5,1},{6,2},{7,3},{8,12},{9,13},{10,... | collective-permute-start | bytes 147464 | tf_op jit(solution)/shard_map/ppermute | solution.py:573
  19.9 7.3 %collective-permute-start.2 = (f32[40,512]{1,0:T(8,128)S(1)}, f32[40,512]{1,0:T(8,128)S(1)}, u32[]{:S(2)}, u32[]{:S(2)}) collective-permute-start(f32[40,512]{1,0:T(8,128)S(1)} %get-tuple-element.16), channel_id=1, source_target_pairs={{0,2},{1,3},{2,0},{3,1},{4,6},{5,7},{6,4},{7,5},{8,10},{9,11},{10,... | collective-permute-start | bytes 245768 | tf_op jit(solution)/shard_map/ppermute | solution.py:573
  24.6 21.0 %collective-permute-start.3 = (f32[40,512]{1,0:T(8,128)S(1)}, f32[40,512]{1,0:T(8,128)S(1)}, u32[]{:S(2)}, u32[]{:S(2)}) collective-permute-start(f32[40,512]{1,0:T(8,128)S(1)} %get-tuple-element.17), channel_id=1, source_target_pairs={{2,16},{3,17},{6,20},{7,21},{10,24},{11,25},{14,28},{15,29},{16,2}... | collective-permute-start | bytes 245768 | tf_op jit(solution)/shard_map/ppermute | solution.py:574
  28.0 29.8 %all-to-all-start = ((f32[128,1,256]{2,1,0:T(1,128)}), f32[128,1,256]{2,1,0:T(1,128)S(1)}, u32[]{:S(2)}, u32[]{:S(2)}) async-start(f32[128,1,256]{2,1,0:T(1,128)} %broadcast_in_dim.2), calls=%async_computation | async-start | bytes 262144 | tf_op jit(solution)/shard_map/all_to_all | solution.py:634
  46.3 11.6 %collective-permute-start.4 = (f32[64,512]{1,0:T(8,128)S(1)}, f32[64,512]{1,0:T(8,128)S(1)}, u32[]{:S(2)}, u32[]{:S(2)}) collective-permute-start(f32[64,512]{1,0:T(8,128)S(1)} %get-tuple-element.18), channel_id=1, source_target_pairs={{1,8},{3,10},{5,12},{7,14},{8,1},{9,64},{10,3},{11,66},{12,5},{13,... | collective-permute-start | bytes 393224 | tf_op jit(solution)/shard_map/ppermute | solution.py:574
  46.9 10.9 %collective-permute-start.5 = (f32[64,512]{1,0:T(8,128)S(1)}, f32[64,512]{1,0:T(8,128)S(1)}, u32[]{:S(2)}, u32[]{:S(2)}) collective-permute-start(f32[64,512]{1,0:T(8,128)S(1)} %get-tuple-element.19), channel_id=1, source_target_pairs={{0,1},{1,0},{2,3},{3,2},{4,5},{5,4},{6,7},{7,6},{8,9},{9,8},{10,11... | collective-permute-start | bytes 393224 | tf_op jit(solution)/shard_map/ppermute | solution.py:573

commit v4 on v3

--- a/solution.py
+++ b/solution.py
@@ -23,6 +23,7 @@
     "up": 512, "basis": 1024, "small": 432, "fine": 1728, "rim": 288, "spot": 80, "far": 9216,
     "back": 1024, "down": 512, "coarse": 64 * 224,
 }
+TABLES = ("up", "basis", "coarse", "rim")
 
 
 def halves(values):
@@ -301,26 +302,19 @@
 
 
 def upward_kernel(
-    ids_ref, mult_hbm, occ_hbm, blob, own_ref, pa_ref, pb_ref, mask_ref,
-    mult_ref, occ_ref, up_ref, basis_ref, sem,
+    ids_ref, mult_ref, occ_ref, blob, own_ref, pa_ref, pb_ref, mask_ref, up_ref, basis_ref, sem
 ):
-    copies = [
-        pltpu.make_async_copy(occ_hbm, occ_ref, sem.at[0]),
-        pltpu.make_async_copy(mult_hbm, mult_ref, sem.at[1]),
-        piece_copy(blob, "up", up_ref, sem.at[2]),
-        piece_copy(blob, "basis", basis_ref, sem.at[3]),
-    ]
-    for copy in copies:
-        copy.start()
-    copies[0].wait()
+    up_copy = piece_copy(blob, "up", up_ref, sem.at[0])
+    basis_copy = piece_copy(blob, "basis", basis_ref, sem.at[1])
+    up_copy.start()
+    basis_copy.start()
     mask_ref[...] = occupancy_mask(occ_ref[...])
-    copies[1].wait()
-    copies[2].wait()
+    up_copy.wait()
     grouped_six = mult_ref[...] * mask_ref[...]
     grouped_five = up_group(grouped_six, up_ref[...])
     grouped_four = up_group(grouped_five, up_ref[...])
     three = upward(jnp.broadcast_to(grouped_four, (8, 512)), up_ref[...])
-    copies[3].wait()
+    basis_copy.wait()
     basis = in_columns(basis_ref)
     own_ref[0:64] = times_exact(grouped_six, basis)
     rest = jnp.concatenate([grouped_five, jnp.broadcast_to(grouped_four, (8, 512))], axis=0)
@@ -448,13 +442,19 @@
 
 
 def inner_kernel(
-    ids_ref, own_ref, zb_ref, za_ref, ya_ref, yb_ref, blob, out_ref,
+    ids_ref, own_ref, zb_ref, za_ref, ya_ref, yb_ref, blob, out_ref, up_ref, basis_ref, coarse_ref, rim_ref,
     fine_src, small_src, wide_zero, wide_one, small_ref, fine_ref, far_ref, sem,
 ):
+    later = [
+        piece_copy(blob, "up", up_ref, sem.at[4]),
+        piece_copy(blob, "basis", basis_ref, sem.at[5]),
+        piece_copy(blob, "coarse", coarse_ref, sem.at[6], ids_ref[3], 64),
+        piece_copy(blob, "rim", rim_ref, sem.at[7]),
+    ]
     small_copy = piece_copy(blob, "small", small_ref, sem.at[0])
     fine_copy = piece_copy(blob, "fine", fine_ref, sem.at[1])
     tables = [piece_copy(blob, "far", far_ref, sem.at[2 + dx], dx, 2) for dx in range(2)]
-    for copy in (small_copy, fine_copy, *tables):
+    for copy in (small_copy, fine_copy, *tables, *later):
         copy.start()
     fine_src[144:] = jnp.zeros((112, 512), F32)
     small_src[64:] = jnp.zeros((64, 512), F32)
@@ -492,33 +492,27 @@
     tables[1].wait()
     both = far_rows(wide_one, far_ref, 1)
     out_ref[...] = far + both[:ROWS] + reflected(both[ROWS:])
+    for copy in later:
+        copy.wait()
 
 
 def outer_kernel(
-    ids_ref, far_in_ref, xb_ref, xa_ref, quads_ref, mask_ref, blob, out_ref,
-    wide_zero, wide_one, coarse_ref, up_ref, basis_ref, rim_ref, far_ref, spot_ref, back_ref, down_ref, sem,
+    ids_ref, far_in_ref, xa_ref, xb_ref, quads_ref, mask_ref, up_ref, basis_ref, coarse_ref, rim_ref, blob, out_ref,
+    wide_zero, wide_one, far_ref, spot_ref, back_ref, down_ref, sem,
 ):
-    first = [
-        piece_copy(blob, "up", up_ref, sem.at[0]),
-        piece_copy(blob, "basis", basis_ref, sem.at[1]),
-        piece_copy(blob, "coarse", coarse_ref, sem.at[2], ids_ref[3], 64),
-        piece_copy(blob, "rim", rim_ref, sem.at[3]),
+    tables = [piece_copy(blob, "far", far_ref, sem.at[dx], dx, 2) for dx in range(2)]
+    last = [
+        piece_copy(blob, "spot", spot_ref, sem.at[2]),
+        piece_copy(blob, "back", back_ref, sem.at[3]),
+        piece_copy(blob, "down", down_ref, sem.at[4]),
     ]
-    tables = [piece_copy(blob, "far", far_ref, sem.at[4 + dx], dx, 2) for dx in range(2)]
-    last = [
-        piece_copy(blob, "spot", spot_ref, sem.at[6]),
-        piece_copy(blob, "back", back_ref, sem.at[7]),
-        piece_copy(blob, "down", down_ref, sem.at[8]),
-    ]
-    for copy in (*first, *tables, *last):
+    for copy in (*tables, *last):
         copy.start()
     three = coarse_rows(quads_ref[...])
     odd = ids_ref[0] == 1
     a, b = xa_ref[...], xb_ref[...]
     low, high = jnp.where(odd, a, b), jnp.where(odd, b, a)
     sides = jnp.concatenate([*split(high), *split(reflected(low))], axis=1)
-    for copy in first:
-        copy.wait()
     two = up_group(three, up_ref[...])
     mixes = mm(rim_ref[:, :X_ROWS], sides)
     upper = jnp.concatenate([three, two, jnp.zeros((56, 512), F32)], axis=0)
@@ -585,7 +579,7 @@
 def call(kernel, shapes, scratch, ids, vmem_args, hbm_args=(), micros=1):
     return pl.pallas_call(
         kernel,
-        out_shape=[jax.ShapeDtypeStruct(shape, F32) for shape in shapes],
+        out_shape=[jax.ShapeDtypeStruct(shape[:2], (*shape, F32)[2]) for shape in shapes],
         in_specs=[SMEM] + [VMEM] * len(vmem_args) + [HBM] * len(hbm_args),
         out_specs=[VMEM] * len(shapes),
         scratch_shapes=scratch,
@@ -618,11 +612,8 @@
     own, pa, pb, mask = call(
         upward_kernel,
         rows_of(ROWS, Z_ROWS, Z_ROWS, 64),
-        scratch_rows(64)
-        + [pltpu.VMEM((1, 512), jnp.int32)]
-        + table_scratch("up", "basis")
-        + [pltpu.SemaphoreType.DMA((4,))],
-        ids, [], [multipoles, occupancy.reshape(1, 512), blob], micros=4,
+        table_scratch("up", "basis") + [pltpu.SemaphoreType.DMA((2,))],
+        ids, [multipoles, occupancy.reshape(1, 512)], [blob], micros=4,
     )
     za, zb = exchange(pa, pb, 2)
     pa, pb = call(
@@ -639,14 +630,14 @@
         ids, [own, zb, za, ya, yb], micros=40,
     )
     xa, xb = exchange(pa, pb, 0)
-    (far,) = call(
+    far, *tables = call(
         inner_kernel,
-        rows_of(ROWS),
+        rows_of(ROWS) + [(PIECES[n] // (64 if n == "coarse" else 1), 256, BF16) for n in TABLES],
         scratch_rows(256, 128)
         + wide_scratch(4, 2 * ROWS, 9 * 128)
         + wide_scratch(4, 4 * ROWS, 9 * 128)
         + table_scratch("small", "fine", "far")
-        + [pltpu.SemaphoreType.DMA((4,))],
+        + [pltpu.SemaphoreType.DMA((8,))],
         ids, [own, zb, za, ya, yb], [blob], micros=1,
     )
     (out,) = call(
@@ -654,10 +645,9 @@
         rows_of(64),
         wide_scratch(4, 2 * SMALL, 9 * 128)
         + wide_scratch(4, 4 * RIM + 4 * SMALL, 9 * 128)
-        + wide_scratch(224, 256)
-        + table_scratch("up", "basis", "rim", "far", "spot", "back", "down")
-        + [pltpu.SemaphoreType.DMA((9,))],
-        ids, [far, xb, xa, quads, mask], [blob], micros=4,
+        + table_scratch("far", "spot", "back", "down")
+        + [pltpu.SemaphoreType.DMA((5,))],
+        ids, [far, xa, xb, quads, mask, *tables], [blob], micros=4,
     )
     return out
 

time: 64 us -> 63.6 us (level)
  starting transfers between devices: 42.5 us -> 40 us
  waiting for transfers between devices: 4.15 us -> 6.53 us
    ppermute x3, starting transfers between devices: 11.5 us -> 9.05 us  [exchange(): lax.ppermute(pa, AXES, pairs(axis, False))]
    all_to_all x1, waiting for transfers between devices: 1 us -> 3.37 us  [local(): lax.all_to_all(jnp.broadcast_to(quad, (128, 256)), ('upper', 'bit0'), 0,...]
where the time goes in v4:
time: 63.6 us; the launch traced here: 63.2 us
  starting transfers between devices  40 us (63%)
  Pallas kernels  14.1 us (22%)
  waiting for transfers between devices  6.53 us (10%)
  local copies, waits for them, and re-layouts  2.41 us (4%)
    all_to_all x1, starting transfers between devices, local(): lax.all_to_all(jnp.broadcast_to(quad, (128, 256)), ('upper', 'bit0'), 0,...  17.6 us
    pallas_call x5, Pallas kernels, call(): pl.pallas_call(kernel, out_shape=[jax.ShapeDtypeStruct(shape[:2], (*shape...  14.1 us
    ppermute x3, starting transfers between devices, exchange(): lax.ppermute(pb, AXES, pairs(axis, True))  13.4 us
    ppermute x3, starting transfers between devices, exchange(): lax.ppermute(pa, AXES, pairs(axis, False))  9.05 us
    all_to_all x1, waiting for transfers between devices, local(): lax.all_to_all(jnp.broadcast_to(quad, (128, 256)), ('upper', 'bit0'), 0,...  3.37 us
    ppermute x3, waiting for transfers between devices, exchange(): lax.ppermute(pa, AXES, pairs(axis, False))  3.15 us
    unnamed x5, local copies, waits for them, and re-layouts  1.6 us
  transfers between devices with their start and end apart: 7, of which 3 were waited for; matrix products, arithmetic and copies ran while one was open for 1% of the time, Pallas kernels for 9%

profile of v4, /device:TPU:1, one launch (start us, length us, event | category | flops | bytes accessed | tf_op | source)
XLA Modules:
  0.0 63.2 jit_solution(12839398640953605419)
XLA Ops:
  0.0 0.1 stack.27.ids_ref
  0.1 0.0 copy-start
  0.1 0.9 %copy-done = f32[64,512]{1,0:T(8,128)S(1)} copy-done((f32[64,512]{1,0:T(8,128)S(1)}, f32[64,512]{1,0:T(8,128)}, u32[]{:S(2)}) %copy-start) | copy-done | bytes 131096
  1.0 0.0 copy-start.1
  1.0 0.7 %copy-done.1 = s32[512]{0:T(512)S(1)} copy-done((s32[512]{0:T(512)S(1)}, s32[512]{0:T(512)}, u32[]{:S(2)}) %copy-start.1) | copy-done | bytes 2072
  1.7 2.3 %shard_map.37 = (f32[80,512]{1,0:T(8,128)S(1)}, f32[24,512]{1,0:T(8,128)S(1)}, f32[24,512]{1,0:T(8,128)S(1)}, f32[64,512]{1,0:T(8,128)S(1)}) custom-call(s32[6]{0:T(128)S(1)} %stack.27.ids_ref, f32[64,512]{1,0:T(8,128)S(1)} %copy-done, s32[1,512]{1,0:T(1,128)S(1)} %bitcast.12, bf16[29152,256]{1,0:T(8,128)(2,1)} %constant.106.clone.blob), custom_call_target="tpu_custom_call" | custom-call | flops 4000000000 | tf_op jit(solution)/shard_map/pallas_call | solution.py:580
  4.0 12.0 %collective-permute-start = (f32[24,512]{1,0:T(8,128)S(1)}, f32[24,512]{1,0:T(8,128)S(1)}, u32[]{:S(2)}, u32[]{:S(2)}) collective-permute-start(f32[24,512]{1,0:T(8,128)S(1)} %get-tuple-element.19), channel_id=1, source_target_pairs={{4,32},{5,33},{6,34},{7,35},{12,40},{13,41},{14,42},{15,43},{20,48... | collective-permute-start | bytes 147464 | tf_op jit(solution)/shard_map/ppermute | solution.py:568
  16.1 1.9 %collective-permute-start.1 = (f32[24,512]{1,0:T(8,128)S(1)}, f32[24,512]{1,0:T(8,128)S(1)}, u32[]{:S(2)}, u32[]{:S(2)}) collective-permute-start(f32[24,512]{1,0:T(8,128)S(1)} %get-tuple-element.20.sent_ref), channel_id=1, source_target_pairs={{0,4},{1,5},{2,6},{3,7},{4,0},{5,1},{6,2},{7,3},{8,12},{9,13},{10,... | collective-permute-start | bytes 147464 | tf_op jit(solution)/shard_map/ppermute | solution.py:567
  18.0 0.0 collective-permute-done.zb_ref
  18.0 1.2 %collective-permute-done.1.za_ref = f32[24,512]{1,0:T(8,128)S(1)} collective-permute-done((f32[24,512]{1,0:T(8,128)S(1)}, f32[24,512]{1,0:T(8,128)S(1)}, u32[]{:S(2)}, u32[]{:S(2)}) %collective-permute-start.1) | collective-permute-done | bytes 49184 | tf_op jit(solution)/shard_map/ppermute | solution.py:567
  19.2 0.6 shard_map.38
  19.8 4.7 %collective-permute-start.2 = (f32[40,512]{1,0:T(8,128)S(1)}, f32[40,512]{1,0:T(8,128)S(1)}, u32[]{:S(2)}, u32[]{:S(2)}) collective-permute-start(f32[40,512]{1,0:T(8,128)S(1)} %get-tuple-element.21), channel_id=1, source_target_pairs={{0,2},{1,3},{2,0},{3,1},{4,6},{5,7},{6,4},{7,5},{8,10},{9,11},{10,... | collective-permute-start | bytes 245768 | tf_op jit(solution)/shard_map/ppermute | solution.py:567
  24.4 0.7 %collective-permute-start.3 = (f32[40,512]{1,0:T(8,128)S(1)}, f32[40,512]{1,0:T(8,128)S(1)}, u32[]{:S(2)}, u32[]{:S(2)}) collective-permute-start(f32[40,512]{1,0:T(8,128)S(1)} %get-tuple-element.22), channel_id=1, source_target_pairs={{2,16},{3,17},{6,20},{7,21},{10,24},{11,25},{14,28},{15,29},{16,2}... | collective-permute-start | bytes 245768 | tf_op jit(solution)/shard_map/ppermute | solution.py:568
  25.1 2.0 %collective-permute-done.2.ya_ref = f32[40,512]{1,0:T(8,128)S(1)} collective-permute-done((f32[40,512]{1,0:T(8,128)S(1)}, f32[40,512]{1,0:T(8,128)S(1)}, u32[]{:S(2)}, u32[]{:S(2)}) %collective-permute-start.2) | collective-permute-done | bytes 81952 | tf_op jit(solution)/shard_map/ppermute | solution.py:567
  27.1 0.7 %broadcast_in_dim.2 = f32[128,1,256]{2,1,0:T(1,128)} broadcast(f32[256]{0:T(256)S(1)} %bitcast.13), dimensions={2} | broadcast | bytes 132096 | tf_op jit(solution)/shard_map/broadcast_in_dim | solution.py:626
  27.8 17.6 %all-to-all-start = ((f32[128,1,256]{2,1,0:T(1,128)}), f32[128,1,256]{2,1,0:T(1,128)S(1)}, u32[]{:S(2)}, u32[]{:S(2)}) async-start(f32[128,1,256]{2,1,0:T(1,128)} %broadcast_in_dim.2), calls=%async_computation | async-start | bytes 262144 | tf_op jit(solution)/shard_map/all_to_all | solution.py:625
  45.4 0.0 collective-permute-done.3.yb_ref
  45.5 0.6 %shard_map.40 = (f32[64,512]{1,0:T(8,128)S(1)}, f32[64,512]{1,0:T(8,128)S(1)}) custom-call(s32[6]{0:T(128)S(1)} %stack.27.ids_ref, f32[80,512]{1,0:T(8,128)S(1)} %get-tuple-element.18.own_ref, f32[24,512]{1,0:T(8,128)S(1)} %collective-permute-done.zb_ref, f32[24,512]{1,0:T(8,128)S(1)} %collective-permute-done.1.za_ref, ...), custom_call_target="tpu_custom_call" | custom-call | flops 40000000000 | tf_op jit(solution)/shard_map/pallas_call | solution.py:580
  46.1 2.5 %collective-permute-start.4 = (f32[64,512]{1,0:T(8,128)S(1)}, f32[64,512]{1,0:T(8,128)S(1)}, u32[]{:S(2)}, u32[]{:S(2)}) collective-permute-start(f32[64,512]{1,0:T(8,128)S(1)} %get-tuple-element.24), channel_id=1, source_target_pairs={{0,1},{1,0},{2,3},{3,2},{4,5},{5,4},{6,7},{7,6},{8,9},{9,8},{10,11... | collective-permute-start | bytes 393224 | tf_op jit(solution)/shard_map/ppermute | solution.py:567
  48.6 0.7 %collective-permute-start.5 = (f32[64,512]{1,0:T(8,128)S(1)}, f32[64,512]{1,0:T(8,128)S(1)}, u32[]{:S(2)}, u32[]{:S(2)}) collective-permute-start(f32[64,512]{1,0:T(8,128)S(1)} %get-tuple-element.25), channel_id=1, source_target_pairs={{1,8},{3,10},{5,12},{7,14},{8,1},{9,64},{10,3},{11,66},{12,5},{13,... | collective-permute-start | bytes 393224 | tf_op jit(solution)/shard_map/ppermute | solution.py:568
  49.3 5.0 %shard_map.39 = (f32[80,512]{1,0:T(8,128)S(1)}, bf16[512,256]{1,0:T(8,128)(2,1)S(1)}, bf16[1024,256]{1,0:T(8,128)(2,1)S(1)}, bf16[224,256]{1,0:T(8,128)(2,1)S(1)}, bf16[288,256]{1,0:T(8,128)(2,1)S(1)}) custom-call(s32[6]{0:T(128)S(1)} %stack.27.ids_ref, f32[80,512]{1,0:T(8,128)S(1)} %get-tuple-element.18.own_ref, f32[24,512]{1,0:T(8,128)S(1)} %collective-permute-done.zb_ref, ...), custom_call_target="tpu_custom_call" | custom-call | flops 1000000000 | tf_op jit(solution)/shard_map/pallas_call | solution.py:580
  54.3 3.4 %all-to-all-done = f32[128,1,256]{2,1,0:T(1,128)S(1)} async-done(((f32[128,1,256]{2,1,0:T(1,128)}), f32[128,1,256]{2,1,0:T(1,128)S(1)}, u32[]{:S(2)}, u32[]{:S(2)}) %all-to-all-start) | async-done | bytes 131104 | tf_op jit(solution)/shard_map/all_to_all | solution.py:625
  57.7 0.0 collective-permute-done.4.xa_ref
  57.7 0.0 collective-permute-done.5.xb_ref
  57.7 5.5 %shard_map.41 = f32[64,512]{1,0:T(8,128)} custom-call(s32[6]{0:T(128)S(1)} %stack.27.ids_ref, f32[80,512]{1,0:T(8,128)S(1)} %get-tuple-element.23.far_in_ref, f32[64,512]{1,0:T(8,128)S(1)} %collective-permute-done.4.xa_ref, f32[64,512]{1,0:T(8,128)S(1)} %collective-permute-done.5.xb_ref, f32[128,256]{1,0:T(8,128)S(1)} %bitcast.11, ...), custom_call_target="tpu_custom_call" | custom-call | flops 4000000000 | tf_op jit(solution)/shard_map/pallas_call | solution.py:580
  (2 shorter events, 0.0 us)
Async XLA Ops:
  0.1 0.9 %copy-start = (f32[64,512]{1,0:T(8,128)S(1)}, f32[64,512]{1,0:T(8,128)}, u32[]{:S(2)}) copy-start(f32[64,512]{1,0:T(8,128)} %mult_ref.1) | copy-start | bytes 393220
  1.0 0.7 %copy-start.1 = (s32[512]{0:T(512)S(1)}, s32[512]{0:T(512)}, u32[]{:S(2)}) copy-start(s32[512]{0:T(512)} %param.4) | copy-start | bytes 6148
  4.0 14.0 %collective-permute-start = (f32[24,512]{1,0:T(8,128)S(1)}, f32[24,512]{1,0:T(8,128)S(1)}, u32[]{:S(2)}, u32[]{:S(2)}) collective-permute-start(f32[24,512]{1,0:T(8,128)S(1)} %get-tuple-element.19), channel_id=1, source_target_pairs={{4,32},{5,33},{6,34},{7,35},{12,40},{13,41},{14,42},{15,43},{20,48... | collective-permute-start | bytes 147464 | tf_op jit(solution)/shard_map/ppermute | solution.py:568
  16.1 3.1 %collective-permute-start.1 = (f32[24,512]{1,0:T(8,128)S(1)}, f32[24,512]{1,0:T(8,128)S(1)}, u32[]{:S(2)}, u32[]{:S(2)}) collective-permute-start(f32[24,512]{1,0:T(8,128)S(1)} %get-tuple-element.20.sent_ref), channel_id=1, source_target_pairs={{0,4},{1,5},{2,6},{3,7},{4,0},{5,1},{6,2},{7,3},{8,12},{9,13},{10,... | collective-permute-start | bytes 147464 | tf_op jit(solution)/shard_map/ppermute | solution.py:567
  19.8 7.3 %collective-permute-start.2 = (f32[40,512]{1,0:T(8,128)S(1)}, f32[40,512]{1,0:T(8,128)S(1)}, u32[]{:S(2)}, u32[]{:S(2)}) collective-permute-start(f32[40,512]{1,0:T(8,128)S(1)} %get-tuple-element.21), channel_id=1, source_target_pairs={{0,2},{1,3},{2,0},{3,1},{4,6},{5,7},{6,4},{7,5},{8,10},{9,11},{10,... | collective-permute-start | bytes 245768 | tf_op jit(solution)/shard_map/ppermute | solution.py:567
  24.4 21.0 %collective-permute-start.3 = (f32[40,512]{1,0:T(8,128)S(1)}, f32[40,512]{1,0:T(8,128)S(1)}, u32[]{:S(2)}, u32[]{:S(2)}) collective-permute-start(f32[40,512]{1,0:T(8,128)S(1)} %get-tuple-element.22), channel_id=1, source_target_pairs={{2,16},{3,17},{6,20},{7,21},{10,24},{11,25},{14,28},{15,29},{16,2}... | collective-permute-start | bytes 245768 | tf_op jit(solution)/shard_map/ppermute | solution.py:568
  27.8 29.8 %all-to-all-start = ((f32[128,1,256]{2,1,0:T(1,128)}), f32[128,1,256]{2,1,0:T(1,128)S(1)}, u32[]{:S(2)}, u32[]{:S(2)}) async-start(f32[128,1,256]{2,1,0:T(1,128)} %broadcast_in_dim.2), calls=%async_computation | async-start | bytes 262144 | tf_op jit(solution)/shard_map/all_to_all | solution.py:625
  46.1 11.6 %collective-permute-start.4 = (f32[64,512]{1,0:T(8,128)S(1)}, f32[64,512]{1,0:T(8,128)S(1)}, u32[]{:S(2)}, u32[]{:S(2)}) collective-permute-start(f32[64,512]{1,0:T(8,128)S(1)} %get-tuple-element.24), channel_id=1, source_target_pairs={{0,1},{1,0},{2,3},{3,2},{4,5},{5,4},{6,7},{7,6},{8,9},{9,8},{10,11... | collective-permute-start | bytes 393224 | tf_op jit(solution)/shard_map/ppermute | solution.py:567
  48.6 9.1 %collective-permute-start.5 = (f32[64,512]{1,0:T(8,128)S(1)}, f32[64,512]{1,0:T(8,128)S(1)}, u32[]{:S(2)}, u32[]{:S(2)}) collective-permute-start(f32[64,512]{1,0:T(8,128)S(1)} %get-tuple-element.25), channel_id=1, source_target_pairs={{1,8},{3,10},{5,12},{7,14},{8,1},{9,64},{10,3},{11,66},{12,5},{13,... | collective-permute-start | bytes 393224 | tf_op jit(solution)/shard_map/ppermute | solution.py:568

commit v5 on v4

--- a/solution.py
+++ b/solution.py
@@ -506,9 +506,9 @@
         piece_copy(blob, "back", back_ref, sem.at[3]),
         piece_copy(blob, "down", down_ref, sem.at[4]),
     ]
-    for copy in (*tables, *last):
+    for copy in (*reversed(tables), *last):
         copy.start()
-    three = coarse_rows(quads_ref[...])
+    three = coarse_rows(quads_ref[...].reshape(128, 256))
     odd = ids_ref[0] == 1
     a, b = xa_ref[...], xb_ref[...]
     low, high = jnp.where(odd, a, b), jnp.where(odd, b, a)
@@ -532,10 +532,10 @@
             place_mix(wide_one, k % 9, ky, kz, mix, 2 * RIM)
         else:
             place_mix(wide_one, k % 9, ky, kz, reflected(mix), 2 * RIM + SMALL)
+    tables[1].wait()
+    one = far_rows(wide_one, far_ref, 1)
     tables[0].wait()
     zero = far_rows(wide_zero, far_ref, 0)
-    tables[1].wait()
-    one = far_rows(wide_one, far_ref, 1)
     rims = jnp.concatenate([one[:RIM], reflected(one[RIM : 2 * RIM])], axis=0)
     small = zero + one[2 * RIM : 2 * RIM + SMALL] + reflected(one[2 * RIM + SMALL :])
     for copy in last:
@@ -623,7 +623,7 @@
     ours, theirs = (p[Y_THREE : Y_THREE + 1, :256] for p in (pa, ya))
     quad = jnp.where(jnp.arange(256)[None] // 64 % 2 == ids[1], ours, theirs)
     quads = lax.all_to_all(
-        jnp.broadcast_to(quad, (128, 256)), ("upper", "bit0"), 0, 0, tiled=True
+        jnp.broadcast_to(quad[None], (128, 1, 256)), ("upper", "bit0"), 0, 0, tiled=True
     )
     pa, pb = call(
         x_kernel, rows_of(X_ROWS, X_ROWS), scratch_rows(Z_ROWS, Z_ROWS, Y_ROWS, Y_ROWS),

time: 63.6 us -> 63.3 us (level)
    unnamed x5 -> x4, local copies, waits for them, and re-layouts: 1.6 us -> 1.59 us
where the time goes in v5:
time: 63.3 us; the launch traced here: 63 us
  starting transfers between devices  40 us (63%)
  Pallas kernels  13.9 us (22%)
  waiting for transfers between devices  6.51 us (10%)
  local copies, waits for them, and re-layouts  2.4 us (4%)
    all_to_all x1, starting transfers between devices, local(): lax.all_to_all(jnp.broadcast_to(quad[None], (128, 1, 256)), ('upper', 'bi...  17.6 us
    pallas_call x5, Pallas kernels, call(): pl.pallas_call(kernel, out_shape=[jax.ShapeDtypeStruct(shape[:2], (*shape...  13.9 us
    ppermute x3, starting transfers between devices, exchange(): lax.ppermute(pb, AXES, pairs(axis, True))  13.4 us
    ppermute x3, starting transfers between devices, exchange(): lax.ppermute(pa, AXES, pairs(axis, False))  9.05 us
    all_to_all x1, waiting for transfers between devices, local(): lax.all_to_all(jnp.broadcast_to(quad[None], (128, 1, 256)), ('upper', 'bi...  3.35 us
    ppermute x3, waiting for transfers between devices, exchange(): lax.ppermute(pa, AXES, pairs(axis, False))  3.15 us
    unnamed x4, local copies, waits for them, and re-layouts  1.59 us
  transfers between devices with their start and end apart: 7, of which 3 were waited for; matrix products, arithmetic and copies ran while one was open for 1% of the time, Pallas kernels for 9%

profile of v5, /device:TPU:1, one launch (start us, length us, event | category | flops | bytes accessed | tf_op | source)
XLA Modules:
  0.0 63.0 jit_solution(3716749164739442240)
XLA Ops:
  0.0 0.1 stack.27.ids_ref
  0.1 0.0 copy-start
  0.1 0.9 %copy-done = f32[64,512]{1,0:T(8,128)S(1)} copy-done((f32[64,512]{1,0:T(8,128)S(1)}, f32[64,512]{1,0:T(8,128)}, u32[]{:S(2)}) %copy-start) | copy-done | bytes 131096
  1.0 0.0 copy-start.1
  1.0 0.7 %copy-done.1 = s32[512]{0:T(512)S(1)} copy-done((s32[512]{0:T(512)S(1)}, s32[512]{0:T(512)}, u32[]{:S(2)}) %copy-start.1) | copy-done | bytes 2072
  1.7 2.3 %shard_map.37 = (f32[80,512]{1,0:T(8,128)S(1)}, f32[24,512]{1,0:T(8,128)S(1)}, f32[24,512]{1,0:T(8,128)S(1)}, f32[64,512]{1,0:T(8,128)S(1)}) custom-call(s32[6]{0:T(128)S(1)} %stack.27.ids_ref, f32[64,512]{1,0:T(8,128)S(1)} %copy-done, s32[1,512]{1,0:T(1,128)S(1)} %bitcast.8, bf16[29152,256]{1,0:T(8,128)(2,1)} %constant.106.clone.blob), custom_call_target="tpu_custom_call" | custom-call | flops 4000000000 | tf_op jit(solution)/shard_map/pallas_call | solution.py:580
  4.0 12.0 %collective-permute-start = (f32[24,512]{1,0:T(8,128)S(1)}, f32[24,512]{1,0:T(8,128)S(1)}, u32[]{:S(2)}, u32[]{:S(2)}) collective-permute-start(f32[24,512]{1,0:T(8,128)S(1)} %get-tuple-element.19), channel_id=1, source_target_pairs={{4,32},{5,33},{6,34},{7,35},{12,40},{13,41},{14,42},{15,43},{20,48... | collective-permute-start | bytes 147464 | tf_op jit(solution)/shard_map/ppermute | solution.py:568
  16.1 1.9 %collective-permute-start.1 = (f32[24,512]{1,0:T(8,128)S(1)}, f32[24,512]{1,0:T(8,128)S(1)}, u32[]{:S(2)}, u32[]{:S(2)}) collective-permute-start(f32[24,512]{1,0:T(8,128)S(1)} %get-tuple-element.20.sent_ref), channel_id=1, source_target_pairs={{0,4},{1,5},{2,6},{3,7},{4,0},{5,1},{6,2},{7,3},{8,12},{9,13},{10,... | collective-permute-start | bytes 147464 | tf_op jit(solution)/shard_map/ppermute | solution.py:567
  18.0 0.0 collective-permute-done.zb_ref
  18.0 1.2 %collective-permute-done.1.za_ref = f32[24,512]{1,0:T(8,128)S(1)} collective-permute-done((f32[24,512]{1,0:T(8,128)S(1)}, f32[24,512]{1,0:T(8,128)S(1)}, u32[]{:S(2)}, u32[]{:S(2)}) %collective-permute-start.1) | collective-permute-done | bytes 49184 | tf_op jit(solution)/shard_map/ppermute | solution.py:567
  19.2 0.6 shard_map.38
  19.8 4.7 %collective-permute-start.2 = (f32[40,512]{1,0:T(8,128)S(1)}, f32[40,512]{1,0:T(8,128)S(1)}, u32[]{:S(2)}, u32[]{:S(2)}) collective-permute-start(f32[40,512]{1,0:T(8,128)S(1)} %get-tuple-element.21), channel_id=1, source_target_pairs={{0,2},{1,3},{2,0},{3,1},{4,6},{5,7},{6,4},{7,5},{8,10},{9,11},{10,... | collective-permute-start | bytes 245768 | tf_op jit(solution)/shard_map/ppermute | solution.py:567
  24.4 0.7 %collective-permute-start.3 = (f32[40,512]{1,0:T(8,128)S(1)}, f32[40,512]{1,0:T(8,128)S(1)}, u32[]{:S(2)}, u32[]{:S(2)}) collective-permute-start(f32[40,512]{1,0:T(8,128)S(1)} %get-tuple-element.22), channel_id=1, source_target_pairs={{2,16},{3,17},{6,20},{7,21},{10,24},{11,25},{14,28},{15,29},{16,2}... | collective-permute-start | bytes 245768 | tf_op jit(solution)/shard_map/ppermute | solution.py:568
  25.1 2.0 %collective-permute-done.2.ya_ref = f32[40,512]{1,0:T(8,128)S(1)} collective-permute-done((f32[40,512]{1,0:T(8,128)S(1)}, f32[40,512]{1,0:T(8,128)S(1)}, u32[]{:S(2)}, u32[]{:S(2)}) %collective-permute-start.2) | collective-permute-done | bytes 81952 | tf_op jit(solution)/shard_map/ppermute | solution.py:567
  27.1 0.7 %broadcast_in_dim.10 = f32[128,1,256]{2,1,0:T(1,128)} broadcast(f32[256]{0:T(256)S(1)} %bitcast.9), dimensions={2} | broadcast | bytes 132096 | tf_op jit(solution)/shard_map/broadcast_in_dim | solution.py:626
  27.8 17.6 %all-to-all-start = ((f32[128,1,256]{2,1,0:T(1,128)}), f32[128,1,256]{2,1,0:T(1,128)S(1)}, u32[]{:S(2)}, u32[]{:S(2)}) async-start(f32[128,1,256]{2,1,0:T(1,128)} %broadcast_in_dim.10), calls=%async_computation | async-start | bytes 262144 | tf_op jit(solution)/shard_map/all_to_all | solution.py:625
  45.4 0.0 collective-permute-done.3.yb_ref
  45.5 0.6 %shard_map.40 = (f32[64,512]{1,0:T(8,128)S(1)}, f32[64,512]{1,0:T(8,128)S(1)}) custom-call(s32[6]{0:T(128)S(1)} %stack.27.ids_ref, f32[80,512]{1,0:T(8,128)S(1)} %get-tuple-element.18.own_ref, f32[24,512]{1,0:T(8,128)S(1)} %collective-permute-done.zb_ref, f32[24,512]{1,0:T(8,128)S(1)} %collective-permute-done.1.za_ref, ...), custom_call_target="tpu_custom_call" | custom-call | flops 40000000000 | tf_op jit(solution)/shard_map/pallas_call | solution.py:580
  46.1 2.5 %collective-permute-start.4 = (f32[64,512]{1,0:T(8,128)S(1)}, f32[64,512]{1,0:T(8,128)S(1)}, u32[]{:S(2)}, u32[]{:S(2)}) collective-permute-start(f32[64,512]{1,0:T(8,128)S(1)} %get-tuple-element.24), channel_id=1, source_target_pairs={{0,1},{1,0},{2,3},{3,2},{4,5},{5,4},{6,7},{7,6},{8,9},{9,8},{10,11... | collective-permute-start | bytes 393224 | tf_op jit(solution)/shard_map/ppermute | solution.py:567
  48.6 0.7 %collective-permute-start.5 = (f32[64,512]{1,0:T(8,128)S(1)}, f32[64,512]{1,0:T(8,128)S(1)}, u32[]{:S(2)}, u32[]{:S(2)}) collective-permute-start(f32[64,512]{1,0:T(8,128)S(1)} %get-tuple-element.25), channel_id=1, source_target_pairs={{1,8},{3,10},{5,12},{7,14},{8,1},{9,64},{10,3},{11,66},{12,5},{13,... | collective-permute-start | bytes 393224 | tf_op jit(solution)/shard_map/ppermute | solution.py:568
  49.3 5.0 %shard_map.39 = (f32[80,512]{1,0:T(8,128)S(1)}, bf16[512,256]{1,0:T(8,128)(2,1)S(1)}, bf16[1024,256]{1,0:T(8,128)(2,1)S(1)}, bf16[224,256]{1,0:T(8,128)(2,1)S(1)}, bf16[288,256]{1,0:T(8,128)(2,1)S(1)}) custom-call(s32[6]{0:T(128)S(1)} %stack.27.ids_ref, f32[80,512]{1,0:T(8,128)S(1)} %get-tuple-element.18.own_ref, f32[24,512]{1,0:T(8,128)S(1)} %collective-permute-done.zb_ref, ...), custom_call_target="tpu_custom_call" | custom-call | flops 1000000000 | tf_op jit(solution)/shard_map/pallas_call | solution.py:580
  54.3 0.0 collective-permute-done.4.xa_ref
  54.3 0.0 collective-permute-done.5.xb_ref
  54.3 3.4 %all-to-all-done.quads_ref = f32[128,1,256]{2,1,0:T(1,128)S(1)} async-done(((f32[128,1,256]{2,1,0:T(1,128)}), f32[128,1,256]{2,1,0:T(1,128)S(1)}, u32[]{:S(2)}, u32[]{:S(2)}) %all-to-all-start) | async-done | bytes 131104 | tf_op jit(solution)/shard_map/all_to_all | solution.py:625
  57.7 5.3 %shard_map.41 = f32[64,512]{1,0:T(8,128)} custom-call(s32[6]{0:T(128)S(1)} %stack.27.ids_ref, f32[80,512]{1,0:T(8,128)S(1)} %get-tuple-element.23.far_in_ref, f32[64,512]{1,0:T(8,128)S(1)} %collective-permute-done.4.xa_ref, f32[64,512]{1,0:T(8,128)S(1)} %collective-permute-done.5.xb_ref, f32[128,1,256]{2,1,0:T(1,128)S(1)} %all-to-all-done.quads_ref, ...), custom_call_target="tpu_custom_call" | custom-call | flops 4000000000 | tf_op jit(solution)/shard_map/pallas_call | solution.py:580
  (1 shorter events, 0.0 us)
Async XLA Ops:
  0.1 0.9 %copy-start = (f32[64,512]{1,0:T(8,128)S(1)}, f32[64,512]{1,0:T(8,128)}, u32[]{:S(2)}) copy-start(f32[64,512]{1,0:T(8,128)} %mult_ref.1) | copy-start | bytes 393220
  1.0 0.7 %copy-start.1 = (s32[512]{0:T(512)S(1)}, s32[512]{0:T(512)}, u32[]{:S(2)}) copy-start(s32[512]{0:T(512)} %param.4) | copy-start | bytes 6148
  4.0 14.0 %collective-permute-start = (f32[24,512]{1,0:T(8,128)S(1)}, f32[24,512]{1,0:T(8,128)S(1)}, u32[]{:S(2)}, u32[]{:S(2)}) collective-permute-start(f32[24,512]{1,0:T(8,128)S(1)} %get-tuple-element.19), channel_id=1, source_target_pairs={{4,32},{5,33},{6,34},{7,35},{12,40},{13,41},{14,42},{15,43},{20,48... | collective-permute-start | bytes 147464 | tf_op jit(solution)/shard_map/ppermute | solution.py:568
  16.1 3.1 %collective-permute-start.1 = (f32[24,512]{1,0:T(8,128)S(1)}, f32[24,512]{1,0:T(8,128)S(1)}, u32[]{:S(2)}, u32[]{:S(2)}) collective-permute-start(f32[24,512]{1,0:T(8,128)S(1)} %get-tuple-element.20.sent_ref), channel_id=1, source_target_pairs={{0,4},{1,5},{2,6},{3,7},{4,0},{5,1},{6,2},{7,3},{8,12},{9,13},{10,... | collective-permute-start | bytes 147464 | tf_op jit(solution)/shard_map/ppermute | solution.py:567
  19.8 7.3 %collective-permute-start.2 = (f32[40,512]{1,0:T(8,128)S(1)}, f32[40,512]{1,0:T(8,128)S(1)}, u32[]{:S(2)}, u32[]{:S(2)}) collective-permute-start(f32[40,512]{1,0:T(8,128)S(1)} %get-tuple-element.21), channel_id=1, source_target_pairs={{0,2},{1,3},{2,0},{3,1},{4,6},{5,7},{6,4},{7,5},{8,10},{9,11},{10,... | collective-permute-start | bytes 245768 | tf_op jit(solution)/shard_map/ppermute | solution.py:567
  24.4 21.0 %collective-permute-start.3 = (f32[40,512]{1,0:T(8,128)S(1)}, f32[40,512]{1,0:T(8,128)S(1)}, u32[]{:S(2)}, u32[]{:S(2)}) collective-permute-start(f32[40,512]{1,0:T(8,128)S(1)} %get-tuple-element.22), channel_id=1, source_target_pairs={{2,16},{3,17},{6,20},{7,21},{10,24},{11,25},{14,28},{15,29},{16,2}... | collective-permute-start | bytes 245768 | tf_op jit(solution)/shard_map/ppermute | solution.py:568
  27.8 29.8 %all-to-all-start = ((f32[128,1,256]{2,1,0:T(1,128)}), f32[128,1,256]{2,1,0:T(1,128)S(1)}, u32[]{:S(2)}, u32[]{:S(2)}) async-start(f32[128,1,256]{2,1,0:T(1,128)} %broadcast_in_dim.10), calls=%async_computation | async-start | bytes 262144 | tf_op jit(solution)/shard_map/all_to_all | solution.py:625
  46.1 8.2 %collective-permute-start.4 = (f32[64,512]{1,0:T(8,128)S(1)}, f32[64,512]{1,0:T(8,128)S(1)}, u32[]{:S(2)}, u32[]{:S(2)}) collective-permute-start(f32[64,512]{1,0:T(8,128)S(1)} %get-tuple-element.24), channel_id=1, source_target_pairs={{0,1},{1,0},{2,3},{3,2},{4,5},{5,4},{6,7},{7,6},{8,9},{9,8},{10,11... | collective-permute-start | bytes 393224 | tf_op jit(solution)/shard_map/ppermute | solution.py:567
  48.6 5.7 %collective-permute-start.5 = (f32[64,512]{1,0:T(8,128)S(1)}, f32[64,512]{1,0:T(8,128)S(1)}, u32[]{:S(2)}, u32[]{:S(2)}) collective-permute-start(f32[64,512]{1,0:T(8,128)S(1)} %get-tuple-element.25), channel_id=1, source_target_pairs={{1,8},{3,10},{5,12},{7,14},{8,1},{9,64},{10,3},{11,66},{12,5},{13,... | collective-permute-start | bytes 393224 | tf_op jit(solution)/shard_map/ppermute | solution.py:568

commit v6 on v5

--- a/solution.py
+++ b/solution.py
@@ -621,10 +621,10 @@
     )
     ya, yb = exchange(pa, pb, 1)
     ours, theirs = (p[Y_THREE : Y_THREE + 1, :256] for p in (pa, ya))
-    quad = jnp.where(jnp.arange(256)[None] // 64 % 2 == ids[1], ours, theirs)
-    quads = lax.all_to_all(
-        jnp.broadcast_to(quad[None], (128, 1, 256)), ("upper", "bit0"), 0, 0, tiled=True
-    )
+    spread = (128, 1, 256)
+    own_side = lax.broadcasted_iota(jnp.int32, spread, 2) // 64 % 2 == ids[1]
+    quad = jnp.where(own_side, jnp.broadcast_to(ours[None], spread), jnp.broadcast_to(theirs[None], spread))
+    quads = lax.all_to_all(quad, ("upper", "bit0"), 0, 0, tiled=True)
     pa, pb = call(
         x_kernel, rows_of(X_ROWS, X_ROWS), scratch_rows(Z_ROWS, Z_ROWS, Y_ROWS, Y_ROWS),
         ids, [own, zb, za, ya, yb], micros=40,

time: 63.3 us -> 63.3 us (level)
  other arithmetic: 0.02 us -> 0.75 us
  local copies, waits for them, and re-layouts: 2.4 us -> 1.68 us
    broadcast_in_dim x1 -> x0, local copies, waits for them, and re-layouts: 0.73 us -> none  [local(): jnp.broadcast_to(quad[None], (128, 1, 256))]
    select_n x1, other arithmetic: 0.02 us -> 0.73 us  [local(): jnp.where(own_side, jnp.broadcast_to(ours[None], spread), jnp.broadcast_t...]
where the time goes in v6:
time: 63.3 us; the launch traced here: 63 us
  starting transfers between devices  40.1 us (63%)
  Pallas kernels  13.9 us (22%)
  waiting for transfers between devices  6.47 us (10%)
  local copies, waits for them, and re-layouts  1.68 us (3%)
  other arithmetic  0.75 us (1%)
    all_to_all x1, starting transfers between devices, local(): quads = lax.all_to_all(quad, ('upper', 'bit0'), 0, 0, tiled=True)  17.6 us
    pallas_call x5, Pallas kernels, call(): pl.pallas_call(kernel, out_shape=[jax.ShapeDtypeStruct(shape[:2], (*shape...  13.9 us
    ppermute x3, starting transfers between devices, exchange(): lax.ppermute(pb, AXES, pairs(axis, True))  13.4 us
    ppermute x3, starting transfers between devices, exchange(): lax.ppermute(pa, AXES, pairs(axis, False))  9.05 us
    all_to_all x1, waiting for transfers between devices, local(): quads = lax.all_to_all(quad, ('upper', 'bit0'), 0, 0, tiled=True)  3.35 us
    ppermute x3, waiting for transfers between devices, exchange(): lax.ppermute(pa, AXES, pairs(axis, False))  3.11 us
    unnamed x4, local copies, waits for them, and re-layouts  1.59 us
  transfers between devices with their start and end apart: 7, of which 3 were waited for; matrix products, arithmetic and copies ran while one was open for 1% of the time, Pallas kernels for 9%

profile of v6, /device:TPU:1, one launch (start us, length us, event | category | flops | bytes accessed | tf_op | source)
XLA Modules:
  0.0 63.0 jit_solution(10385141907425173378)
XLA Ops:
  0.0 0.1 stack.27.ids_ref
  0.1 0.0 copy-start
  0.1 0.9 %copy-done = f32[64,512]{1,0:T(8,128)S(1)} copy-done((f32[64,512]{1,0:T(8,128)S(1)}, f32[64,512]{1,0:T(8,128)}, u32[]{:S(2)}) %copy-start) | copy-done | bytes 131096
  1.0 0.0 copy-start.1
  1.0 0.7 %copy-done.1 = s32[512]{0:T(512)S(1)} copy-done((s32[512]{0:T(512)S(1)}, s32[512]{0:T(512)}, u32[]{:S(2)}) %copy-start.1) | copy-done | bytes 2072
  1.7 2.3 %shard_map.37 = (f32[80,512]{1,0:T(8,128)S(1)}, f32[24,512]{1,0:T(8,128)S(1)}, f32[24,512]{1,0:T(8,128)S(1)}, f32[64,512]{1,0:T(8,128)S(1)}) custom-call(s32[6]{0:T(128)S(1)} %stack.27.ids_ref, f32[64,512]{1,0:T(8,128)S(1)} %copy-done, s32[1,512]{1,0:T(1,128)S(1)} %bitcast.9, bf16[29152,256]{1,0:T(8,128)(2,1)} %constant.108.clone.blob), custom_call_target="tpu_custom_call" | custom-call | flops 4000000000 | tf_op jit(solution)/shard_map/pallas_call | solution.py:580
  4.0 12.0 %collective-permute-start = (f32[24,512]{1,0:T(8,128)S(1)}, f32[24,512]{1,0:T(8,128)S(1)}, u32[]{:S(2)}, u32[]{:S(2)}) collective-permute-start(f32[24,512]{1,0:T(8,128)S(1)} %get-tuple-element.19), channel_id=1, source_target_pairs={{4,32},{5,33},{6,34},{7,35},{12,40},{13,41},{14,42},{15,43},{20,48... | collective-permute-start | bytes 147464 | tf_op jit(solution)/shard_map/ppermute | solution.py:568
  16.1 1.9 %collective-permute-start.1 = (f32[24,512]{1,0:T(8,128)S(1)}, f32[24,512]{1,0:T(8,128)S(1)}, u32[]{:S(2)}, u32[]{:S(2)}) collective-permute-start(f32[24,512]{1,0:T(8,128)S(1)} %get-tuple-element.20.sent_ref), channel_id=1, source_target_pairs={{0,4},{1,5},{2,6},{3,7},{4,0},{5,1},{6,2},{7,3},{8,12},{9,13},{10,... | collective-permute-start | bytes 147464 | tf_op jit(solution)/shard_map/ppermute | solution.py:567
  18.0 0.0 collective-permute-done.zb_ref
  18.0 1.2 %collective-permute-done.1.za_ref = f32[24,512]{1,0:T(8,128)S(1)} collective-permute-done((f32[24,512]{1,0:T(8,128)S(1)}, f32[24,512]{1,0:T(8,128)S(1)}, u32[]{:S(2)}, u32[]{:S(2)}) %collective-permute-start.1) | collective-permute-done | bytes 49184 | tf_op jit(solution)/shard_map/ppermute | solution.py:567
  19.2 0.6 shard_map.38
  19.8 4.7 %collective-permute-start.2 = (f32[40,512]{1,0:T(8,128)S(1)}, f32[40,512]{1,0:T(8,128)S(1)}, u32[]{:S(2)}, u32[]{:S(2)}) collective-permute-start(f32[40,512]{1,0:T(8,128)S(1)} %get-tuple-element.21), channel_id=1, source_target_pairs={{0,2},{1,3},{2,0},{3,1},{4,6},{5,7},{6,4},{7,5},{8,10},{9,11},{10,... | collective-permute-start | bytes 245768 | tf_op jit(solution)/shard_map/ppermute | solution.py:567
  24.5 0.7 %collective-permute-start.3 = (f32[40,512]{1,0:T(8,128)S(1)}, f32[40,512]{1,0:T(8,128)S(1)}, u32[]{:S(2)}, u32[]{:S(2)}) collective-permute-start(f32[40,512]{1,0:T(8,128)S(1)} %get-tuple-element.22), channel_id=1, source_target_pairs={{2,16},{3,17},{6,20},{7,21},{10,24},{11,25},{14,28},{15,29},{16,2}... | collective-permute-start | bytes 245768 | tf_op jit(solution)/shard_map/ppermute | solution.py:568
  25.1 1.9 %collective-permute-done.2.ya_ref = f32[40,512]{1,0:T(8,128)S(1)} collective-permute-done((f32[40,512]{1,0:T(8,128)S(1)}, f32[40,512]{1,0:T(8,128)S(1)}, u32[]{:S(2)}, u32[]{:S(2)}) %collective-permute-start.2) | collective-permute-done | bytes 81952 | tf_op jit(solution)/shard_map/ppermute | solution.py:567
  27.1 0.7 %compare_select_fusion.2 = f32[128,1,256]{2,1,0:T(1,128)} fusion(pred[256]{0:T(512)(128)(4,1)S(1)} %compare_and_fusion, f32[256]{0:T(256)S(1)} %bitcast.11, f32[256]{0:T(256)S(1)} %bitcast.10, s32[]{:T(128)} %select_n.74, s32[256]{0:T(256)S(1)} %get-tuple-element.31, s32[256]{0:T(256)S(1)} %get-tuple-element.32), kind=kLoop, calls=%fused_computation.2 | loop fusion | flops 458752 | bytes 135428 | tf_op jit(solution)/shard_map/jit(_where)/select_n | solution.py:626
  27.8 17.6 %all-to-all-start = ((f32[128,1,256]{2,1,0:T(1,128)}), f32[128,1,256]{2,1,0:T(1,128)S(1)}, u32[]{:S(2)}, u32[]{:S(2)}) async-start(f32[128,1,256]{2,1,0:T(1,128)} %compare_select_fusion.2), calls=%async_computation | async-start | bytes 262144 | tf_op jit(solution)/shard_map/all_to_all | solution.py:627
  45.5 0.0 collective-permute-done.3.yb_ref
  45.5 0.6 %shard_map.40 = (f32[64,512]{1,0:T(8,128)S(1)}, f32[64,512]{1,0:T(8,128)S(1)}) custom-call(s32[6]{0:T(128)S(1)} %stack.27.ids_ref, f32[80,512]{1,0:T(8,128)S(1)} %get-tuple-element.18.own_ref, f32[24,512]{1,0:T(8,128)S(1)} %collective-permute-done.zb_ref, f32[24,512]{1,0:T(8,128)S(1)} %collective-permute-done.1.za_ref, ...), custom_call_target="tpu_custom_call" | custom-call | flops 40000000000 | tf_op jit(solution)/shard_map/pallas_call | solution.py:580
  46.1 2.5 %collective-permute-start.4 = (f32[64,512]{1,0:T(8,128)S(1)}, f32[64,512]{1,0:T(8,128)S(1)}, u32[]{:S(2)}, u32[]{:S(2)}) collective-permute-start(f32[64,512]{1,0:T(8,128)S(1)} %get-tuple-element.24), channel_id=1, source_target_pairs={{0,1},{1,0},{2,3},{3,2},{4,5},{5,4},{6,7},{7,6},{8,9},{9,8},{10,11... | collective-permute-start | bytes 393224 | tf_op jit(solution)/shard_map/ppermute | solution.py:567
  48.6 0.7 %collective-permute-start.5 = (f32[64,512]{1,0:T(8,128)S(1)}, f32[64,512]{1,0:T(8,128)S(1)}, u32[]{:S(2)}, u32[]{:S(2)}) collective-permute-start(f32[64,512]{1,0:T(8,128)S(1)} %get-tuple-element.25), channel_id=1, source_target_pairs={{1,8},{3,10},{5,12},{7,14},{8,1},{9,64},{10,3},{11,66},{12,5},{13,... | collective-permute-start | bytes 393224 | tf_op jit(solution)/shard_map/ppermute | solution.py:568
  49.3 5.0 %shard_map.39 = (f32[80,512]{1,0:T(8,128)S(1)}, bf16[512,256]{1,0:T(8,128)(2,1)S(1)}, bf16[1024,256]{1,0:T(8,128)(2,1)S(1)}, bf16[224,256]{1,0:T(8,128)(2,1)S(1)}, bf16[288,256]{1,0:T(8,128)(2,1)S(1)}) custom-call(s32[6]{0:T(128)S(1)} %stack.27.ids_ref, f32[80,512]{1,0:T(8,128)S(1)} %get-tuple-element.18.own_ref, f32[24,512]{1,0:T(8,128)S(1)} %collective-permute-done.zb_ref, ...), custom_call_target="tpu_custom_call" | custom-call | flops 1000000000 | tf_op jit(solution)/shard_map/pallas_call | solution.py:580
  54.3 0.0 collective-permute-done.4.xa_ref
  54.3 0.0 collective-permute-done.5.xb_ref
  54.3 3.4 %all-to-all-done.quads_ref = f32[128,1,256]{2,1,0:T(1,128)S(1)} async-done(((f32[128,1,256]{2,1,0:T(1,128)}), f32[128,1,256]{2,1,0:T(1,128)S(1)}, u32[]{:S(2)}, u32[]{:S(2)}) %all-to-all-start) | async-done | bytes 131104 | tf_op jit(solution)/shard_map/all_to_all | solution.py:627
  57.7 5.3 %shard_map.41 = f32[64,512]{1,0:T(8,128)} custom-call(s32[6]{0:T(128)S(1)} %stack.27.ids_ref, f32[80,512]{1,0:T(8,128)S(1)} %get-tuple-element.23.far_in_ref, f32[64,512]{1,0:T(8,128)S(1)} %collective-permute-done.4.xa_ref, f32[64,512]{1,0:T(8,128)S(1)} %collective-permute-done.5.xb_ref, f32[128,1,256]{2,1,0:T(1,128)S(1)} %all-to-all-done.quads_ref, ...), custom_call_target="tpu_custom_call" | custom-call | flops 4000000000 | tf_op jit(solution)/shard_map/pallas_call | solution.py:580
  (4 shorter events, 0.0 us)
Async XLA Ops:
  0.1 0.9 %copy-start = (f32[64,512]{1,0:T(8,128)S(1)}, f32[64,512]{1,0:T(8,128)}, u32[]{:S(2)}) copy-start(f32[64,512]{1,0:T(8,128)} %mult_ref.1) | copy-start | bytes 393220
  1.0 0.7 %copy-start.1 = (s32[512]{0:T(512)S(1)}, s32[512]{0:T(512)}, u32[]{:S(2)}) copy-start(s32[512]{0:T(512)} %param.4) | copy-start | bytes 6148
  4.0 14.0 %collective-permute-start = (f32[24,512]{1,0:T(8,128)S(1)}, f32[24,512]{1,0:T(8,128)S(1)}, u32[]{:S(2)}, u32[]{:S(2)}) collective-permute-start(f32[24,512]{1,0:T(8,128)S(1)} %get-tuple-element.19), channel_id=1, source_target_pairs={{4,32},{5,33},{6,34},{7,35},{12,40},{13,41},{14,42},{15,43},{20,48... | collective-permute-start | bytes 147464 | tf_op jit(solution)/shard_map/ppermute | solution.py:568
  16.1 3.1 %collective-permute-start.1 = (f32[24,512]{1,0:T(8,128)S(1)}, f32[24,512]{1,0:T(8,128)S(1)}, u32[]{:S(2)}, u32[]{:S(2)}) collective-permute-start(f32[24,512]{1,0:T(8,128)S(1)} %get-tuple-element.20.sent_ref), channel_id=1, source_target_pairs={{0,4},{1,5},{2,6},{3,7},{4,0},{5,1},{6,2},{7,3},{8,12},{9,13},{10,... | collective-permute-start | bytes 147464 | tf_op jit(solution)/shard_map/ppermute | solution.py:567
  19.8 7.3 %collective-permute-start.2 = (f32[40,512]{1,0:T(8,128)S(1)}, f32[40,512]{1,0:T(8,128)S(1)}, u32[]{:S(2)}, u32[]{:S(2)}) collective-permute-start(f32[40,512]{1,0:T(8,128)S(1)} %get-tuple-element.21), channel_id=1, source_target_pairs={{0,2},{1,3},{2,0},{3,1},{4,6},{5,7},{6,4},{7,5},{8,10},{9,11},{10,... | collective-permute-start | bytes 245768 | tf_op jit(solution)/shard_map/ppermute | solution.py:567
  24.5 21.0 %collective-permute-start.3 = (f32[40,512]{1,0:T(8,128)S(1)}, f32[40,512]{1,0:T(8,128)S(1)}, u32[]{:S(2)}, u32[]{:S(2)}) collective-permute-start(f32[40,512]{1,0:T(8,128)S(1)} %get-tuple-element.22), channel_id=1, source_target_pairs={{2,16},{3,17},{6,20},{7,21},{10,24},{11,25},{14,28},{15,29},{16,2}... | collective-permute-start | bytes 245768 | tf_op jit(solution)/shard_map/ppermute | solution.py:568
  27.8 29.9 %all-to-all-start = ((f32[128,1,256]{2,1,0:T(1,128)}), f32[128,1,256]{2,1,0:T(1,128)S(1)}, u32[]{:S(2)}, u32[]{:S(2)}) async-start(f32[128,1,256]{2,1,0:T(1,128)} %compare_select_fusion.2), calls=%async_computation | async-start | bytes 262144 | tf_op jit(solution)/shard_map/all_to_all | solution.py:627
  46.1 8.2 %collective-permute-start.4 = (f32[64,512]{1,0:T(8,128)S(1)}, f32[64,512]{1,0:T(8,128)S(1)}, u32[]{:S(2)}, u32[]{:S(2)}) collective-permute-start(f32[64,512]{1,0:T(8,128)S(1)} %get-tuple-element.24), channel_id=1, source_target_pairs={{0,1},{1,0},{2,3},{3,2},{4,5},{5,4},{6,7},{7,6},{8,9},{9,8},{10,11... | collective-permute-start | bytes 393224 | tf_op jit(solution)/shard_map/ppermute | solution.py:567
  48.6 5.7 %collective-permute-start.5 = (f32[64,512]{1,0:T(8,128)S(1)}, f32[64,512]{1,0:T(8,128)S(1)}, u32[]{:S(2)}, u32[]{:S(2)}) collective-permute-start(f32[64,512]{1,0:T(8,128)S(1)} %get-tuple-element.25), channel_id=1, source_target_pairs={{1,8},{3,10},{5,12},{7,14},{8,1},{9,64},{10,3},{11,66},{12,5},{13,... | collective-permute-start | bytes 393224 | tf_op jit(solution)/shard_map/ppermute | solution.py:568
